TPU v7x, 32 devices: a whole 2x2x4 slice. The times are simulated.
32 devices in a mesh: dp: 16 (over z, y, core), fsdp: 2 (over x).
Axes of the slice: x: 2, y: 2, z: 4, core: 2. Of those that a mesh axis runs over, the one named last changes fastest.
Arguments:
- tokens: bfloat16 [32, 512, 1024], P(('dp', 'fsdp')), may hold values from -6 to 6
- lengths: int32 [32], P(('dp', 'fsdp')), may hold values from 76 to 512, as said below
- local_project: bfloat16 [1024, 4096], P('dp', 'fsdp'), may hold values from -0.1875 to 0.1875
- local_output: bfloat16 [1024, 1024], P('dp', 'fsdp'), may hold values from -0.1875 to 0.1875
- local_expand: bfloat16 [1024, 5632], P('dp', 'fsdp'), may hold values from -0.1875 to 0.1875
- local_shrink: bfloat16 [2816, 1024], P('dp', 'fsdp'), may hold values from -0.109375 to 0.109375
- linear_project: bfloat16 [1024, 4096], P('dp', 'fsdp'), may hold values from -0.1875 to 0.1875
- linear_output: bfloat16 [1024, 1024], P('dp', 'fsdp'), may hold values from -0.1875 to 0.1875
- linear_expand: bfloat16 [1024, 5632], P('dp', 'fsdp'), may hold values from -0.1875 to 0.1875
- linear_shrink: bfloat16 [2816, 1024], P('dp', 'fsdp'), may hold values from -0.109375 to 0.109375
- cotangent: bfloat16 [32, 512, 1024], P(('dp', 'fsdp')), may hold values from -6 to 6
Outputs:
- mixed_out: bfloat16 [32, 512, 1024], P(('dp', 'fsdp'))
- tokens_gradient: float32 [32, 512, 1024], P(('dp', 'fsdp'))
- local_project_gradient: float32 [1024, 4096], P('dp', 'fsdp')
- local_output_gradient: float32 [1024, 1024], P('dp', 'fsdp')
- local_expand_gradient: float32 [1024, 5632], P('dp', 'fsdp')
- local_shrink_gradient: float32 [2816, 1024], P('dp', 'fsdp')
- linear_project_gradient: float32 [1024, 4096], P('dp', 'fsdp')
- linear_output_gradient: float32 [1024, 1024], P('dp', 'fsdp')
- linear_expand_gradient: float32 [1024, 5632], P('dp', 'fsdp')
- linear_shrink_gradient: float32 [2816, 1024], P('dp', 'fsdp')
Inputs may be any that keep to these rules, and one draw needn't show every extreme that they name: `lengths`: number of real tokens of each sequence; slots from there to 512 are padding; some sequence fills all 512 slots.
All inputs are finite; a program needn't handle non-finite values.
Results may differ from a plain program's by a relative error of at most 0.023.
Values may be sent and summed in bfloat16 or wider, within the bound.
A program may use at most 320 MiB of HBM per device.

v0:
```python
import jax
import jax.numpy as jnp
from jax import lax
from jax.sharding import PartitionSpec as P

HEADS = 16
HEAD = 64
BLOCK = 64


epsilon = 1e-05
highest = lax.Precision.HIGHEST


def simple_norm(values):
    return values * lax.rsqrt(jnp.mean(values * values, axis=-1, keepdims=True) + epsilon)


def norm_back(values, upstream):
    inverse_rms = lax.rsqrt(jnp.mean(values * values, axis=-1, keepdims=True) + epsilon)
    return inverse_rms * (
        upstream
        - values * (inverse_rms * inverse_rms) * jnp.mean(upstream * values, axis=-1, keepdims=True)
    )


def head_norm(values):
    shaped = values.reshape(values.shape[0], HEADS, HEAD)
    return simple_norm(shaped).reshape(values.shape)


def head_back(values, upstream):
    shaped = values.reshape(values.shape[0], HEADS, HEAD)
    coming = upstream.reshape(values.shape[0], HEADS, HEAD)
    return norm_back(shaped, coming).reshape(values.shape)


def silu_slope(values):
    logistic = jax.nn.sigmoid(values)
    return logistic * (1.0 + values * (1.0 - logistic))


def contract_rows(first_matrix, second_matrix):
    return lax.dot_general(
        first_matrix, second_matrix, (((0,), (0,)), ((), ())), preferred_element_type=jnp.float32
    )


def contract_cols(first_matrix, second_matrix):
    return lax.dot_general(
        first_matrix, second_matrix, (((1,), (1,)), ((), ())), preferred_element_type=jnp.float32
    )


def causal_table():
    return lax.broadcasted_iota(jnp.int32, (BLOCK, BLOCK), 0) >= lax.broadcasted_iota(
        jnp.int32, (BLOCK, BLOCK), 1
    )


def split_heads(values):
    return values.reshape(values.shape[0] // BLOCK, BLOCK, HEADS, HEAD)


def join_heads(values):
    return values.reshape(values.shape[0] * BLOCK, HEADS * HEAD)


def gather_weights(project, output, expand, shrink):
    wide_parts = (
        lax.all_gather(project, "fsdp", axis=1, tiled=True),
        lax.all_gather(output, "fsdp", axis=1, tiled=True),
        lax.all_gather(expand, "fsdp", axis=1, tiled=True),
        lax.all_gather(shrink, "fsdp", axis=1, tiled=True),
    )
    return (
        lax.all_gather(wide_parts[0], "dp", axis=0, tiled=True),
        lax.all_gather(wide_parts[1], "dp", axis=0, tiled=True),
        lax.all_gather(wide_parts[2], "dp", axis=0, tiled=True),
        lax.all_gather(wide_parts[3], "dp", axis=0, tiled=True),
    )


def settle_gradients(project, output, expand, shrink):
    tall_parts = (
        lax.psum_scatter(
            project.astype(jnp.bfloat16), "dp", scatter_dimension=0, tiled=True
        ).astype(jnp.float32),
        lax.psum_scatter(output.astype(jnp.bfloat16), "dp", scatter_dimension=0, tiled=True).astype(
            jnp.float32
        ),
        lax.psum_scatter(expand.astype(jnp.bfloat16), "dp", scatter_dimension=0, tiled=True).astype(
            jnp.float32
        ),
        lax.psum_scatter(shrink.astype(jnp.bfloat16), "dp", scatter_dimension=0, tiled=True).astype(
            jnp.float32
        ),
    )
    return (
        lax.psum_scatter(
            tall_parts[0].astype(jnp.bfloat16), "fsdp", scatter_dimension=1, tiled=True
        ).astype(jnp.float32),
        lax.psum_scatter(
            tall_parts[1].astype(jnp.bfloat16), "fsdp", scatter_dimension=1, tiled=True
        ).astype(jnp.float32),
        lax.psum_scatter(
            tall_parts[2].astype(jnp.bfloat16), "fsdp", scatter_dimension=1, tiled=True
        ).astype(jnp.float32),
        lax.psum_scatter(
            tall_parts[3].astype(jnp.bfloat16), "fsdp", scatter_dimension=1, tiled=True
        ).astype(jnp.float32),
    )


def local_scores(queries, keys_all):
    query_blocks = split_heads(queries.astype(jnp.bfloat16))
    key_blocks = split_heads(keys_all.astype(jnp.bfloat16))
    scores = jnp.einsum(
        "bihd,bjhd->bhij", query_blocks, key_blocks, preferred_element_type=jnp.float32
    ) * HEAD ** (-0.5)
    return (query_blocks, key_blocks, jnp.where(causal_table(), scores, -1e30))


def local_forward(queries, keys_all, values_low, validity):
    query_blocks, key_blocks, scores = local_scores(queries, keys_all)
    highest_score = jnp.max(scores, axis=-1, keepdims=True)
    expweights = jnp.exp(scores - highest_score)
    row_total = jnp.sum(expweights, axis=-1, keepdims=True)
    attend = (expweights / row_total).astype(jnp.bfloat16)
    mixture = jnp.einsum(
        "bhij,bjhd->bihd", attend, split_heads(values_low), preferred_element_type=jnp.float32
    )
    return (join_heads(mixture) * validity, highest_score + jnp.log(row_total))


def local_backward(queries, keys_all, values_low, validity, logsum, back_mixture):
    query_blocks, key_blocks, scores = local_scores(queries, keys_all)
    value_blocks = split_heads(values_low)
    coming = split_heads(back_mixture * validity.astype(jnp.bfloat16))
    attend = jnp.exp(scores - logsum)
    back_values = jnp.einsum(
        "bhij,bihd->bjhd", attend.astype(jnp.bfloat16), coming, preferred_element_type=jnp.float32
    )
    back_attend = jnp.einsum(
        "bihd,bjhd->bhij", coming, value_blocks, preferred_element_type=jnp.float32
    )
    back_scores = (
        attend * (back_attend - jnp.sum(back_attend * attend, axis=-1, keepdims=True))
    ).astype(jnp.bfloat16)
    back_queries = jnp.einsum(
        "bhij,bjhd->bihd", back_scores, key_blocks, preferred_element_type=jnp.float32
    ) * HEAD ** (-0.5)
    back_keys = jnp.einsum(
        "bhij,bihd->bjhd", back_scores, query_blocks, preferred_element_type=jnp.float32
    ) * HEAD ** (-0.5)
    return (join_heads(back_queries), join_heads(back_keys), join_heads(back_values))


def linear_parts(queries, keys_all, values_low):
    feature_q = split_heads(jax.nn.softplus(queries).astype(jnp.bfloat16))
    feature_k = split_heads(jax.nn.softplus(keys_all).astype(jnp.bfloat16))
    value_blocks = split_heads(values_low)
    causal = causal_table().astype(jnp.float32)
    inner_scores = (
        jnp.einsum("bihd,bjhd->bhij", feature_q, feature_k, preferred_element_type=jnp.float32)
        * causal
    ).astype(jnp.bfloat16)
    states = jnp.einsum(
        "bjhd,bjhe->bhde", feature_k, value_blocks, preferred_element_type=jnp.float32
    )
    running = jnp.cumsum(states, axis=0)
    prior_states = jnp.concatenate([jnp.zeros_like(states[:1]), running[:-1]], axis=0)
    return (feature_q, feature_k, value_blocks, causal, inner_scores, prior_states)


def linear_forward(queries, keys_all, values_low):
    feature_q, feature_k, value_blocks, causal, inner_scores, prior_states = linear_parts(
        queries, keys_all, values_low
    )
    mixture = jnp.einsum(
        "bhij,bjhe->bihe", inner_scores, value_blocks, preferred_element_type=jnp.float32
    )
    mixture = mixture + jnp.einsum(
        "bihd,bhde->bihe", feature_q.astype(jnp.float32), prior_states, precision=highest
    )
    return join_heads(mixture)


def linear_backward(queries, keys_all, values_low, back_mixture):
    feature_q, feature_k, value_blocks, causal, inner_scores, prior_states = linear_parts(
        queries, keys_all, values_low
    )
    coming = split_heads(back_mixture)
    coming_wide = coming.astype(jnp.float32)
    back_inner = (
        jnp.einsum("bihe,bjhe->bhij", coming, value_blocks, preferred_element_type=jnp.float32)
        * causal
    ).astype(jnp.bfloat16)
    back_feature_q = jnp.einsum(
        "bhij,bjhd->bihd", back_inner, feature_k, preferred_element_type=jnp.float32
    )
    back_feature_q = back_feature_q + jnp.einsum(
        "bihe,bhde->bihd", coming_wide, prior_states, precision=highest
    )
    back_feature_k = jnp.einsum(
        "bhij,bihd->bjhd", back_inner, feature_q, preferred_element_type=jnp.float32
    )
    back_values = jnp.einsum(
        "bhij,bihe->bjhe", inner_scores, coming, preferred_element_type=jnp.float32
    )
    back_prior = jnp.einsum(
        "bihd,bihe->bhde", feature_q.astype(jnp.float32), coming_wide, precision=highest
    )
    running = jnp.cumsum(back_prior[::-1], axis=0)[::-1]
    later_states = jnp.concatenate([running[1:], jnp.zeros_like(running[:1])], axis=0)
    back_feature_k = back_feature_k + jnp.einsum(
        "bjhe,bhde->bjhd", value_blocks.astype(jnp.float32), later_states, precision=highest
    )
    back_values = back_values + jnp.einsum(
        "bjhd,bhde->bjhe", feature_k.astype(jnp.float32), later_states, precision=highest
    )
    return (
        join_heads(back_feature_q) * jax.nn.sigmoid(queries),
        join_heads(back_feature_k) * jax.nn.sigmoid(keys_all),
        join_heads(back_values),
    )


def forward_layer(layer_in, validity, weights, local):
    project, output, expand, shrink = weights
    normed = simple_norm(layer_in).astype(jnp.bfloat16)
    projected = jnp.dot(normed, project, preferred_element_type=jnp.float32)
    queries, keys_all, values, update = jnp.split(projected, 4, axis=1)
    values_low = values.astype(jnp.bfloat16)
    if local:
        mixture, logsum = local_forward(queries, keys_all, values_low, validity)
    else:
        mixture = linear_forward(queries, keys_all, values_low)
        logsum = None
    gated_rows = (head_norm(mixture) * jax.nn.silu(update)).astype(jnp.bfloat16)
    middle = layer_in + jnp.dot(gated_rows, output, preferred_element_type=jnp.float32)
    second = simple_norm(middle).astype(jnp.bfloat16)
    expanded = jnp.dot(second, expand, preferred_element_type=jnp.float32)
    half_width = expanded.shape[1] // 2
    hidden = (expanded[:, :half_width] * expanded[:, half_width:]).astype(jnp.bfloat16)
    result = middle + jnp.dot(hidden, shrink, preferred_element_type=jnp.float32)
    return (
        result,
        (layer_in, normed, projected, values_low, mixture, logsum, gated_rows, middle, second),
    )


def backward_layer(upstream, saved, weights, validity, local):
    project, output, expand, shrink = weights
    layer_in, normed, projected, values_low, mixture, logsum, gated_rows, middle, second = saved
    expanded = jnp.dot(second, expand, preferred_element_type=jnp.float32)
    half_width = expanded.shape[1] // 2
    first_half = expanded[:, :half_width]
    second_half = expanded[:, half_width:]
    hidden = (first_half * second_half).astype(jnp.bfloat16)
    back_branch = upstream.astype(jnp.bfloat16)
    shrink_term = contract_rows(hidden, back_branch)
    back_hidden = contract_cols(back_branch, shrink)
    back_expanded = jnp.concatenate(
        [back_hidden * second_half, back_hidden * first_half], axis=1
    ).astype(jnp.bfloat16)
    expand_term = contract_rows(second, back_expanded)
    back_second = contract_cols(back_expanded, expand)
    back_middle = upstream + norm_back(middle, back_second)
    back_gated = back_middle.astype(jnp.bfloat16)
    output_term = contract_rows(gated_rows, back_gated)
    back_rows_gated = contract_cols(back_gated, output)
    queries, keys_all, unused_values, update = jnp.split(projected, 4, axis=1)
    back_update = back_rows_gated * head_norm(mixture) * silu_slope(update)
    back_mixture = head_back(mixture, back_rows_gated * jax.nn.silu(update)).astype(jnp.bfloat16)
    if local:
        back_queries, back_keys, back_values = local_backward(
            queries, keys_all, values_low, validity, logsum, back_mixture
        )
    else:
        back_queries, back_keys, back_values = linear_backward(
            queries, keys_all, values_low, back_mixture
        )
    back_projected = jnp.concatenate(
        [back_queries, back_keys, back_values, back_update], axis=1
    ).astype(jnp.bfloat16)
    project_term = contract_rows(normed, back_projected)
    back_normed = contract_cols(back_projected, project)
    back_input = back_middle + norm_back(layer_in, back_normed)
    return (back_input, (project_term, output_term, expand_term, shrink_term))


def shards(
    tokens,
    lengths,
    local_project,
    local_output,
    local_expand,
    local_shrink,
    linear_project,
    linear_output,
    linear_expand,
    linear_shrink,
    cotangent,
):
    positions = lax.broadcasted_iota(jnp.int32, (tokens.shape[1], 1), 0)
    validity = (positions < lengths[0]).astype(jnp.float32)
    layer_in = tokens[0].astype(jnp.float32) * validity
    local_weights = gather_weights(local_project, local_output, local_expand, local_shrink)
    between, local_saved = forward_layer(layer_in, validity, local_weights, True)
    linear_weights = gather_weights(linear_project, linear_output, linear_expand, linear_shrink)
    result, linear_saved = forward_layer(between, validity, linear_weights, False)
    result = result * validity
    linear_again = gather_weights(linear_project, linear_output, linear_expand, linear_shrink)
    upstream = cotangent[0].astype(jnp.float32) * validity
    back_between, linear_terms = backward_layer(
        upstream, linear_saved, linear_again, validity, False
    )
    linear_sums = settle_gradients(
        linear_terms[0], linear_terms[1], linear_terms[2], linear_terms[3]
    )
    local_again = gather_weights(local_project, local_output, local_expand, local_shrink)
    back_input, local_terms = backward_layer(back_between, local_saved, local_again, validity, True)
    local_sums = settle_gradients(local_terms[0], local_terms[1], local_terms[2], local_terms[3])
    return (
        result.astype(jnp.bfloat16)[None],
        (back_input * validity)[None],
        local_sums[0],
        local_sums[1],
        local_sums[2],
        local_sums[3],
        linear_sums[0],
        linear_sums[1],
        linear_sums[2],
        linear_sums[3],
    )


def solution(mesh):
    in_specs = (
        P(("dp", "fsdp"), None, None),
        P(("dp", "fsdp")),
        P("dp", "fsdp"),
        P("dp", "fsdp"),
        P("dp", "fsdp"),
        P("dp", "fsdp"),
        P("dp", "fsdp"),
        P("dp", "fsdp"),
        P("dp", "fsdp"),
        P("dp", "fsdp"),
        P(("dp", "fsdp"), None, None),
    )
    out_specs = (
        P(("dp", "fsdp"), None, None),
        P(("dp", "fsdp"), None, None),
        P("dp", "fsdp"),
        P("dp", "fsdp"),
        P("dp", "fsdp"),
        P("dp", "fsdp"),
        P("dp", "fsdp"),
        P("dp", "fsdp"),
        P("dp", "fsdp"),
        P("dp", "fsdp"),
    )
    return jax.shard_map(shards, mesh=mesh, in_specs=in_specs, out_specs=out_specs, check_vma=False)
```

profile of v0, /device:TPU:0, one launch (start us, length us, event | category | flops | bytes accessed | tf_op | source)
XLA Modules:
  0.0 1588.6 jit_solution(8273537100092221456)
XLA Ops:
  7.2 12.0 all_gather.64
  19.3 5.3 all_gather.66
  24.7 11.2 all_gather.68
  36.0 6.4 all_gather.70
  42.5 7.7 all_gather.72
  50.3 5.7 all_gather.74
  56.1 10.1 all_gather.76
  66.4 6.3 all_gather.78
  74.5 20.2 %all-gather.9.cloned.1.call-done = bf16[1024,4096]{1,0:T(8,128)(2,1)} async-done(((bf16[64,4096]{1,0:T(8,128)(2,1)}), bf16[1024,4096]{1,0:T(8,128)(2,1)}) %all-gather.9.cloned.1.call-update) | async-done | bytes 8388624 | tf_op jit(solution)/shard_map/all_gather | solution.py:77
  94.7 10.3 fusion.95
  133.2 5.7 copy.172
  151.4 80.5 %all-gather.13.cloned.1.call-done = bf16[1024,5632]{1,0:T(8,128)(2,1)} async-done(((bf16[64,5632]{1,0:T(8,128)(2,1)}), bf16[1024,5632]{1,0:T(8,128)(2,1)}) %all-gather.13.cloned.1.call-update) | async-done | bytes 11534352 | tf_op jit(solution)/shard_map/all_gather | solution.py:79
  231.9 9.1 fusion.88
  245.7 45.6 %all-gather.15.cloned.1.call-done = bf16[2816,1024]{1,0:T(8,128)(2,1)} async-done(((bf16[176,1024]{1,0:T(8,128)(2,1)}), bf16[2816,1024]{1,0:T(8,128)(2,1)}) %all-gather.15.cloned.1.call-update) | async-done | bytes 5767184 | tf_op jit(solution)/shard_map/all_gather | solution.py:80
  291.3 7.4 multiply_reduce_fusion.9
  299.2 67.6 %all-gather.17.cloned.1.call-done = bf16[1024,4096]{1,0:T(8,128)(2,1)} async-done(((bf16[64,4096]{1,0:T(8,128)(2,1)}), bf16[1024,4096]{1,0:T(8,128)(2,1)}) %all-gather.17.cloned.1.call-update) | async-done | bytes 8388624 | tf_op jit(solution)/shard_map/all_gather | solution.py:77
  366.9 7.7 fusion.89
  380.9 5.5 fusion.15
  404.7 5.6 fusion.97
  415.7 5.3 copy.188
  420.9 5.6 copy.183
  445.4 5.2 multiply_convert_fusion.19
  450.6 5.3 multiply_reduce_fusion.8
  455.9 48.0 %all-gather.21.cloned.1.call-done = bf16[1024,5632]{1,0:T(8,128)(2,1)} async-done(((bf16[64,5632]{1,0:T(8,128)(2,1)}), bf16[1024,5632]{1,0:T(8,128)(2,1)}) %all-gather.21.cloned.1.call-update) | async-done | bytes 11534352 | tf_op jit(solution)/shard_map/all_gather | solution.py:79
  504.0 12.6 fusion.90
  516.5 47.0 %all-gather.23.cloned.1.call-done = bf16[2816,1024]{1,0:T(8,128)(2,1)} async-done(((bf16[176,1024]{1,0:T(8,128)(2,1)}), bf16[2816,1024]{1,0:T(8,128)(2,1)}) %all-gather.23.cloned.1.call-update) | async-done | bytes 5767184 | tf_op jit(solution)/shard_map/all_gather | solution.py:80
  563.5 11.3 multiply_convert_fusion.3
  574.9 11.2 multiply_reduce_fusion.7
  590.7 7.0 fusion.71
  608.1 5.1 multiply_convert_fusion.16
  620.0 5.0 multiply_convert_fusion.9
  642.3 8.6 fusion.50
  650.9 5.8 fusion.41
  665.6 5.7 copy.195
  676.3 5.8 add_bitcast_fusion
  690.2 5.7 copy.200
  695.9 5.4 reshape.280
  701.3 5.5 multiply_convert_fusion.15
  706.8 11.0 multiply_reduce_fusion.5
  722.4 9.0 multiply_convert_fusion.1
  731.4 11.3 multiply_reduce_fusion.4
  747.5 7.9 convolution_convert_fusion.4
  755.5 7.0 convolution_convert_fusion.5
  764.1 9.9 convolution_convert_fusion.2
  774.7 7.5 copy.207
  789.3 7.1 fusion.70
  816.6 5.0 convert_bitcast_fusion
  851.9 10.1 convolution_convert_fusion.3
  863.7 11.7 convolution_convert_fusion
  877.2 11.7 convolution_convert_fusion.1
  892.3 84.5 %reduce-scatter.29.cloned.1.call-done = bf16[176,1024]{1,0:T(8,128)(2,1)} async-done(((bf16[2816,1024]{1,0:T(8,128)(2,1)}), bf16[176,1024]{1,0:T(8,128)(2,1)}) %reduce-scatter.29.cloned.1.call-update) | async-done | bytes 360464 | tf_op jit(solution)/shard_map/reduce_scatter | solution.py:95
  976.8 107.8 %reduce-scatter.33.cloned.1.call-done = bf16[64,4096]{1,0:T(8,128)(2,1)} async-done(((bf16[1024,4096]{1,0:T(8,128)(2,1)}), bf16[64,4096]{1,0:T(8,128)(2,1)}) %reduce-scatter.33.cloned.1.call-update) | async-done | bytes 524304 | tf_op jit(solution)/shard_map/reduce_scatter | solution.py:86
  1084.7 108.2 %reduce-scatter.17.cloned.1.call-done = bf16[64,4096]{1,0:T(8,128)(2,1)} async-done(((bf16[1024,4096]{1,0:T(8,128)(2,1)}), bf16[64,4096]{1,0:T(8,128)(2,1)}) %reduce-scatter.17.cloned.1.call-update) | async-done | bytes 524304 | tf_op jit(solution)/shard_map/reduce_scatter | solution.py:86
  1192.9 129.9 %reduce-scatter.41.cloned.1.call-done = bf16[64,5632]{1,0:T(8,128)(2,1)} async-done(((bf16[1024,5632]{1,0:T(8,128)(2,1)}), bf16[64,5632]{1,0:T(8,128)(2,1)}) %reduce-scatter.41.cloned.1.call-update) | async-done | bytes 720912 | tf_op jit(solution)/shard_map/reduce_scatter | solution.py:92
  1323.2 10.6 fusion.31
  1333.8 119.6 %reduce-scatter.25.cloned.1.call-done = bf16[64,5632]{1,0:T(8,128)(2,1)} async-done(((bf16[1024,5632]{1,0:T(8,128)(2,1)}), bf16[64,5632]{1,0:T(8,128)(2,1)}) %reduce-scatter.25.cloned.1.call-update) | async-done | bytes 720912 | tf_op jit(solution)/shard_map/reduce_scatter | solution.py:92
  1457.2 6.7 fusion.47
  1467.1 10.8 reduce-scatter.23.cloned.1.call-done
  1479.5 13.5 reduce-scatter.47.cloned.1.call-done
  1494.7 13.2 reduce-scatter.31.cloned.1.call-done
  1509.5 15.1 reduce-scatter.35.cloned.1.call-done
  1526.5 15.1 reduce-scatter.19.cloned.1.call-done
  1543.4 17.3 %reduce-scatter.43.cloned.1.call-done = bf16[64,2816]{1,0:T(8,128)(2,1)} async-done(((bf16[64,5632]{1,0:T(8,128)(2,1)}), bf16[64,2816]{1,0:T(8,128)(2,1)}) %reduce-scatter.43.cloned.1.call-update) | async-done | bytes 360464 | tf_op jit(solution)/shard_map/reduce_scatter | solution.py:106
  1562.5 17.1 %reduce-scatter.27.cloned.1.call-done = bf16[64,2816]{1,0:T(8,128)(2,1)} async-done(((bf16[64,5632]{1,0:T(8,128)(2,1)}), bf16[64,2816]{1,0:T(8,128)(2,1)}) %reduce-scatter.27.cloned.1.call-update) | async-done | bytes 360464 | tf_op jit(solution)/shard_map/reduce_scatter | solution.py:106
  (305 shorter events, 252.8 us)
Async XLA Ops:
  7.2 28.8 %copy-start.51 = (bf16[176,512]{1,0:T(8,128)(2,1)S(1)}, bf16[176,512]{1,0:T(8,128)(2,1)}, u32[]{:S(2)}) copy-start(bf16[176,512]{1,0:T(8,128)(2,1)} %param.16) | copy-start | bytes 540676
  7.2 35.3 %copy-start.50 = (bf16[64,2048]{1,0:T(8,128)(2,1)S(1)}, bf16[64,2048]{1,0:T(8,128)(2,1)}, u32[]{:S(2)}) copy-start(bf16[64,2048]{1,0:T(8,128)(2,1)} %param.17) | copy-start | bytes 786436
  7.2 87.5 %all-gather.9.cloned.1.call-start = ((), (), s32[]{:S(2)}) async-start(), calls=%async_computation.16 | async-start | bytes 8912896 | tf_op jit(solution)/shard_map/all_gather | solution.py:77
  19.3 128.2 %all-gather.11.cloned.1.call-start = ((), (), s32[]{:S(2)}) async-start(), calls=%async_computation.17 | async-start | bytes 2228224 | tf_op jit(solution)/shard_map/all_gather | solution.py:78
  24.6 25.7 %copy-start.53 = (bf16[64,512]{1,0:T(8,128)(2,1)S(1)}, bf16[64,512]{1,0:T(8,128)(2,1)}, u32[]{:S(2)}) copy-start(bf16[64,512]{1,0:T(8,128)(2,1)} %param.18) | copy-start | bytes 196612
  24.6 31.5 %copy-start.47 = (bf16[64,2816]{1,0:T(8,128)(2,1)S(1)}, bf16[64,2816]{1,0:T(8,128)(2,1)}, u32[]{:S(2)}) copy-start(bf16[64,2816]{1,0:T(8,128)(2,1)} %param.19) | copy-start | bytes 1081348
  24.6 207.3 %all-gather.13.cloned.1.call-start = ((), (), s32[]{:S(2)}) async-start(), calls=%async_computation.18 | async-start | bytes 12255232 | tf_op jit(solution)/shard_map/all_gather | solution.py:79
  36.0 30.4 %copy-start.52 = (bf16[176,512]{1,0:T(8,128)(2,1)S(1)}, bf16[176,512]{1,0:T(8,128)(2,1)}, u32[]{:S(2)}) copy-start(bf16[176,512]{1,0:T(8,128)(2,1)} %param.20) | copy-start | bytes 540676
  36.0 255.3 %all-gather.15.cloned.1.call-start = ((), (), s32[]{:S(2)}) async-start(), calls=%async_computation.19 | async-start | bytes 6127616 | tf_op jit(solution)/shard_map/all_gather | solution.py:80
  42.5 30.9 %copy-start.30 = (bf16[1,512,1024]{2,1,0:T(8,128)(2,1)S(1)}, bf16[1,512,1024]{2,1,0:T(8,128)(2,1)}, u32[]{:S(2)}) copy-start(bf16[1,512,1024]{2,1,0:T(8,128)(2,1)} %param.11) | copy-start | bytes 3145732
  42.5 324.4 %all-gather.17.cloned.1.call-start = ((), (), s32[]{:S(2)}) async-start(), calls=%async_computation.20 | async-start | bytes 8912896 | tf_op jit(solution)/shard_map/all_gather | solution.py:77
  50.3 400.4 %all-gather.19.cloned.1.call-start = ((), (), s32[]{:S(2)}) async-start(), calls=%async_computation.21 | async-start | bytes 2228224 | tf_op jit(solution)/shard_map/all_gather | solution.py:78
  56.1 447.9 %all-gather.21.cloned.1.call-start = ((), (), s32[]{:S(2)}) async-start(), calls=%async_computation.22 | async-start | bytes 12255232 | tf_op jit(solution)/shard_map/all_gather | solution.py:79
  66.3 497.2 %all-gather.23.cloned.1.call-start = ((), (), s32[]{:S(2)}) async-start(), calls=%async_computation.23 | async-start | bytes 6127616 | tf_op jit(solution)/shard_map/all_gather | solution.py:80
  72.7 816.4 %reduce-scatter.37.cloned.1.call-start = ((), (), s32[]{:S(2)}) async-start(), calls=%async_computation.34 | async-start | bytes 2228224 | tf_op jit(solution)/shard_map/reduce_scatter | solution.py:89
  74.4 30.6 %copy-start.55 = (f32[512]{0:T(512)}, f32[512]{0:T(512)S(1)}, u32[]{:S(2)}) copy-start(f32[512]{0:T(512)S(1)} %get-tuple-element.29) | copy-start | bytes 6148
  142.6 4.9 copy-start.16
  142.6 4.9 copy-start.31
  150.8 81.1 %copy-start.37 = (f32[512,1024]{1,0:T(8,128)}, f32[512,1024]{1,0:T(8,128)S(1)}, u32[]{:S(2)}) copy-start(f32[512,1024]{1,0:T(8,128)S(1)} %get-tuple-element.43) | copy-start | bytes 6291460
  151.4 89.6 %copy-start.57 = (f32[512]{0:T(512)}, f32[512]{0:T(512)S(1)}, u32[]{:S(2)}) copy-start(f32[512]{0:T(512)S(1)} %get-tuple-element.31) | copy-start | bytes 6148
  245.7 52.9 %copy-start.33 = (bf16[512,2816]{1,0:T(8,128)(2,1)}, bf16[512,2816]{1,0:T(8,128)(2,1)S(1)}, u32[]{:S(2)}) copy-start(bf16[512,2816]{1,0:T(8,128)(2,1)S(1)} %multiply_convert_fusion.5) | copy-start | bytes 8650756
  299.2 75.3 %copy-start.61 = (f32[512]{0:T(512)}, f32[512]{0:T(512)S(1)}, u32[]{:S(2)}) copy-start(f32[512]{0:T(512)S(1)} %get-tuple-element.33) | copy-start | bytes 6148
  455.9 130.2 %copy-start.59 = (f32[512]{0:T(512)}, f32[512]{0:T(512)S(1)}, u32[]{:S(2)}) copy-start(f32[512]{0:T(512)S(1)} %get-tuple-element.35) | copy-start | bytes 6148
  563.5 11.3 copy-start.34
  574.8 11.3 copy-start.66
  574.8 11.3 copy-start.67
  574.8 11.3 copy-start.41
  619.9 5.0 copy-start.6
  642.3 8.6 copy-start
  642.3 8.6 copy-start.11
  656.7 232.9 %reduce-scatter.21.cloned.1.call-start = ((), (), s32[]{:S(2)}) async-start(), calls=%async_computation.26 | async-start | bytes 2228224 | tf_op jit(solution)/shard_map/reduce_scatter | solution.py:89
  676.3 5.8 copy-start.8
  676.3 5.8 copy-start.19
  676.3 6.8 copy-start.23
  695.9 5.4 copy-start.25
  701.3 21.1 %slice-start = ((s8[11534336]{0:T(1024)(128)(4,1)}), s8[4194304]{0:T(1024)(128)(4,1)S(1)}, s32[]{:S(2)}) async-start(s8[11534336]{0:T(1024)(128)(4,1)} %bitcast.131), calls=%async_computation.40 | async-start | bytes 8388608
  706.8 11.0 copy-start.62
  706.8 11.0 copy-start.64
  706.8 15.6 slice-start.1
  706.8 15.6 slice-start.2
  731.4 11.4 copy-start.21
  731.4 11.4 copy-start.38
  731.4 11.4 copy-start.58
  731.4 11.4 copy-start.63
  747.3 144.9 %reduce-scatter.45.cloned.1.call-start = ((), (), s32[]{:S(2)}) async-start(), calls=%async_computation.38 | async-start | bytes 6127616 | tf_op jit(solution)/shard_map/reduce_scatter | solution.py:95
  755.4 221.3 %reduce-scatter.29.cloned.1.call-start = ((), (), s32[]{:S(2)}) async-start(), calls=%async_computation.30 | async-start | bytes 6127616 | tf_op jit(solution)/shard_map/reduce_scatter | solution.py:95
  762.5 322.1 %reduce-scatter.33.cloned.1.call-start = ((), (), s32[]{:S(2)}) async-start(), calls=%async_computation.32 | async-start | bytes 8912896 | tf_op jit(solution)/shard_map/reduce_scatter | solution.py:86
  774.0 418.9 %reduce-scatter.17.cloned.1.call-start = ((), (), s32[]{:S(2)}) async-start(), calls=%async_computation.24 | async-start | bytes 8912896 | tf_op jit(solution)/shard_map/reduce_scatter | solution.py:86
  784.3 5.0 copy-start.44
  784.3 5.0 copy-start.49
  784.3 5.0 copy-start.17
  830.8 4.5 copy-start.4
  862.1 460.8 %reduce-scatter.41.cloned.1.call-start = ((), (), s32[]{:S(2)}) async-start(), calls=%async_computation.36 | async-start | bytes 12255232 | tf_op jit(solution)/shard_map/reduce_scatter | solution.py:92
  875.5 578.0 %reduce-scatter.25.cloned.1.call-start = ((), (), s32[]{:S(2)}) async-start(), calls=%async_computation.28 | async-start | bytes 12255232 | tf_op jit(solution)/shard_map/reduce_scatter | solution.py:92
  889.0 576.6 %reduce-scatter.39.cloned.1.call-start = ((), (), s32[]{:S(2)}) async-start(), calls=%async_computation.35 | async-start | bytes 196608 | tf_op jit(solution)/shard_map/reduce_scatter | solution.py:103
  889.6 588.4 %reduce-scatter.23.cloned.1.call-start = ((), (), s32[]{:S(2)}) async-start(), calls=%async_computation.27 | async-start | bytes 196608 | tf_op jit(solution)/shard_map/reduce_scatter | solution.py:103
  890.1 602.8 %reduce-scatter.47.cloned.1.call-start = ((), (), s32[]{:S(2)}) async-start(), calls=%async_computation.39 | async-start | bytes 540672 | tf_op jit(solution)/shard_map/reduce_scatter | solution.py:109
  892.2 615.6 %reduce-scatter.31.cloned.1.call-start = ((), (), s32[]{:S(2)}) async-start(), calls=%async_computation.31 | async-start | bytes 540672 | tf_op jit(solution)/shard_map/reduce_scatter | solution.py:109
  976.8 547.9 %reduce-scatter.35.cloned.1.call-start = ((), (), s32[]{:S(2)}) async-start(), calls=%async_computation.33 | async-start | bytes 786432 | tf_op jit(solution)/shard_map/reduce_scatter | solution.py:100
  1084.6 457.0 %reduce-scatter.19.cloned.1.call-start = ((), (), s32[]{:S(2)}) async-start(), calls=%async_computation.25 | async-start | bytes 786432 | tf_op jit(solution)/shard_map/reduce_scatter | solution.py:100
  1192.9 367.7 %reduce-scatter.43.cloned.1.call-start = ((), (), s32[]{:S(2)}) async-start(), calls=%async_computation.37 | async-start | bytes 1081344 | tf_op jit(solution)/shard_map/reduce_scatter | solution.py:106
  1322.9 130.6 %copy-start.54 = (f32[512]{0:T(512)S(1)}, f32[512]{0:T(512)}, u32[]{:S(2)}) copy-start(f32[512]{0:T(512)} %get-tuple-element.28) | copy-start | bytes 6148
  1322.9 256.7 %reduce-scatter.27.cloned.1.call-start = ((), (), s32[]{:S(2)}) async-start(), calls=%async_computation.29 | async-start | bytes 1081344 | tf_op jit(solution)/shard_map/reduce_scatter | solution.py:106
  1323.2 130.3 %copy-start.28 = (f32[512,1024]{1,0:T(8,128)S(1)}, f32[512,1024]{1,0:T(8,128)}, u32[]{:S(2)}) copy-start(f32[512,1024]{1,0:T(8,128)} %copy-done.27) | copy-start | bytes 6291460
  (31 other events, 78.7 us)
Sparse Core Ops, SparseCore 0:
  19.4 75.2 all-gather.8
  96.8 39.6 all-gather.10
  138.8 93.0 all-gather.12
  234.1 57.1 all-gather.14
  293.3 73.4 all-gather.16
  368.9 39.6 all-gather.18
  410.8 93.0 all-gather.20
  506.2 57.1 all-gather.22
  656.9 60.2 reduce-scatter.36
  747.4 60.1 reduce-scatter.20
  811.6 80.5 reduce-scatter.44
  896.0 80.7 reduce-scatter.28
  980.8 103.7 reduce-scatter.32
  1088.5 104.3 reduce-scatter.16
  1196.8 126.0 reduce-scatter.40
  1327.4 126.0 reduce-scatter.24
  1455.5 10.0 reduce-scatter.38
  1467.7 10.2 reduce-scatter.22
  1480.2 12.7 reduce-scatter.46
  1495.1 12.7 reduce-scatter.30
  1510.1 14.5 reduce-scatter.34
  1527.0 14.5 reduce-scatter.18
  1543.9 16.7 reduce-scatter.42
  1562.8 16.7 reduce-scatter.26
where the time goes:
time: 1600 us; the launch traced here: 1590 us
  waiting for transfers between devices  966 us (60%)
  matrix products  271 us (17%)
  local copies, waits for them, and re-layouts  196 us (12%)
  other arithmetic  72.6 us (5%)
  blocking collectives  64.8 us (4%)
  between operations  16.3 us (1%)
    reduce_scatter x2, waiting for transfers between devices, settle_gradients(): lax.psum_scatter(expand.astype(jnp.bfloat16), 'dp', scatter_dimension=0,...  250 us
    reduce_scatter x2, waiting for transfers between devices, settle_gradients(): lax.psum_scatter(project.astype(jnp.bfloat16), 'dp', scatter_dimension=0,...  216 us
    all_gather x2, waiting for transfers between devices, gather_weights(): lax.all_gather(wide_parts[2], 'dp', axis=0, tiled=True)  129 us
    all_gather x2, waiting for transfers between devices, gather_weights(): lax.all_gather(wide_parts[3], 'dp', axis=0, tiled=True)  92.5 us
    all_gather x2, waiting for transfers between devices, gather_weights(): lax.all_gather(wide_parts[0], 'dp', axis=0, tiled=True)  87.8 us
    reduce_scatter x2, waiting for transfers between devices, settle_gradients(): lax.psum_scatter(shrink.astype(jnp.bfloat16), 'dp', scatter_dimension=0,...  86.5 us
    dot_general x8, matrix products, contract_cols(): lax.dot_general(first_matrix, second_matrix, (((1,), (1,)), ((), ())), pr...  78.6 us
    dot_general x8, matrix products, contract_rows(): lax.dot_general(first_matrix, second_matrix, (((0,), (0,)), ((), ())), pr...  63.6 us
  transfers between devices with their start and end apart: 24, of which 20 were waited for; matrix products, arithmetic and copies ran while one was open for 27% of the time, Pallas kernels for 0%

commit v1 on v0

--- a/solution.py
+++ b/solution.py
@@ -1,6 +1,10 @@
+import functools
+
 import jax
 import jax.numpy as jnp
 from jax import lax
+from jax.experimental import pallas as pl
+from jax.experimental.pallas import tpu as pltpu
 from jax.sharding import PartitionSpec as P
 
 HEADS = 16
@@ -66,50 +70,375 @@
     return values.reshape(values.shape[0] * BLOCK, HEADS * HEAD)
 
 
-def gather_weights(project, output, expand, shrink):
-    wide_parts = (
-        lax.all_gather(project, "fsdp", axis=1, tiled=True),
-        lax.all_gather(output, "fsdp", axis=1, tiled=True),
-        lax.all_gather(expand, "fsdp", axis=1, tiled=True),
-        lax.all_gather(shrink, "fsdp", axis=1, tiled=True),
-    )
-    return (
-        lax.all_gather(wide_parts[0], "dp", axis=0, tiled=True),
-        lax.all_gather(wide_parts[1], "dp", axis=0, tiled=True),
-        lax.all_gather(wide_parts[2], "dp", axis=0, tiled=True),
-        lax.all_gather(wide_parts[3], "dp", axis=0, tiled=True),
-    )
-
-
-def settle_gradients(project, output, expand, shrink):
-    tall_parts = (
-        lax.psum_scatter(
-            project.astype(jnp.bfloat16), "dp", scatter_dimension=0, tiled=True
-        ).astype(jnp.float32),
-        lax.psum_scatter(output.astype(jnp.bfloat16), "dp", scatter_dimension=0, tiled=True).astype(
-            jnp.float32
+MESH = pl.DeviceIdType.MESH
+ANY = pl.BlockSpec(memory_space=pl.ANY)
+WEIGHTS = 8
+AXIS_NAMES = ("f", "zh", "zl", "y", "c")
+AXIS_OF = {"c": "c", "y": "y", "x": "f", "z1": "zl", "z2": "zh"}
+GATHER_LAG = 3
+GATHER_SLOTS = 8
+SCATTER_LAG = 3
+SCATTER_SLOTS = 3 * SCATTER_LAG + 1
+TERM_SLOTS = SCATTER_LAG + 1
+TALL = 64
+TALL_WIDTH = 256
+OTHER_WIDTH = 128
+
+
+def neighbours():
+    dp = lax.axis_index("dp")
+    x = lax.axis_index("fsdp")
+    z = dp // 4
+    y = (dp // 2) % 2
+    c = dp % 2
+    places = {"f": x, "zh": z // 2, "zl": z % 2, "y": y, "c": c}
+    targets = {
+        "z1": ((z + 1 - 2 * (z % 2)) * 4 + y * 2 + c, x),
+        "z2": (lax.rem(z + 2, 4) * 4 + y * 2 + c, x),
+        "y": (z * 4 + (1 - y) * 2 + c, x),
+        "c": (z * 4 + y * 2 + (1 - c), x),
+        "x": (dp, 1 - x),
+    }
+    return places, targets
+
+
+def greet(targets):
+    barrier = pltpu.get_barrier_semaphore()
+    for target in targets.values():
+        pl.semaphore_signal(barrier, inc=1, device_id=target, device_id_type=MESH)
+    return barrier
+
+
+def late_z(chunk):
+    return chunk % 5 == 3
+
+
+def gather_kernel(chunks, *refs):
+    own = refs[:WEIGHTS]
+    held = refs[WEIGHTS : 2 * WEIGHTS]
+    local_sem, send_sem, recv_sem = refs[2 * WEIGHTS :]
+    places, targets = neighbours()
+    x, zh, zl, y, c = (places[name] for name in AXIS_NAMES)
+    barrier = greet(targets)
+    local = [
+        pltpu.make_async_copy(own[i], held[i].at[x, zh, zl, y, c], local_sem.at[i])
+        for i in range(WEIGHTS)
+    ]
+    for copy in local:
+        copy.start()
+    pl.semaphore_wait(barrier, len(targets))
+
+    def messages(phase, chunk):
+        weight, start, width = chunks[chunk]
+        ref = held[weight]
+        half = width // 2
+        every = pl.ds(start, width)
+        first = pl.ds(start, half)
+        second = pl.ds(start + half, half)
+
+        def message(block, target, part):
+            slot = chunk % GATHER_SLOTS
+            return pltpu.make_async_remote_copy(
+                src_ref=block,
+                dst_ref=block,
+                send_sem=send_sem.at[2 * phase + part, slot],
+                recv_sem=recv_sem.at[2 * phase + part, slot],
+                device_id=targets[target],
+                device_id_type=MESH,
+            )
+
+        if phase == 4:
+            return [message(ref.at[:, :, :, :, c, :, every], "c", 0)]
+        if late_z(chunk):
+            if phase == 0:
+                return [
+                    message(ref.at[x, zh, zl, y, c, :, first], "x", 0),
+                    message(ref.at[x, zh, zl, y, c, :, second], "y", 1),
+                ]
+            if phase == 1:
+                return [
+                    message(ref.at[:, zh, zl, y, c, :, first], "y", 0),
+                    message(ref.at[x, zh, zl, :, c, :, second], "x", 1),
+                ]
+            if phase == 2:
+                return [message(ref.at[:, zh, zl, :, c, :, every], "z2", 0)]
+            return [message(ref.at[:, :, zl, :, c, :, every], "z1", 0)]
+        if phase == 0:
+            return [message(ref.at[x, zh, zl, y, c, :, every], "z2", 0)]
+        if phase == 1:
+            return [message(ref.at[x, :, zl, y, c, :, every], "z1", 0)]
+        if phase == 2:
+            return [
+                message(ref.at[x, :, :, y, c, :, first], "x", 0),
+                message(ref.at[x, :, :, y, c, :, second], "y", 1),
+            ]
+        return [
+            message(ref.at[:, :, :, y, c, :, first], "y", 0),
+            message(ref.at[x, :, :, :, c, :, second], "x", 1),
+        ]
+
+    phases = 5
+    landed = set()
+    live = {}
+    for step in range(len(chunks) + phases * GATHER_LAG):
+        for phase in range(phases, -1, -1):
+            chunk = step - phase * GATHER_LAG
+            if not 0 <= chunk < len(chunks):
+                continue
+            if phase >= 1:
+                for copy in live.pop((phase - 1, chunk)):
+                    copy.wait()
+            weight = chunks[chunk][0]
+            if phase == 0 and weight not in landed:
+                local[weight].wait()
+                landed.add(weight)
+            if phase < phases:
+                live[(phase, chunk)] = messages(phase, chunk)
+                for copy in live[(phase, chunk)]:
+                    copy.start()
+
+
+def gather_all(shards_of):
+    chunks = [
+        (i, start, 256) for i in range(WEIGHTS) for start in range(0, shards_of[i].shape[1], 256)
+    ]
+    return pl.pallas_call(
+        functools.partial(gather_kernel, chunks),
+        out_shape=tuple(
+            jax.ShapeDtypeStruct((2, 2, 2, 2, 2) + item.shape, item.dtype) for item in shards_of
         ),
-        lax.psum_scatter(expand.astype(jnp.bfloat16), "dp", scatter_dimension=0, tiled=True).astype(
-            jnp.float32
+        in_specs=[ANY] * WEIGHTS,
+        out_specs=(ANY,) * WEIGHTS,
+        scratch_shapes=[
+            pltpu.SemaphoreType.DMA((WEIGHTS,)),
+            pltpu.SemaphoreType.DMA((10, GATHER_SLOTS)),
+            pltpu.SemaphoreType.DMA((10, GATHER_SLOTS)),
+        ],
+        compiler_params=pltpu.CompilerParams(collective_id=0, has_side_effects=True),
+    )(*shards_of)
+
+
+class Scatter:
+    def __init__(self, chunks, rows_of, terms, outs, sems, buffers):
+        self.chunks = chunks
+        self.rows_of = rows_of
+        self.terms = terms
+        self.outs = outs
+        self.load_sem, self.store_sem, self.send_sem, self.recv_sem = sems
+        self.buffers = buffers
+        self.places, self.targets = neighbours()
+
+    def load(self, chunk):
+        weight, start, width = self.chunks[chunk]
+        return pltpu.make_async_copy(
+            self.terms[weight].at[..., pl.ds(start, width)],
+            self.buffers[self.rows_of[weight]][0].at[chunk % TERM_SLOTS],
+            self.load_sem.at[chunk % TERM_SLOTS],
+        )
+
+    def store(self, chunk):
+        weight, start, width = self.chunks[chunk]
+        return pltpu.make_async_copy(
+            self.result(chunk),
+            self.outs[weight].at[:, pl.ds(start, width)],
+            self.store_sem.at[chunk % 2],
+        )
+
+    def result(self, chunk):
+        return self.buffers[self.rows_of[self.chunks[chunk][0]]][6].at[chunk % 2]
+
+    def parts(self, chunk):
+        weight, start, width = self.chunks[chunk]
+        if self.rows_of[weight] == TALL:
+            halves = [(0, width // 2, 0), (width // 2, width // 2, 1)]
+        else:
+            halves = [(0, width, chunk % 2)]
+        out = []
+        for begin, extent, turn in halves:
+            plane = ("y", "x") if turn == 0 else ("x", "y")
+            order = ("z1", "z2") + plane if late_z(chunk) else plane + ("z1", "z2")
+            out.append((begin, extent, ("c",) + order))
+        return out
+
+    def arrived(self, chunk, phase):
+        rows = self.rows_of[self.chunks[chunk][0]]
+        return self.buffers[rows][1 + phase].at[chunk % SCATTER_SLOTS]
+
+    def dims_after(self, order, phase):
+        used = set(AXIS_OF[target] for target in order[: phase + 1])
+        return [name for name in AXIS_NAMES if name not in used]
+
+    def source(self, chunk, phase, order):
+        rows = self.rows_of[self.chunks[chunk][0]]
+        if phase == 0:
+            return self.buffers[rows][0].at[chunk % TERM_SLOTS], list(AXIS_NAMES)
+        return self.arrived(chunk, phase - 1), self.dims_after(order, phase - 1)
+
+    def messages(self, phase, chunk):
+        parts = self.parts(chunk)
+        if len(set(order[: phase + 1] for _, _, order in parts)) == 1:
+            parts = [(0, self.chunks[chunk][2], parts[0][2])]
+        out = []
+        for part, (begin, extent, order) in enumerate(parts):
+            source, dims = self.source(chunk, phase, order)
+            target = order[phase]
+            cut = AXIS_OF[target]
+            lanes = pl.ds(begin, extent)
+            away = tuple(1 - self.places[d] if d == cut else slice(None) for d in dims)
+            whole = tuple(slice(None) for _ in self.dims_after(order, phase))
+            slot = chunk % SCATTER_SLOTS
+            out.append(
+                pltpu.make_async_remote_copy(
+                    src_ref=source.at[away + (slice(None), lanes)],
+                    dst_ref=self.arrived(chunk, phase).at[whole + (slice(None), lanes)],
+                    send_sem=self.send_sem.at[2 * phase + part, slot],
+                    recv_sem=self.recv_sem.at[2 * phase + part, slot],
+                    device_id=self.targets[target],
+                    device_id_type=MESH,
+                )
+            )
+        return out
+
+    def add(self, phase, chunk):
+        for begin, extent, order in self.parts(chunk):
+            source, dims = self.source(chunk, phase, order)
+            cut = AXIS_OF[order[phase]]
+            kept = self.dims_after(order, phase)
+            ref = self.arrived(chunk, phase)
+            lanes = pl.ds(begin, extent)
+            result = self.result(chunk)
+
+            def body(unit, carry):
+                index = tuple((unit >> (len(kept) - 1 - b)) & 1 for b in range(len(kept)))
+                where = dict(zip(kept, index))
+                where[cut] = self.places[cut]
+                mine = source[tuple(where[d] for d in dims) + (slice(None), lanes)]
+                came = ref[index + (slice(None), lanes)]
+                if phase < 4:
+                    ref[index + (slice(None), lanes)] = came + mine
+                else:
+                    result[:, lanes] = came.astype(jnp.float32) + mine.astype(jnp.float32)
+                return carry
+
+            if kept:
+                lax.fori_loop(0, 2 ** len(kept), body, 0)
+            else:
+                body(0, 0)
+
+
+def scatter_kernel(chunks, rows_of, *refs):
+    terms = refs[:WEIGHTS]
+    outs = refs[WEIGHTS : 2 * WEIGHTS]
+    scratch = refs[2 * WEIGHTS :]
+    buffers = {TALL: scratch[4:11], rows_of[3]: scratch[11:18]}
+    work = Scatter(chunks, rows_of, terms, outs, scratch[:4], buffers)
+    barrier = greet(work.targets)
+    loads = {0: work.load(0)}
+    loads[0].start()
+    pl.semaphore_wait(barrier, len(work.targets))
+    phases = 5
+    live = {}
+    stores = {}
+    for step in range(len(chunks) + phases * SCATTER_LAG):
+        for phase in range(phases, -1, -1):
+            chunk = step - phase * SCATTER_LAG
+            if not 0 <= chunk < len(chunks):
+                continue
+            if phase == 0:
+                loads.pop(chunk).wait()
+            else:
+                for copy in live.pop((phase - 1, chunk)):
+                    copy.wait()
+                if phase == phases and chunk - 2 in stores:
+                    stores.pop(chunk - 2).wait()
+                work.add(phase - 1, chunk)
+            if phase < phases:
+                live[(phase, chunk)] = work.messages(phase, chunk)
+                for copy in live[(phase, chunk)]:
+                    copy.start()
+            else:
+                stores[chunk] = work.store(chunk)
+                stores[chunk].start()
+        if step + 1 < len(chunks):
+            loads[step + 1] = work.load(step + 1)
+            loads[step + 1].start()
+    for copy in stores.values():
+        copy.wait()
+
+
+def scatter_buffers(rows, width):
+    low = jnp.bfloat16
+    out = [pltpu.VMEM((TERM_SLOTS, 2, 2, 2, 2, 2, rows, width), low)]
+    for phase in range(5):
+        out.append(pltpu.VMEM((SCATTER_SLOTS,) + (2,) * (4 - phase) + (rows, width), low))
+    out.append(pltpu.VMEM((2, rows, width), jnp.float32))
+    return out
+
+
+def scatter_all(terms):
+    shapes = [item.shape[5:] for item in terms]
+    rows_of = [shape[0] for shape in shapes]
+    chunks = []
+    for i in range(WEIGHTS - 1, -1, -1):
+        width = TALL_WIDTH if rows_of[i] == TALL else OTHER_WIDTH
+        chunks += [(i, start, width) for start in range(0, shapes[i][1], width)]
+    return pl.pallas_call(
+        functools.partial(scatter_kernel, chunks, rows_of),
+        out_shape=tuple(jax.ShapeDtypeStruct(shape, jnp.float32) for shape in shapes),
+        in_specs=[ANY] * WEIGHTS,
+        out_specs=(ANY,) * WEIGHTS,
+        scratch_shapes=[
+            pltpu.SemaphoreType.DMA((TERM_SLOTS,)),
+            pltpu.SemaphoreType.DMA((2,)),
+            pltpu.SemaphoreType.DMA((10, SCATTER_SLOTS)),
+            pltpu.SemaphoreType.DMA((10, SCATTER_SLOTS)),
+        ]
+        + scatter_buffers(TALL, TALL_WIDTH)
+        + scatter_buffers(rows_of[3], OTHER_WIDTH),
+        compiler_params=pltpu.CompilerParams(
+            collective_id=1, has_side_effects=True, vmem_limit_bytes=60 << 20
         ),
-        lax.psum_scatter(shrink.astype(jnp.bfloat16), "dp", scatter_dimension=0, tiled=True).astype(
-            jnp.float32
-        ),
-    )
-    return (
-        lax.psum_scatter(
-            tall_parts[0].astype(jnp.bfloat16), "fsdp", scatter_dimension=1, tiled=True
-        ).astype(jnp.float32),
-        lax.psum_scatter(
-            tall_parts[1].astype(jnp.bfloat16), "fsdp", scatter_dimension=1, tiled=True
-        ).astype(jnp.float32),
-        lax.psum_scatter(
-            tall_parts[2].astype(jnp.bfloat16), "fsdp", scatter_dimension=1, tiled=True
-        ).astype(jnp.float32),
-        lax.psum_scatter(
-            tall_parts[3].astype(jnp.bfloat16), "fsdp", scatter_dimension=1, tiled=True
-        ).astype(jnp.float32),
-    )
+    )(*terms)
+
+
+def gather_weights(shards_of, direct):
+    if direct:
+        return [
+            item.reshape(2, 16 * item.shape[5], item.shape[6]) for item in gather_all(shards_of)
+        ]
+    wide = [
+        lax.all_gather(lax.all_gather(item, "fsdp", axis=1, tiled=True), "dp", axis=0, tiled=True)
+        for item in shards_of
+    ]
+    return [
+        item.reshape(item.shape[0], 2, item.shape[1] // 2).transpose(1, 0, 2) for item in wide
+    ]
+
+
+def settle_gradients(terms, direct):
+    if direct:
+        return scatter_all(
+            [
+                item.reshape(2, 2, 2, 2, 2, item.shape[1] // 16, item.shape[2])
+                for item in terms
+            ]
+        )
+    wide = [
+        item.transpose(1, 0, 2).reshape(item.shape[1], 2 * item.shape[2]) for item in terms
+    ]
+    tall = [lax.psum_scatter(item, "dp", scatter_dimension=0, tiled=True) for item in wide]
+    return [
+        lax.psum_scatter(item, "fsdp", scatter_dimension=1, tiled=True).astype(jnp.float32)
+        for item in tall
+    ]
+
+
+def halves(matrix):
+    return matrix.reshape(matrix.shape[0], 2, matrix.shape[1] // 2).transpose(1, 0, 2)
+
+
+def joined(stack):
+    return stack.transpose(1, 0, 2).reshape(stack.shape[1], 2 * stack.shape[2])
 
 
 def local_scores(queries, keys_all):
@@ -291,6 +620,7 @@
 
 
 def shards(
+    direct,
     tokens,
     lengths,
     local_project,
@@ -306,34 +636,39 @@
     positions = lax.broadcasted_iota(jnp.int32, (tokens.shape[1], 1), 0)
     validity = (positions < lengths[0]).astype(jnp.float32)
     layer_in = tokens[0].astype(jnp.float32) * validity
-    local_weights = gather_weights(local_project, local_output, local_expand, local_shrink)
+    gathered = gather_weights(
+        [
+            local_project,
+            local_output,
+            local_expand,
+            local_shrink,
+            linear_project,
+            linear_output,
+            linear_expand,
+            linear_shrink,
+        ],
+        direct,
+    )
+    whole = [joined(item) for item in gathered]
+    local_weights = whole[:4]
+    linear_weights = whole[4:]
     between, local_saved = forward_layer(layer_in, validity, local_weights, True)
-    linear_weights = gather_weights(linear_project, linear_output, linear_expand, linear_shrink)
     result, linear_saved = forward_layer(between, validity, linear_weights, False)
     result = result * validity
-    linear_again = gather_weights(linear_project, linear_output, linear_expand, linear_shrink)
     upstream = cotangent[0].astype(jnp.float32) * validity
     back_between, linear_terms = backward_layer(
-        upstream, linear_saved, linear_again, validity, False
-    )
-    linear_sums = settle_gradients(
-        linear_terms[0], linear_terms[1], linear_terms[2], linear_terms[3]
-    )
-    local_again = gather_weights(local_project, local_output, local_expand, local_shrink)
-    back_input, local_terms = backward_layer(back_between, local_saved, local_again, validity, True)
-    local_sums = settle_gradients(local_terms[0], local_terms[1], local_terms[2], local_terms[3])
+        upstream, linear_saved, linear_weights, validity, False
+    )
+    back_input, local_terms = backward_layer(
+        back_between, local_saved, local_weights, validity, True
+    )
+    sums = settle_gradients(
+        [halves(item.astype(jnp.bfloat16)) for item in local_terms + linear_terms], direct
+    )
     return (
         result.astype(jnp.bfloat16)[None],
         (back_input * validity)[None],
-        local_sums[0],
-        local_sums[1],
-        local_sums[2],
-        local_sums[3],
-        linear_sums[0],
-        linear_sums[1],
-        linear_sums[2],
-        linear_sums[3],
-    )
+    ) + tuple(sums)
 
 
 def solution(mesh):
@@ -362,4 +697,5 @@
         P("dp", "fsdp"),
         P("dp", "fsdp"),
     )
-    return jax.shard_map(shards, mesh=mesh, in_specs=in_specs, out_specs=out_specs, check_vma=False)
+    direct = dict(mesh.shape) == {"dp": 16, "fsdp": 2}
+    return jax.shard_map(functools.partial(shards, direct), mesh=mesh, in_specs=in_specs, out_specs=out_specs, check_vma=False)

time: 1600 us -> 1070 us (0.67)
  waiting for transfers between devices: 966 us -> 0 us
  Pallas kernels: 0 us -> 431 us
  local copies, waits for them, and re-layouts: 196 us -> 341 us
  blocking collectives: 64.8 us -> 0 us
  matrix products: 271 us -> 232 us
  other arithmetic: 72.6 us -> 53.5 us
    reduce_scatter x16 -> x0, waiting for transfers between devices: 656 us -> none  [the longest x2 250 us: settle_gradients(): lax.psum_scatter(expand.astype(jnp.bfloat16), 'dp', scatter_dimension=0,...]
    pallas_call x0 -> x2, Pallas kernels: none -> 431 us  [the longest x1 223 us: gather_all(): pl.pallas_call(functools.partial(gather_kernel, chunks), out_shape=tuple(...]
    all_gather x8 -> x0, waiting for transfers between devices: 309 us -> none  [the longest x2 129 us: gather_weights(): lax.all_gather(wide_parts[2], 'dp', axis=0, tiled=True)]
    reshape x0 -> x16, local copies, waits for them, and re-layouts: none -> 130 us  [the longest x8 78.2 us: gather_weights(): item.reshape(2, 16 * item.shape[5], item.shape[6])]
    all_gather x8 -> x0, blocking collectives: 64.8 us -> none  [the longest x2 21.4 us: gather_weights(): lax.all_gather(expand, 'fsdp', axis=1, tiled=True)]
  transfers between devices with their start and end apart: 24 -> 0, of which waited for: 20 -> 0; matrix products, arithmetic and copies ran while one was open for 27% -> 0% of each run, Pallas kernels for 0% -> 0%
where the time goes in v1:
time: 1070 us; the launch traced here: 1060 us
  Pallas kernels  431 us (40%)
  local copies, waits for them, and re-layouts  341 us (32%)
  matrix products  232 us (22%)
  other arithmetic  53.5 us (5%)
    pallas_call x1, Pallas kernels, gather_all(): pl.pallas_call(functools.partial(gather_kernel, chunks), out_shape=tuple(...  223 us
    pallas_call x1, Pallas kernels, scatter_all(): pl.pallas_call(functools.partial(scatter_kernel, chunks, rows_of), out_sh...  209 us
    reshape x8, local copies, waits for them, and re-layouts, gather_weights(): item.reshape(2, 16 * item.shape[5], item.shape[6])  78.2 us
    dot_general x8, matrix products, contract_cols(): lax.dot_general(first_matrix, second_matrix, (((1,), (1,)), ((), ())), pr...  64.3 us
    dot_general x8, matrix products, contract_rows(): lax.dot_general(first_matrix, second_matrix, (((0,), (0,)), ((), ())), pr...  57.6 us
    reshape x8, local copies, waits for them, and re-layouts, halves(): matrix.reshape(matrix.shape[0], 2, matrix.shape[1] // 2).transpose(1, 0, 2)  52.2 us
    reshape x14, local copies, waits for them, and re-layouts, split_heads(): return values.reshape(values.shape[0] // BLOCK, BLOCK, HEADS, HEAD)  45.5 us
    reshape x8, local copies, waits for them, and re-layouts, join_heads(): return values.reshape(values.shape[0] * BLOCK, HEADS * HEAD)  33.8 us

profile of v1, /device:TPU:0, one launch (start us, length us, event | category | flops | bytes accessed | tf_op | source)
XLA Modules:
  0.0 1059.9 jit_solution(12821484962277398620)
XLA Ops:
  4.8 222.7 %shard_map.186 = (bf16[2,2,2,2,2,64,2048]{6,5,4,3,2,1,0:T(8,128)(2,1)}, bf16[2,2,2,2,2,64,512]{6,5,4,3,2,1,0:T(8,128)(2,1)}, bf16[2,2,2,2,2,64,2816]{6,5,4,3,2,1...) custom-call(bf16[64,2048]{1,0:T(8,128)(2,1)} %refs_0_.1, ...), custom_call_target="tpu_custom_call" | custom-call | tf_op jit(solution)/shard_map/pallas_call | solution.py:205
  227.5 12.3 %copy.208 = bf16[2,1024,2048]{1,2,0:T(8,128)(2,1)} copy(bf16[2,1024,2048]{2,1,0:T(8,128)(2,1)} %bitcast.268) | data formatting | bytes 16777216 | tf_op jit(solution)/shard_map/reshape | solution.py:407
  246.5 8.4 copy.218
  254.9 8.5 copy.233
  263.4 11.9 %copy.219 = bf16[2,1024,2048]{1,2,0:T(8,128)(2,1)} copy(bf16[2,1024,2048]{2,1,0:T(8,128)(2,1)} %bitcast.267) | data formatting | bytes 16777216 | tf_op jit(solution)/shard_map/reshape | solution.py:407
  275.3 15.2 %copy.217 = bf16[2,1024,2816]{1,2,0:T(8,128)(2,1)} copy(bf16[2,1024,2816]{2,1,0:T(8,128)(2,1)} %bitcast.260) | data formatting | bytes 23068672 | tf_op jit(solution)/shard_map/reshape | solution.py:407
  290.5 15.2 %copy.232 = bf16[2,1024,2816]{1,2,0:T(8,128)(2,1)} copy(bf16[2,1024,2816]{2,1,0:T(8,128)(2,1)} %bitcast.259) | data formatting | bytes 23068672 | tf_op jit(solution)/shard_map/reshape | solution.py:407
  305.7 10.4 fusion.108
  327.1 4.6 copy.264
  345.5 7.6 copy.255
  353.1 4.8 reshape.418
  357.8 5.6 copy.213
  375.0 9.8 fusion.104
  389.4 4.5 multiply_reduce_fusion.9
  394.5 7.7 fusion.105
  407.4 5.4 fusion.36
  416.8 4.5 copy.224
  423.6 4.4 copy.244
  434.7 5.4 fusion.110
  440.1 5.1 multiply_reduce_fusion.1
  454.5 7.5 copy.236
  462.0 4.8 reshape_reshape.8
  466.7 5.6 copy.228
  472.3 4.8 reshape_reshape.7
  477.2 5.3 multiply_convert_fusion.19
  485.2 13.3 %fusion.106 = f32[512,5632]{1,0:T(8,128)} fusion(bf16[1024,5632]{0,1:T(8,128)(2,1)} %bitcast.255, f32[512,1024]{1,0:T(8,128)S(1)} %get-tuple-element.81, f32[512]{0:T(512)S(1)} %get-tuple-element.67), kind=kOutput, calls=%fused_computation.185 | convolution fusion | flops 5906628608 | bytes 25167872 | tf_op jit(solution)/shard_map/dot_general | solution.py:572
  498.6 9.5 multiply_convert_fusion.3
  508.1 6.1 fusion.52
  514.2 8.5 multiply_reduce_fusion.7
  524.4 5.9 fusion.87
  547.1 5.1 multiply_convert_fusion.16
  554.8 4.5 copy.249
  566.5 4.5 add_bitcast_fusion.1
  571.0 5.7 copy.243
  576.6 4.9 reshape.414
  581.6 6.9 convolution_convert_fusion.4
  588.5 8.4 copy.278
  596.9 9.6 convolution_convert_fusion
  606.5 5.5 copy.315
  615.3 4.7 rev.4
  624.7 4.3 slice.32
  629.0 6.0 fusion.55
  650.4 6.0 copy.248
  656.4 5.0 reshape.415
  661.4 5.2 multiply_convert_fusion.15
  666.7 9.1 multiply_reduce_fusion.5
  676.4 4.8 multiply_convert_fusion.1
  681.3 11.8 %multiply_reduce_fusion.4 = (f32[512]{0:T(512)S(1)}, f32[512,1024]{1,0:T(8,128)S(1)}) fusion(f32[512,1024]{1,0:T(8,128)} %get-tuple-element.75, bf16[1024,5632]{0,1:T(8,128)(2,1)} %bitcast.254, bf16[512,2816]{1,0:T(8,128)(2,1)} %get-tuple-element.45, bf16[512,2816]{1,0:T(8,128)(2,1)S(1)} %get-tuple-element.44), kind=kOutput, calls=%fused_computation.82 | convolution fusion | flops 5918162432 | bytes 21497856 | tf_op jit(solution)/shard_map/dot_general | solution.py:54
  696.0 5.9 fusion.86
  701.9 5.2 convolution_convert_fusion.5
  707.1 8.4 copy.274
  723.7 10.5 convolution_convert_fusion.2
  734.2 8.4 copy.317
  763.0 4.7 convert_bitcast_fusion.2
  767.7 4.4 copy.270
  775.4 4.7 multiply_reduce_fusion
  787.3 4.5 reshape.420
  794.5 4.3 reshape.421
  798.8 8.7 fusion.25
  809.5 9.3 convolution_convert_fusion.1
  818.9 5.2 copy.316
  824.1 9.3 convolution_convert_fusion.3
  833.4 8.3 copy.318
  841.7 208.6 %shard_map.187 = (f32[64,2048]{1,0:T(8,128)}, f32[64,512]{1,0:T(8,128)}, f32[64,2816]{1,0:T(8,128)}, f32[176,512]{1,0:T(8,128)}, f32[64,2048]{1,0:T(8,128)}, /*i...) custom-call(bf16[2,2,2,2,2,64,2048]{6,5,4,3,2,1,0:T(8,128)(2,1)} %bitcast.242, ...), custom_call_target="tpu_custom_call" | custom-call | tf_op jit(solution)/shard_map/pallas_call | solution.py:385
  (290 shorter events, 189.5 us)
Async XLA Ops:
  4.1 301.6 %copy-start.71 = (f32[512]{0:T(512)}, f32[512]{0:T(512)S(1)}, u32[]{:S(2)}) copy-start(f32[512]{0:T(512)S(1)} %get-tuple-element.61) | copy-start | bytes 6148
  290.5 15.2 %copy-start.34 = (bf16[1,512,1024]{2,1,0:T(8,128)(2,1)S(1)}, bf16[1,512,1024]{2,1,0:T(8,128)(2,1)}, u32[]{:S(2)}) copy-start(bf16[1,512,1024]{2,1,0:T(8,128)(2,1)} %param.11) | copy-start | bytes 3145732
  324.7 6.9 copy-start.13
  371.1 18.3 %slice-start.3 = ((s8[5767168]{0:T(1024)(128)(4,1)}), s8[4194304]{0:T(1024)(128)(4,1)S(1)}, s32[]{:S(2)}) async-start(s8[5767168]{0:T(1024)(128)(4,1)} %bitcast.245), calls=%async_computation.3 | async-start | bytes 8388608
  375.0 14.4 %slice-start.4 = ((s8[5767168]{0:T(1024)(128)(4,1)}), s8[1572864]{0:T(1024)(128)(4,1)S(1)}, s32[]{:S(2)}) async-start(s8[5767168]{0:T(1024)(128)(4,1)} %bitcast.245), calls=%async_computation.4 | async-start | bytes 3145728
  384.8 4.6 copy-start.12
  384.8 4.6 copy-start.44
  389.4 4.5 copy-start.38
  394.5 7.7 copy-start.76
  423.6 4.5 copy-start.69
  434.6 5.4 copy-start.5
  440.1 5.2 copy-start.1
  477.2 5.3 copy-start.42
  477.2 5.3 copy-start.47
  482.5 16.1 %slice-start.10 = ((s8[5767168]{0:T(1024)(128)(4,1)}), s8[4194304]{0:T(1024)(128)(4,1)S(1)}, s32[]{:S(2)}) async-start(s8[5767168]{0:T(1024)(128)(4,1)} %bitcast.279), calls=%async_computation.10 | async-start | bytes 8388608
  485.2 13.3 %slice-start.11 = ((s8[5767168]{0:T(1024)(128)(4,1)}), s8[1572864]{0:T(1024)(128)(4,1)S(1)}, s32[]{:S(2)}) async-start(s8[5767168]{0:T(1024)(128)(4,1)} %bitcast.279), calls=%async_computation.11 | async-start | bytes 3145728
  498.6 9.5 copy-start.50
  498.6 15.6 %slice-start.7 = ((s8[11534336]{0:T(1024)(128)(4,1)}), s8[3145728]{0:T(1024)(128)(4,1)S(1)}, s32[]{:S(2)}) async-start(s8[11534336]{0:T(1024)(128)(4,1)} %bitcast.256), calls=%async_computation.7 | async-start | bytes 6291456
  498.6 15.6 %slice-start.8 = ((s8[11534336]{0:T(1024)(128)(4,1)}), s8[4194304]{0:T(1024)(128)(4,1)S(1)}, s32[]{:S(2)}) async-start(s8[11534336]{0:T(1024)(128)(4,1)} %bitcast.256), calls=%async_computation.8 | async-start | bytes 8388608
  508.1 6.1 slice-start.9
  514.2 8.6 copy-start.60
  524.4 5.9 copy-start.30
  559.3 4.3 copy-start.26
  576.6 4.9 copy-start.61
  606.5 5.5 copy-start.6
  606.5 5.5 copy-start.9
  629.0 6.0 copy-start.7
  629.0 6.0 copy-start.22
  635.0 4.2 copy-start.11
  650.3 16.2 %copy-start.52 = (bf16[512,1024]{1,0:T(8,128)(2,1)}, bf16[512,1024]{1,0:T(8,128)(2,1)S(1)}, u32[]{:S(2)}) copy-start(bf16[512,1024]{1,0:T(8,128)(2,1)S(1)} %reshape.416) | copy-start | bytes 3145732
  656.4 5.0 copy-start.28
  661.4 5.2 copy-start.48
  661.4 14.9 %slice-start = ((s8[11534336]{0:T(1024)(128)(4,1)}), s8[4194304]{0:T(1024)(128)(4,1)S(1)}, s32[]{:S(2)}) async-start(s8[11534336]{0:T(1024)(128)(4,1)} %bitcast.243), calls=%async_computation | async-start | bytes 8388608
  661.4 14.9 %slice-start.5 = ((s8[5767168]{0:T(1024)(128)(4,1)}), s8[4194304]{0:T(1024)(128)(4,1)S(1)}, s32[]{:S(2)}) async-start(s8[5767168]{0:T(1024)(128)(4,1)} %bitcast.248), calls=%async_computation.5 | async-start | bytes 8388608
  666.6 9.2 copy-start.54
  666.6 9.2 copy-start.31
  666.6 9.2 copy-start.77
  666.6 9.2 copy-start.79
  666.6 9.7 slice-start.1
  666.6 9.7 slice-start.2
  666.6 9.7 slice-start.6
  676.4 4.8 copy-start.23
  681.2 11.8 %copy-start.37 = (bf16[512,2816]{1,0:T(8,128)(2,1)}, bf16[512,2816]{1,0:T(8,128)(2,1)S(1)}, u32[]{:S(2)}) copy-start(bf16[512,2816]{1,0:T(8,128)(2,1)S(1)} %get-tuple-element.44) | copy-start | bytes 8650756
  681.2 11.8 %copy-start.24 = (f32[512,1024]{1,0:T(8,128)S(1)}, f32[512,1024]{1,0:T(8,128)}, u32[]{:S(2)}) copy-start(f32[512,1024]{1,0:T(8,128)} %copy-done.23) | copy-start | bytes 6291460
  681.2 11.8 %copy-start.45 = (f32[512,1024]{1,0:T(8,128)S(1)}, f32[512,1024]{1,0:T(8,128)}, u32[]{:S(2)}) copy-start(f32[512,1024]{1,0:T(8,128)} %get-tuple-element.75) | copy-start | bytes 6291460
  681.2 11.8 %copy-start.75 = (f32[512]{0:T(512)S(1)}, f32[512]{0:T(512)}, u32[]{:S(2)}) copy-start(f32[512]{0:T(512)} %copy-done.74) | copy-start | bytes 6148
  681.3 11.8 %copy-start.78 = (f32[512]{0:T(512)S(1)}, f32[512]{0:T(512)}, u32[]{:S(2)}) copy-start(f32[512]{0:T(512)} %get-tuple-element.62) | copy-start | bytes 6148
  696.0 5.9 copy-start.32
  696.0 5.9 copy-start.39
  707.0 8.4 copy-start.63
  775.3 23.4 %copy-start.55 = (bf16[512,1024]{1,0:T(8,128)(2,1)}, bf16[512,1024]{1,0:T(8,128)(2,1)S(1)}, u32[]{:S(2)}) copy-start(bf16[512,1024]{1,0:T(8,128)(2,1)S(1)} %reshape.422) | copy-start | bytes 3145732
  775.4 4.7 copy-start.4
  794.5 4.3 copy-start.36
  794.5 4.3 copy-start.57
  798.8 8.8 copy-start.33
  798.8 8.8 copy-start.72
  798.8 8.8 copy-start.73
  818.8 5.2 copy-start.56
  818.8 5.2 copy-start.58
  818.8 5.2 copy-start.59
  1050.3 5.6 copy-start.68
  1050.3 6.4 copy-start.66
  1050.3 7.2 copy-start.70
  1052.3 5.9 copy-start.65
  (29 other events, 76.3 us)

commit v2 on v1

--- a/solution.py
+++ b/solution.py
@@ -72,17 +72,24 @@
 
 MESH = pl.DeviceIdType.MESH
 ANY = pl.BlockSpec(memory_space=pl.ANY)
+FULL = pl.BlockSpec(memory_space=pltpu.VMEM)
 WEIGHTS = 8
-AXIS_NAMES = ("f", "zh", "zl", "y", "c")
-AXIS_OF = {"c": "c", "y": "y", "x": "f", "z1": "zl", "z2": "zh"}
-GATHER_LAG = 3
+WIDTH = 256
+LAG = 3
+PHASES = 5
+HEAD_GROUPS = 4
+PROJECT_CHUNKS = 8
+OUTPUT_CHUNKS = 2
+EXPAND_CHUNKS = 11
+LAYER_CHUNKS = PROJECT_CHUNKS + OUTPUT_CHUNKS + EXPAND_CHUNKS
+CHUNKS = 2 * LAYER_CHUNKS
+SHRINK_PARTS = 4
+SHRINK_WIDTH = 128
 GATHER_SLOTS = 8
-SCATTER_LAG = 3
-SCATTER_SLOTS = 3 * SCATTER_LAG + 1
-TERM_SLOTS = SCATTER_LAG + 1
-TALL = 64
-TALL_WIDTH = 256
-OTHER_WIDTH = 128
+LOAD_SLOTS = 3
+LOW = jnp.bfloat16
+WIDE = jnp.float32
+ROWS = 512
 
 
 def neighbours():
@@ -106,116 +113,467 @@
     barrier = pltpu.get_barrier_semaphore()
     for target in targets.values():
         pl.semaphore_signal(barrier, inc=1, device_id=target, device_id_type=MESH)
-    return barrier
+    pl.semaphore_wait(barrier, len(targets))
+
+
+def dot(left, right):
+    return jnp.dot(left, right, preferred_element_type=WIDE)
+
+
+def softplus(values):
+    return jnp.maximum(values, 0.0) + jnp.log1p(jnp.exp(-jnp.abs(values)))
+
+
+def logistic(values):
+    return 1.0 / (1.0 + jnp.exp(-values))
+
+
+def first_lanes(rows):
+    return lax.broadcasted_iota(jnp.int32, (rows, 128), 1) < HEAD
+
+
+def pair_mean(values, first):
+    left = jnp.sum(jnp.where(first, values, 0.0), axis=-1, keepdims=True)
+    right = jnp.sum(jnp.where(first, 0.0, values), axis=-1, keepdims=True)
+    return jnp.where(first, left, right) * (1.0 / HEAD)
+
+
+def block_mask(rows):
+    i = lax.broadcasted_iota(jnp.int32, (rows, rows), 0)
+    j = lax.broadcasted_iota(jnp.int32, (rows, rows), 1)
+    return (i // BLOCK == j // BLOCK) & (j <= i)
+
+
+def norm_into(source, target):
+    def body(t, carry):
+        rows = pl.ds(pl.multiple_of(t * 128, 128), 128)
+        target[rows, :] = simple_norm(source[rows, :]).astype(LOW)
+        return carry
+
+    lax.fori_loop(0, ROWS // 128, body, 0)
+
+
+def local_mixer(group, parts, validity, gated, stage):
+    def body(turn, carry):
+        t = turn // 2
+        rows = pl.ds(pl.multiple_of(t * 128, 128), 128)
+        pair = turn % 2
+        lanes = pl.ds(pl.multiple_of(pair * 128, 128), 128)
+        first = first_lanes(128)
+        q = parts[0, 0, rows, lanes].astype(LOW)
+        k = parts[1, 0, rows, lanes].astype(LOW)
+        v = parts[0, 1, rows, lanes].astype(LOW)
+        u = parts[1, 1, rows, lanes]
+        keep = block_mask(128)
+        mixed = []
+        for head in range(2):
+            mine = jnp.where(first == (head == 0), q, jnp.zeros_like(q))
+            scores = contract_cols(mine, k) * HEAD ** (-0.5)
+            scores = jnp.where(keep, scores, -1e30)
+            highest_score = jnp.max(scores, axis=-1, keepdims=True)
+            weights = jnp.exp(scores - highest_score)
+            attend = weights / jnp.sum(weights, axis=-1, keepdims=True)
+            mixed.append(dot(attend.astype(LOW), v))
+        mixture = jnp.where(first, mixed[0], mixed[1]) * validity[rows, :]
+        scale = lax.rsqrt(pair_mean(mixture * mixture, first) + epsilon)
+        columns = pl.ds(pl.multiple_of(group * WIDTH + pair * 128, 128), 128)
+        gated[rows, columns] = (mixture * scale * (u * logistic(u))).astype(LOW)
+        stage[4, rows, lanes] = mixture.astype(LOW)
+        return carry
+
+    lax.fori_loop(0, 2 * ROWS // 128, body, 0)
+
+
+def linear_mixer(group, parts, gated, stage):
+    half = ROWS // 2
+
+    def body(pair, carry):
+        lanes = pl.ds(pl.multiple_of(pair * 128, 128), 128)
+        columns = pl.ds(pl.multiple_of(group * WIDTH + pair * 128, 128), 128)
+        first = first_lanes(half)
+        fk = softplus(parts[1, 0, :, lanes]).astype(LOW)
+        v = parts[0, 1, :, lanes].astype(LOW)
+        for t in range(2):
+            rows = pl.ds(t * half, half)
+            reach = (t + 1) * half
+            fq = softplus(parts[0, 0, rows, lanes]).astype(LOW)
+            i = lax.broadcasted_iota(jnp.int32, (half, reach), 0) + t * half
+            j = lax.broadcasted_iota(jnp.int32, (half, reach), 1)
+            mixed = []
+            for head in range(2):
+                mine = jnp.where(first == (head == 0), fq, jnp.zeros_like(fq))
+                scores = jnp.where(j <= i, contract_cols(mine, fk[:reach]), 0.0).astype(LOW)
+                mixed.append(dot(scores, v[:reach]))
+            mixture = jnp.where(first, mixed[0], mixed[1])
+            scale = lax.rsqrt(pair_mean(mixture * mixture, first) + epsilon)
+            u = parts[1, 1, rows, lanes]
+            gated[rows, columns] = (mixture * scale * (u * logistic(u))).astype(LOW)
+            stage[4, rows, lanes] = mixture.astype(LOW)
+        return carry
+
+    lax.fori_loop(0, 2, body, 0)
+
+
+def chunk_columns(weight, part):
+    if weight == 0:
+        return (part % 2) * 1024 + (part // 2) * WIDTH
+    return part * WIDTH
+
+
+class Gather:
+    def __init__(self, own, held, tall, sems):
+        self.own, self.held, self.tall = own, held, tall
+        self.local_sem, self.send_sem, self.recv_sem, self.tall_send, self.tall_recv = sems
+        self.places, self.targets = neighbours()
+        self.at = tuple(self.places[name] for name in ("f", "zh", "zl", "y", "c"))
+
+    def begin(self):
+        counts = (PROJECT_CHUNKS, OUTPUT_CHUNKS, EXPAND_CHUNKS)
+        for layer in range(2):
+            chunk = LAYER_CHUNKS * layer
+            for weight in range(3):
+                for part in range(counts[weight]):
+                    start = chunk_columns(weight, part)
+                    pltpu.make_async_copy(
+                        self.own[4 * layer + weight].at[:, pl.ds(start, WIDTH)],
+                        self.held.at[(chunk,) + self.at],
+                        self.local_sem.at[chunk],
+                    ).start()
+                    chunk += 1
+            pltpu.make_async_copy(
+                self.own[4 * layer + 3],
+                self.tall.at[(layer,) + self.at],
+                self.local_sem.at[CHUNKS + layer],
+            ).start()
+        greet(self.targets)
+
+    def message(self, block, target, sems, place):
+        return pltpu.make_async_remote_copy(
+            src_ref=block,
+            dst_ref=block,
+            send_sem=sems[0].at[place],
+            recv_sem=sems[1].at[place],
+            device_id=self.targets[target],
+            device_id_type=MESH,
+        )
+
+    def wide_messages(self, phase, chunk):
+        x, zh, zl, y, c = self.at
+        ref = self.held
+        sems = (self.send_sem, self.recv_sem)
+        slot = chunk % GATHER_SLOTS
+        half = WIDTH // 2
+        low, high = pl.ds(0, half), pl.ds(half, half)
+
+        def one(index, target, part):
+            return self.message(ref.at[(chunk,) + index], target, sems, (2 * phase + part, slot))
+
+        a = slice(None)
+        if phase == 0:
+            return [one((x, zh, zl, y, c), "z2", 0)]
+        if phase == 1:
+            return [one((x, a, zl, y, c), "z1", 0)]
+        if phase == 2:
+            return [one((x, a, a, y, c, a, low), "x", 0), one((x, a, a, y, c, a, high), "y", 1)]
+        if phase == 3:
+            return [one((a, a, a, y, c, a, low), "y", 0), one((x, a, a, a, c, a, high), "x", 1)]
+        return [one((a, a, a, a, c), "c", 0)]
+
+    def tall_message(self, phase, layer, part, odd):
+        x, zh, zl, y, c = self.at
+        a = slice(None)
+        lanes = pl.ds(pl.multiple_of(part * SHRINK_WIDTH, SHRINK_WIDTH), SHRINK_WIDTH)
+        index, target = {
+            (0, 0): ((x, zh, zl, y, c), "x"),
+            (0, 1): ((x, zh, zl, y, c), "y"),
+            (1, 0): ((a, zh, zl, y, c), "y"),
+            (1, 1): ((x, zh, zl, a, c), "x"),
+            (2, 0): ((a, zh, zl, a, c), "z2"),
+            (3, 0): ((a, a, zl, a, c), "z1"),
+            (4, 0): ((a, a, a, a, c), "c"),
+        }[(phase, odd)]
+        return self.message(
+            self.tall.at[(layer,) + index + (a, lanes)],
+            target,
+            (self.tall_send, self.tall_recv),
+            (phase, layer * SHRINK_PARTS + part),
+        )
+
+    def tall_turn(self, chunk):
+        layer = chunk // LAYER_CHUNKS
+        place = chunk % LAYER_CHUNKS
+        return layer, place // 5, place % 5 == 4
+
+    def for_tall(self, phase, chunk, act):
+        layer, part, due = self.tall_turn(chunk)
+        if phase >= 2:
+            pl.when(due)(lambda: act(self.tall_message(phase, layer, part, 0)))
+        else:
+            for odd in range(2):
+                pl.when(due & (part % 2 == odd))(
+                    lambda odd=odd: act(self.tall_message(phase, layer, part, odd))
+                )
+
+    def step(self, step):
+        for phase in range(PHASES, -1, -1):
+            chunk = step - phase * LAG
+
+            @pl.when((chunk >= 0) & (chunk < CHUNKS))
+            def _(phase=phase, chunk=chunk):
+                if phase >= 1:
+                    for copy in self.wide_messages(phase - 1, chunk):
+                        copy.wait()
+                    self.for_tall(phase - 1, chunk, lambda copy: copy.wait())
+                else:
+                    pltpu.make_async_copy(
+                        self.own[0].at[:, pl.ds(0, WIDTH)],
+                        self.held.at[(chunk,) + self.at],
+                        self.local_sem.at[chunk],
+                    ).wait()
+                    layer = chunk // LAYER_CHUNKS
+
+                    @pl.when(chunk % LAYER_CHUNKS == 4)
+                    def _():
+                        pltpu.make_async_copy(
+                            self.own[3],
+                            self.tall.at[(layer,) + self.at],
+                            self.local_sem.at[CHUNKS + layer],
+                        ).wait()
+
+                if phase < PHASES:
+                    for copy in self.wide_messages(phase, chunk):
+                        copy.start()
+                    self.for_tall(phase, chunk, lambda copy: copy.start())
+
+
+def forward_kernel(*refs):
+    own = refs[:WEIGHTS]
+    tokens, validity = refs[WEIGHTS : WEIGHTS + 2]
+    held, tall, mixed_out, between, middles, gates, stages, halves_out = refs[10:18]
+    scratch = refs[18:]
+    sems, (load_sem, tall_sem, stage_sem, half_sem, misc_sem) = scratch[:5], scratch[5:10]
+    loaded, shrink, x, middle, normed, gated, hidden, parts, stage, half_stage, final = scratch[10:]
+    gather = Gather(own, held, tall, sems)
+    gather.begin()
+
+    def rows_of(t):
+        return pl.ds(pl.multiple_of(t * 128, 128), 128)
+
+    def start_rows(t, carry):
+        rows = rows_of(t)
+        x[rows, :] = tokens[rows, :].astype(WIDE) * validity[rows, :]
+        return carry
+
+    lax.fori_loop(0, ROWS // 128, start_rows, 0)
+    norm_into(x, normed)
+
+    def load(chunk):
+        return pltpu.make_async_copy(
+            held.at[chunk], loaded.at[chunk % LOAD_SLOTS], load_sem.at[chunk % LOAD_SLOTS]
+        )
+
+    def load_tall(layer):
+        return pltpu.make_async_copy(tall.at[layer], shrink, tall_sem)
+
+    def keep_stage(layer, group):
+        return pltpu.make_async_copy(stage, stages.at[layer, group], stage_sem)
+
+    def keep_half(layer, part):
+        return pltpu.make_async_copy(
+            half_stage.at[part % 2], halves_out.at[layer, part], half_sem.at[part % 2]
+        )
+
+    def keep(kind, layer):
+        source, target = ((gated, gates), (middle, middles))[kind]
+        return pltpu.make_async_copy(source, target.at[layer], misc_sem.at[kind])
+
+    def keep_between():
+        return pltpu.make_async_copy(x, between, misc_sem.at[2])
+
+    def weight(slot, f):
+        return loaded[slot, f].reshape(1024, WIDTH)
+
+    def project_step(layer, place, slot):
+        group = place // 2
+        for f in range(2):
+            parts[place % 2, f] = dot(normed[...], weight(slot, f))
+
+        @pl.when(place % 2 == 1)
+        def _():
+            @pl.when((layer > 0) | (group > 0))
+            def _():
+                keep_stage(layer, group).wait()
+
+            @pl.when((layer > 0) & (group == 0))
+            def _():
+                keep(0, 0).wait()
+
+            for kind in range(4):
+                stage[kind] = parts[kind % 2, kind // 2].astype(LOW)
+            pl.when(layer == 0)(lambda: local_mixer(group, parts, validity, gated, stage))
+            pl.when(layer > 0)(lambda: linear_mixer(group, parts, gated, stage))
+            keep_stage(layer, group).start()
+
+    def output_step(layer, part, slot):
+        @pl.when(part == 0)
+        def _():
+            keep(0, layer).start()
+
+            @pl.when(layer > 0)
+            def _():
+                keep(1, 0).wait()
+
+        for f in range(2):
+            lanes = pl.ds(pl.multiple_of(f * 512 + part * WIDTH, WIDTH), WIDTH)
+            middle[:, lanes] = x[:, lanes] + dot(gated[...], weight(slot, f))
+
+        @pl.when(part == OUTPUT_CHUNKS - 1)
+        def _():
+            keep(1, layer).start()
+            norm_into(middle, normed)
+
+    def expand_step(layer, part, slot):
+        @pl.when((layer > 0) | (part > 1))
+        def _():
+            keep_half(layer, part).wait()
+
+        first = dot(normed[...], weight(slot, 0))
+        second = dot(normed[...], weight(slot, 1))
+        half_stage[part % 2, 0] = first.astype(LOW)
+        half_stage[part % 2, 1] = second.astype(LOW)
+        hidden[:, pl.ds(pl.multiple_of(part * WIDTH, WIDTH), WIDTH)] = (first * second).astype(LOW)
+        keep_half(layer, part).start()
+
+    def shrink_step(layer):
+        load_tall(layer).wait()
+
+        @pl.when(layer > 0)
+        def _():
+            keep_between().wait()
+
+        def body(turn, carry):
+            f = turn // 2
+            columns = pl.ds(pl.multiple_of((turn % 2) * WIDTH, WIDTH), WIDTH)
+            lanes = pl.ds(pl.multiple_of(turn * WIDTH, WIDTH), WIDTH)
+            matrix = shrink[f, :, :, :, :, :, columns].reshape(hidden.shape[1], WIDTH)
+            x[:, lanes] = middle[:, lanes] + dot(hidden[...], matrix)
+            return carry
+
+        lax.fori_loop(0, 4, body, 0)
+
+        @pl.when(layer == 0)
+        def _():
+            keep_between().start()
+            norm_into(x, normed)
+
+        @pl.when(layer > 0)
+        def _():
+            def last_rows(t, carry):
+                rows = rows_of(t)
+                final[rows, :] = (x[rows, :] * validity[rows, :]).astype(LOW)
+                return carry
+
+            lax.fori_loop(0, ROWS // 128, last_rows, 0)
+
+    def body(step, carry):
+        gather.step(step)
+        arrived = step - PHASES * LAG
+
+        @pl.when((arrived >= 0) & (arrived < CHUNKS))
+        def _():
+            load(arrived).start()
+
+            @pl.when(arrived % LAYER_CHUNKS == LAYER_CHUNKS - 2)
+            def _():
+                load_tall(arrived // LAYER_CHUNKS).start()
+
+        ready = arrived - 1
+
+        @pl.when((ready >= 0) & (ready < CHUNKS))
+        def _():
+            load(ready).wait()
+            layer = ready // LAYER_CHUNKS
+            place = ready % LAYER_CHUNKS
+            slot = ready % LOAD_SLOTS
+            pl.when(place < PROJECT_CHUNKS)(lambda: project_step(layer, place, slot))
+            pl.when((place >= PROJECT_CHUNKS) & (place < PROJECT_CHUNKS + OUTPUT_CHUNKS))(
+                lambda: output_step(layer, place - PROJECT_CHUNKS, slot)
+            )
+            pl.when(place >= PROJECT_CHUNKS + OUTPUT_CHUNKS)(
+                lambda: expand_step(layer, place - PROJECT_CHUNKS - OUTPUT_CHUNKS, slot)
+            )
+            pl.when(place == LAYER_CHUNKS - 1)(lambda: shrink_step(layer))
+
+        return carry
+
+    lax.fori_loop(0, CHUNKS + PHASES * LAG + 1, body, 0)
+    last = pltpu.make_async_copy(final, mixed_out, misc_sem.at[3])
+    last.start()
+    keep_stage(1, HEAD_GROUPS - 1).wait()
+    keep(0, 1).wait()
+    keep(1, 1).wait()
+    keep_half(1, EXPAND_CHUNKS - 2).wait()
+    keep_half(1, EXPAND_CHUNKS - 1).wait()
+    last.wait()
+
+
+def run_forward(shards_of, tokens, validity):
+    bits = (2, 2, 2, 2, 2)
+    struct = jax.ShapeDtypeStruct
+    return pl.pallas_call(
+        forward_kernel,
+        out_shape=(
+            struct((CHUNKS,) + bits + (64, WIDTH), LOW),
+            struct((2,) + bits + (176, 512), LOW),
+            struct((ROWS, 1024), LOW),
+            struct((ROWS, 1024), WIDE),
+            struct((2, ROWS, 1024), WIDE),
+            struct((2, ROWS, 1024), LOW),
+            struct((2, HEAD_GROUPS, 5, ROWS, WIDTH), LOW),
+            struct((2, EXPAND_CHUNKS, 2, ROWS, WIDTH), LOW),
+        ),
+        in_specs=[ANY] * WEIGHTS + [FULL, FULL],
+        out_specs=(ANY,) * 8,
+        scratch_shapes=[
+            pltpu.SemaphoreType.DMA((CHUNKS + 2,)),
+            pltpu.SemaphoreType.DMA((10, GATHER_SLOTS)),
+            pltpu.SemaphoreType.DMA((10, GATHER_SLOTS)),
+            pltpu.SemaphoreType.DMA((PHASES, 2 * SHRINK_PARTS)),
+            pltpu.SemaphoreType.DMA((PHASES, 2 * SHRINK_PARTS)),
+            pltpu.SemaphoreType.DMA((LOAD_SLOTS,)),
+            pltpu.SemaphoreType.DMA,
+            pltpu.SemaphoreType.DMA,
+            pltpu.SemaphoreType.DMA((2,)),
+            pltpu.SemaphoreType.DMA((4,)),
+            pltpu.VMEM((LOAD_SLOTS,) + bits + (64, WIDTH), LOW),
+            pltpu.VMEM(bits + (176, 512), LOW),
+            pltpu.VMEM((ROWS, 1024), WIDE),
+            pltpu.VMEM((ROWS, 1024), WIDE),
+            pltpu.VMEM((ROWS, 1024), LOW),
+            pltpu.VMEM((ROWS, 1024), LOW),
+            pltpu.VMEM((ROWS, 2816), LOW),
+            pltpu.VMEM((2, 2, ROWS, WIDTH), WIDE),
+            pltpu.VMEM((5, ROWS, WIDTH), LOW),
+            pltpu.VMEM((2, 2, ROWS, WIDTH), LOW),
+            pltpu.VMEM((ROWS, 1024), LOW),
+        ],
+        compiler_params=pltpu.CompilerParams(
+            collective_id=0, has_side_effects=True, vmem_limit_bytes=60 << 20
+        ),
+    )(*shards_of, tokens, validity)
+
+AXIS_NAMES = ("f", "zh", "zl", "y", "c")
+AXIS_OF = {"c": "c", "y": "y", "x": "f", "z1": "zl", "z2": "zh"}
+SCATTER_LAG = 3
+SCATTER_SLOTS = 3 * SCATTER_LAG + 1
+TERM_SLOTS = SCATTER_LAG + 1
+TALL = 64
+TALL_WIDTH = 256
+OTHER_WIDTH = 128
 
 
 def late_z(chunk):
     return chunk % 5 == 3
-
-
-def gather_kernel(chunks, *refs):
-    own = refs[:WEIGHTS]
-    held = refs[WEIGHTS : 2 * WEIGHTS]
-    local_sem, send_sem, recv_sem = refs[2 * WEIGHTS :]
-    places, targets = neighbours()
-    x, zh, zl, y, c = (places[name] for name in AXIS_NAMES)
-    barrier = greet(targets)
-    local = [
-        pltpu.make_async_copy(own[i], held[i].at[x, zh, zl, y, c], local_sem.at[i])
-        for i in range(WEIGHTS)
-    ]
-    for copy in local:
-        copy.start()
-    pl.semaphore_wait(barrier, len(targets))
-
-    def messages(phase, chunk):
-        weight, start, width = chunks[chunk]
-        ref = held[weight]
-        half = width // 2
-        every = pl.ds(start, width)
-        first = pl.ds(start, half)
-        second = pl.ds(start + half, half)
-
-        def message(block, target, part):
-            slot = chunk % GATHER_SLOTS
-            return pltpu.make_async_remote_copy(
-                src_ref=block,
-                dst_ref=block,
-                send_sem=send_sem.at[2 * phase + part, slot],
-                recv_sem=recv_sem.at[2 * phase + part, slot],
-                device_id=targets[target],
-                device_id_type=MESH,
-            )
-
-        if phase == 4:
-            return [message(ref.at[:, :, :, :, c, :, every], "c", 0)]
-        if late_z(chunk):
-            if phase == 0:
-                return [
-                    message(ref.at[x, zh, zl, y, c, :, first], "x", 0),
-                    message(ref.at[x, zh, zl, y, c, :, second], "y", 1),
-                ]
-            if phase == 1:
-                return [
-                    message(ref.at[:, zh, zl, y, c, :, first], "y", 0),
-                    message(ref.at[x, zh, zl, :, c, :, second], "x", 1),
-                ]
-            if phase == 2:
-                return [message(ref.at[:, zh, zl, :, c, :, every], "z2", 0)]
-            return [message(ref.at[:, :, zl, :, c, :, every], "z1", 0)]
-        if phase == 0:
-            return [message(ref.at[x, zh, zl, y, c, :, every], "z2", 0)]
-        if phase == 1:
-            return [message(ref.at[x, :, zl, y, c, :, every], "z1", 0)]
-        if phase == 2:
-            return [
-                message(ref.at[x, :, :, y, c, :, first], "x", 0),
-                message(ref.at[x, :, :, y, c, :, second], "y", 1),
-            ]
-        return [
-            message(ref.at[:, :, :, y, c, :, first], "y", 0),
-            message(ref.at[x, :, :, :, c, :, second], "x", 1),
-        ]
-
-    phases = 5
-    landed = set()
-    live = {}
-    for step in range(len(chunks) + phases * GATHER_LAG):
-        for phase in range(phases, -1, -1):
-            chunk = step - phase * GATHER_LAG
-            if not 0 <= chunk < len(chunks):
-                continue
-            if phase >= 1:
-                for copy in live.pop((phase - 1, chunk)):
-                    copy.wait()
-            weight = chunks[chunk][0]
-            if phase == 0 and weight not in landed:
-                local[weight].wait()
-                landed.add(weight)
-            if phase < phases:
-                live[(phase, chunk)] = messages(phase, chunk)
-                for copy in live[(phase, chunk)]:
-                    copy.start()
-
-
-def gather_all(shards_of):
-    chunks = [
-        (i, start, 256) for i in range(WEIGHTS) for start in range(0, shards_of[i].shape[1], 256)
-    ]
-    return pl.pallas_call(
-        functools.partial(gather_kernel, chunks),
-        out_shape=tuple(
-            jax.ShapeDtypeStruct((2, 2, 2, 2, 2) + item.shape, item.dtype) for item in shards_of
-        ),
-        in_specs=[ANY] * WEIGHTS,
-        out_specs=(ANY,) * WEIGHTS,
-        scratch_shapes=[
-            pltpu.SemaphoreType.DMA((WEIGHTS,)),
-            pltpu.SemaphoreType.DMA((10, GATHER_SLOTS)),
-            pltpu.SemaphoreType.DMA((10, GATHER_SLOTS)),
-        ],
-        compiler_params=pltpu.CompilerParams(collective_id=0, has_side_effects=True),
-    )(*shards_of)
 
 
 class Scatter:
@@ -332,10 +690,9 @@
     scratch = refs[2 * WEIGHTS :]
     buffers = {TALL: scratch[4:11], rows_of[3]: scratch[11:18]}
     work = Scatter(chunks, rows_of, terms, outs, scratch[:4], buffers)
-    barrier = greet(work.targets)
+    greet(work.targets)
     loads = {0: work.load(0)}
     loads[0].start()
-    pl.semaphore_wait(barrier, len(work.targets))
     phases = 5
     live = {}
     stores = {}
@@ -401,11 +758,7 @@
     )(*terms)
 
 
-def gather_weights(shards_of, direct):
-    if direct:
-        return [
-            item.reshape(2, 16 * item.shape[5], item.shape[6]) for item in gather_all(shards_of)
-        ]
+def gather_weights(shards_of):
     wide = [
         lax.all_gather(lax.all_gather(item, "fsdp", axis=1, tiled=True), "dp", axis=0, tiled=True)
         for item in shards_of
@@ -636,25 +989,64 @@
     positions = lax.broadcasted_iota(jnp.int32, (tokens.shape[1], 1), 0)
     validity = (positions < lengths[0]).astype(jnp.float32)
     layer_in = tokens[0].astype(jnp.float32) * validity
-    gathered = gather_weights(
-        [
-            local_project,
-            local_output,
-            local_expand,
-            local_shrink,
-            linear_project,
-            linear_output,
-            linear_expand,
-            linear_shrink,
-        ],
-        direct,
-    )
-    whole = [joined(item) for item in gathered]
-    local_weights = whole[:4]
-    linear_weights = whole[4:]
-    between, local_saved = forward_layer(layer_in, validity, local_weights, True)
-    result, linear_saved = forward_layer(between, validity, linear_weights, False)
-    result = result * validity
+    shards_of = [
+        local_project,
+        local_output,
+        local_expand,
+        local_shrink,
+        linear_project,
+        linear_output,
+        linear_expand,
+        linear_shrink,
+    ]
+    if direct:
+        held, tall, result, between, middles, gates, stages, kept = run_forward(
+            shards_of, tokens[0], validity
+        )
+        whole = []
+        saved = []
+        for layer in range(2):
+            mats = held.reshape(2, LAYER_CHUNKS, 2, 1024, WIDTH)[layer]
+            project = mats[:8].reshape(4, 2, 2, 1024, WIDTH).transpose(3, 2, 1, 0, 4)
+            output = mats[8:10].transpose(2, 1, 0, 3)
+            expand = mats[10:].transpose(2, 1, 0, 3)
+            whole += [
+                project.reshape(1024, 4096),
+                output.reshape(1024, 1024),
+                expand.reshape(1024, 5632),
+                joined(tall[layer].reshape(2, 2816, 512)),
+            ]
+            source = (layer_in, between)[layer]
+            five = stages[layer].transpose(1, 2, 0, 3).reshape(5, ROWS, 1024).astype(jnp.float32)
+            projected = jnp.concatenate([five[0], five[1], five[2], five[3]], axis=1)
+            projected = jnp.concatenate([five[0], five[1], five[2], five[3]], axis=1)
+            queries, keys_all = five[0], five[1]
+            logsum = None
+            if layer == 0:
+                scores = local_scores(queries, keys_all)[2]
+                logsum = jax.nn.logsumexp(scores, axis=-1, keepdims=True)
+            saved.append(
+                (
+                    source,
+                    simple_norm(source).astype(jnp.bfloat16),
+                    projected,
+                    five[2].astype(jnp.bfloat16),
+                    five[4],
+                    logsum,
+                    gates[layer],
+                    middles[layer],
+                    simple_norm(middles[layer]).astype(jnp.bfloat16),
+                )
+            )
+        local_weights, linear_weights = whole[:4], whole[4:]
+        local_saved, linear_saved = saved
+    else:
+        whole = [joined(item) for item in gather_weights(shards_of)]
+        local_weights = whole[:4]
+        linear_weights = whole[4:]
+        between, local_saved = forward_layer(layer_in, validity, local_weights, True)
+        result, linear_saved = forward_layer(between, validity, linear_weights, False)
+        result = (result * validity).astype(jnp.bfloat16)
     upstream = cotangent[0].astype(jnp.float32) * validity
     back_between, linear_terms = backward_layer(
         upstream, linear_saved, linear_weights, validity, False
@@ -666,7 +1058,7 @@
         [halves(item.astype(jnp.bfloat16)) for item in local_terms + linear_terms], direct
     )
     return (
-        result.astype(jnp.bfloat16)[None],
+        result[None],
         (back_input * validity)[None],
     ) + tuple(sums)
 

time: 1070 us -> 1100 us (1.028)
  matrix products: 232 us -> 201 us
  other arithmetic: 53.5 us -> 77.3 us
  Pallas kernels: 431 us -> 452 us
  local copies, waits for them, and re-layouts: 341 us -> 357 us
    slice x0 -> x21, local copies, waits for them, and re-layouts: none -> 105 us  [the longest x3 47.6 us: shards(): expand = mats[10:].transpose(2, 1, 0, 3)]
    reshape x8 -> x2, local copies, waits for them, and re-layouts: 78.2 us -> 23.1 us  [shards(): project = mats[:8].reshape(4, 2, 2, 1024, WIDTH).transpose(3, 2, 1, 0, 4)]
    dot_general x12 -> x2, matrix products: 69.3 us -> 21.7 us  [backward_layer(): expanded = jnp.dot(second, expand, preferred_element_type=jnp.float32)]
    reshape x14 -> x4, local copies, waits for them, and re-layouts: 45.5 us -> 12.4 us  [split_heads(): return values.reshape(values.shape[0] // BLOCK, BLOCK, HEADS, HEAD)]
    unnamed x194 -> x149, local copies, waits for them, and re-layouts: 29.8 us -> 10.8 us
    convert_element_type x1 -> x7, local copies, waits for them, and re-layouts: 0.7 us -> 18.7 us  [the longest x3 6.21 us: shards(): five[2].astype(jnp.bfloat16)]
    pallas_call x1, Pallas kernels: 223 us -> 241 us  [run_forward(): pl.pallas_call(forward_kernel, out_shape=(struct((CHUNKS,) + bits + (64,...]
    squeeze x0 -> x4, local copies, waits for them, and re-layouts: none -> 15.3 us  [shards(): projected = jnp.concatenate([five[0], five[1], five[2], five[3]], axis=1)]
where the time goes in v2:
time: 1100 us; the launch traced here: 1090 us
  Pallas kernels  452 us (41%)
  local copies, waits for them, and re-layouts  357 us (32%)
  matrix products  201 us (18%)
  other arithmetic  77.3 us (7%)
    pallas_call x1, Pallas kernels, run_forward(): pl.pallas_call(forward_kernel, out_shape=(struct((CHUNKS,) + bits + (64,...  241 us
    pallas_call x1, Pallas kernels, scatter_all(): pl.pallas_call(functools.partial(scatter_kernel, chunks, rows_of), out_sh...  212 us
    dot_general x8, matrix products, contract_rows(): lax.dot_general(first_matrix, second_matrix, (((0,), (0,)), ((), ())), pr...  63.1 us
    dot_general x8, matrix products, contract_cols(): lax.dot_general(first_matrix, second_matrix, (((1,), (1,)), ((), ())), pr...  61.6 us
    reshape x8, local copies, waits for them, and re-layouts, halves(): matrix.reshape(matrix.shape[0], 2, matrix.shape[1] // 2).transpose(1, 0, 2)  56.4 us
    slice x3, local copies, waits for them, and re-layouts, shards(): expand = mats[10:].transpose(2, 1, 0, 3)  47.6 us
    reshape x6, local copies, waits for them, and re-layouts, join_heads(): return values.reshape(values.shape[0] * BLOCK, HEADS * HEAD)  24.7 us
    reshape x2, local copies, waits for them, and re-layouts, shards(): project = mats[:8].reshape(4, 2, 2, 1024, WIDTH).transpose(3, 2, 1, 0, 4)  23.1 us

profile of v2, /device:TPU:0, one launch (start us, length us, event | category | flops | bytes accessed | tf_op | source)
XLA Modules:
  0.0 1090.6 jit_solution(17787806871812738868)
XLA Ops:
  3.9 240.6 %shard_map.186 = (bf16[42,2,2,2,2,2,64,256]{7,6,5,4,3,2,1,0:T(8,128)(2,1)}, bf16[2,2,2,2,2,2,176,512]{7,6,5,4,3,2,1,0:T(8,128)(2,1)}, bf16[512,1024]{1,0:T(8,128...) custom-call(bf16[64,2048]{1,0:T(8,128)(2,1)} %refs_0_.1, ...), custom_call_target="tpu_custom_call" | custom-call | tf_op jit(solution)/shard_map/pallas_call | solution.py:523
  246.4 4.0 fusion.109
  250.4 4.0 copy.99
  256.9 9.8 fusion.112
  266.7 8.4 copy.91
  275.1 8.4 copy.53
  283.4 11.9 %fusion.110 = (bf16[8,2,2,2,2,2,64,256]{7,6,5,4,3,2,1,0:T(8,128)(2,1)}, bf16[8,2,2,2,2,2,64,256]{7,6,5,4,3,2,1,0:T(8,128)(2,1)}) fusion(bf16[42,2,2,2,2,2,64,256]{7,6,5,4,3,2,1,0:T(8,128)(2,1)} %get-tuple-element.28), kind=kLoop, calls=%fused_computation.188 | loop fusion | bytes 33554432 | tf_op jit(solution)/shard_map/slice | solution.py:1010
  295.3 17.2 %fusion.111 = (bf16[11,2,2,2,2,2,64,256]{7,6,5,4,3,2,1,0:T(8,128)(2,1)}, bf16[11,2,2,2,2,2,64,256]{7,6,5,4,3,2,1,0:T(8,128)(2,1)}) fusion(bf16[42,2,2,2,2,2,64,256]{7,6,5,4,3,2,1,0:T(8,128)(2,1)} %get-tuple-element.28), kind=kLoop, calls=%fused_computation.189 | loop fusion | bytes 46137344 | tf_op jit(solution)/shard_map/slice | solution.py:1012
  312.5 15.2 %copy.92 = bf16[11,2,1024,256]{2,3,0,1:T(8,128)(2,1)} copy(bf16[11,2,1024,256]{3,2,1,0:T(8,128)(2,1)} %bitcast.271) | data formatting | bytes 23068672 | tf_op jit(solution)/shard_map/slice | solution.py:1012
  327.7 15.3 %copy.54 = bf16[11,2,1024,256]{2,3,0,1:T(8,128)(2,1)} copy(bf16[11,2,1024,256]{3,2,1,0:T(8,128)(2,1)} %bitcast.270) | data formatting | bytes 23068672 | tf_op jit(solution)/shard_map/slice | solution.py:1012
  343.0 11.5 %copy.126 = bf16[4,2,2,1024,256]{3,4,0,1,2:T(8,128)(2,1)} copy(bf16[4,2,2,1024,256]{4,3,2,1,0:T(8,128)(2,1)} %bitcast.275) | data formatting | bytes 16777216 | tf_op jit(solution)/shard_map/reshape | solution.py:1010
  354.5 11.6 %copy.90 = bf16[4,2,2,1024,256]{3,4,0,1,2:T(8,128)(2,1)} copy(bf16[4,2,2,1024,256]{4,3,2,1,0:T(8,128)(2,1)} %bitcast.274) | data formatting | bytes 16777216 | tf_op jit(solution)/shard_map/reshape | solution.py:1010
  366.1 12.5 %fusion.50 = f32[512,5632]{1,0:T(8,128)} fusion(bf16[1024,5632]{0,1:T(8,128)(2,1)} %bitcast.293, f32[2,512,1024]{2,1,0:T(8,128)} %get-tuple-element.26, f32[512]{0:T(512)S(1)} %get-tuple-element.90), kind=kOutput, calls=%fused_computation.117 | convolution fusion | flops 5906628608 | bytes 25167872 | tf_op jit(solution)/shard_map/dot_general | solution.py:938
  378.6 7.9 multiply_convert_fusion.5
  386.6 9.7 convolution_convert_fusion.4
  396.3 8.4 fusion.16
  404.7 8.3 copy.134
  420.1 12.2 %convolution_convert_fusion = bf16[1024,5632]{1,0:T(8,128)(2,1)} fusion(bf16[512,2816]{1,0:T(8,128)(2,1)} %get-tuple-element.59, bf16[512,2816]{1,0:T(8,128)(2,1)} %get-tuple-element.58, f32[2,512,1024]{2,1,0:T(8,128)} %get-tuple-element.26, f32[512]{0:T(512)S(1)} %get-tuple-element.90), kind=kOutput, calls=%fused_computation.4 | convolution fusion | flops 5923930112 | bytes 19400704 | tf_op jit(solution)/shard_map/dot_general | solution.py:48
  432.3 11.1 %copy.170 = bf16[128,2,8,2816]{3,2,0,1:T(8,128)(2,1)} copy(bf16[128,2,8,2816]{3,2,1,0:T(8,128)(2,1)} %bitcast.298) | data formatting | bytes 23068672 | tf_op jit(solution)/shard_map/reshape | solution.py:790
  443.5 9.2 fusion.53
  452.6 12.4 %slice_bitcast_fusion = (bf16[5,512,4,256]{3,1,0,2:T(8,128)(2,1)S(1)}, f32[5,512,4,256]{3,1,0,2:T(8,128)}, f32[5,512,4,256]{3,1,0,2:T(8,128)}, bf16[5,512,4,256]{3,1,0,2:T(8,128)(2,1)}) fusion(bf16[2,4,5,512,256]{4,3,2,1,0:T(8,128)(2,1)} %get-tuple-element.30), kind=kLoop, calls=%fused_computation.20 | loop fusion | flops 5242880 | bytes 41943040 | tf_op jit(solution)/shard_map/convert_element_type | solution.py:1020
  481.0 4.4 fusion.113
  501.4 7.7 add_divide_fusion.2
  526.2 4.4 squeeze.49
  530.7 5.8 fusion.1
  536.4 4.2 copy.135
  549.3 4.6 squeeze.23
  553.8 5.8 fusion
  559.6 4.2 copy.85
  563.8 6.1 multiply_multiply_fusion.1
  581.4 7.2 multiply_convert_fusion.21
  604.5 4.8 rev.4
  614.0 4.4 slice.151
  618.4 6.3 fusion.120
  627.6 5.7 copy.80
  633.3 5.2 reshape.403
  642.2 7.2 fusion.121
  649.4 6.5 fusion.42
  659.0 5.4 fusion.115
  664.5 4.4 add_bitcast_fusion.1
  668.9 5.7 copy.72
  680.9 4.5 copy.86
  685.5 4.2 reshape.404
  689.8 9.6 multiply_reduce_fusion.8
  700.0 7.9 multiply_convert_fusion.3
  707.8 9.8 convolution_convert_fusion.5
  717.7 8.0 fusion.21
  730.0 3.9 copy.128
  734.0 8.3 copy.130
  742.2 9.6 convolution_convert_fusion.1
  751.9 5.3 copy.171
  757.2 10.1 convolution_convert_fusion.2
  767.3 8.5 copy.172
  775.8 4.9 multiply_multiply_fusion
  795.0 4.1 fusion.55
  808.6 4.8 convert_bitcast_fusion.1
  813.4 4.4 copy.122
  821.1 4.8 multiply_reduce_fusion
  833.0 4.3 reshape.412
  840.1 4.2 reshape.413
  844.3 8.8 multiply_reduce_fusion.4
  855.1 7.7 convolution_convert_fusion.3
  862.7 8.3 copy.173
  871.0 211.7 %shard_map.187 = (f32[64,2048]{1,0:T(8,128)}, f32[64,512]{1,0:T(8,128)}, f32[64,2816]{1,0:T(8,128)}, f32[176,512]{1,0:T(8,128)}, f32[64,2048]{1,0:T(8,128)}, /*i...) custom-call(bf16[2,2,2,2,2,64,2048]{6,5,4,3,2,1,0:T(8,128)(2,1)} %bitcast.273, ...), custom_call_target="tpu_custom_call" | custom-call | tf_op jit(solution)/shard_map/pallas_call | solution.py:742
  (246 shorter events, 170.6 us)
Async XLA Ops:
  1.9 411.2 %copy-start.49 = (f32[512]{0:T(512)}, f32[512]{0:T(512)S(1)}, u32[]{:S(2)}) copy-start(f32[512]{0:T(512)S(1)} %get-tuple-element.104) | copy-start | bytes 6148
  354.5 24.1 %slice-start.11 = ((s8[5767168]{0:T(1024)(128)(4,1)}), s8[1572864]{0:T(1024)(128)(4,1)S(1)}, s32[]{:S(2)}) async-start(s8[5767168]{0:T(1024)(128)(4,1)} %bitcast.317), calls=%async_computation.11 | async-start | bytes 3145728
  366.1 12.5 %slice-start.12 = ((s8[5767168]{0:T(1024)(128)(4,1)}), s8[4194304]{0:T(1024)(128)(4,1)S(1)}, s32[]{:S(2)}) async-start(s8[5767168]{0:T(1024)(128)(4,1)} %bitcast.317), calls=%async_computation.12 | async-start | bytes 8388608
  366.1 12.5 %copy-start.37 = (bf16[1,512,1024]{2,1,0:T(8,128)(2,1)S(1)}, bf16[1,512,1024]{2,1,0:T(8,128)(2,1)}, u32[]{:S(2)}) copy-start(bf16[1,512,1024]{2,1,0:T(8,128)(2,1)} %param.21) | copy-start | bytes 3145732
  378.6 17.6 %slice-start.8 = ((s8[11534336]{0:T(1024)(128)(4,1)}), s8[4194304]{0:T(1024)(128)(4,1)S(1)}, s32[]{:S(2)}) async-start(s8[11534336]{0:T(1024)(128)(4,1)} %bitcast.294), calls=%async_computation.8 | async-start | bytes 8388608
  378.6 17.6 %slice-start.9 = ((s8[11534336]{0:T(1024)(128)(4,1)}), s8[4194304]{0:T(1024)(128)(4,1)S(1)}, s32[]{:S(2)}) async-start(s8[11534336]{0:T(1024)(128)(4,1)} %bitcast.294), calls=%async_computation.9 | async-start | bytes 8388608
  386.6 9.7 slice-start.10
  386.6 9.7 copy-start.13
  413.1 3.0 copy-start.55
  415.4 2.0 copy-start.21
  416.0 27.4 %copy-start.51 = (f32[512]{0:T(512)}, f32[512]{0:T(512)S(1)}, u32[]{:S(2)}) copy-start(f32[512]{0:T(512)S(1)} %get-tuple-element.86) | copy-start | bytes 6148
  420.1 23.4 %slice-start.2 = ((s8[11534336]{0:T(1024)(128)(4,1)}), s8[3145728]{0:T(1024)(128)(4,1)S(1)}, s32[]{:S(2)}) async-start(s8[11534336]{0:T(1024)(128)(4,1)} %bitcast.287), calls=%async_computation.2 | async-start | bytes 6291456
  420.1 23.4 %slice-start.3 = ((s8[11534336]{0:T(1024)(128)(4,1)}), s8[4194304]{0:T(1024)(128)(4,1)S(1)}, s32[]{:S(2)}) async-start(s8[11534336]{0:T(1024)(128)(4,1)} %bitcast.287), calls=%async_computation.3 | async-start | bytes 8388608
  432.3 11.2 %slice-start.4 = ((s8[11534336]{0:T(1024)(128)(4,1)}), s8[4194304]{0:T(1024)(128)(4,1)S(1)}, s32[]{:S(2)}) async-start(s8[11534336]{0:T(1024)(128)(4,1)} %bitcast.287), calls=%async_computation.4 | async-start | bytes 8388608
  432.3 11.2 %copy-start.14 = (f32[2,512,1024]{2,1,0:T(8,128)S(1)}, f32[2,512,1024]{2,1,0:T(8,128)}, u32[]{:S(2)}) copy-start(f32[2,512,1024]{2,1,0:T(8,128)} %get-tuple-element.26) | copy-start | bytes 12582916
  487.4 2.0 copy-start.6
  492.3 3.5 copy-start.16
  492.3 3.5 copy-start.45
  588.6 101.1 %copy-start.30 = (bf16[512,1024]{1,0:T(8,128)(2,1)}, bf16[512,1024]{1,0:T(8,128)(2,1)S(1)}, u32[]{:S(2)}) copy-start(bf16[512,1024]{1,0:T(8,128)(2,1)S(1)} %get-tuple-element.78) | copy-start | bytes 3145732
  590.9 3.9 copy-start.44
  594.8 3.0 copy-start.3
  597.9 3.3 copy-start.8
  597.9 3.3 copy-start.4
  618.4 6.3 copy-start.5
  618.4 6.3 copy-start.9
  638.5 3.7 copy-start
  659.0 5.4 copy-start.12
  680.9 19.0 %slice-start = ((s8[5767168]{0:T(1024)(128)(4,1)}), s8[1572864]{0:T(1024)(128)(4,1)S(1)}, s32[]{:S(2)}) async-start(s8[5767168]{0:T(1024)(128)(4,1)} %bitcast.276), calls=%async_computation | async-start | bytes 3145728
  689.7 9.7 copy-start.22
  689.7 9.7 copy-start.27
  689.7 10.2 slice-start.1
  699.9 17.7 %slice-start.5 = ((s8[11534336]{0:T(1024)(128)(4,1)}), s8[4194304]{0:T(1024)(128)(4,1)S(1)}, s32[]{:S(2)}) async-start(s8[11534336]{0:T(1024)(128)(4,1)} %bitcast.290), calls=%async_computation.5 | async-start | bytes 8388608
  699.9 17.7 %slice-start.6 = ((s8[11534336]{0:T(1024)(128)(4,1)}), s8[4194304]{0:T(1024)(128)(4,1)S(1)}, s32[]{:S(2)}) async-start(s8[11534336]{0:T(1024)(128)(4,1)} %bitcast.290), calls=%async_computation.6 | async-start | bytes 8388608
  707.8 9.8 slice-start.7
  707.8 9.8 copy-start.15
  707.8 9.8 copy-start.26
  717.7 8.0 copy-start.52
  717.7 8.0 copy-start.53
  727.3 48.5 %copy-start.23 = (f32[512,1024]{1,0:T(8,128)}, f32[512,1024]{1,0:T(8,128)S(1)}, u32[]{:S(2)}) copy-start(f32[512,1024]{1,0:T(8,128)S(1)} %fusion.20) | copy-start | bytes 6291460
  751.9 5.3 copy-start.31
  751.9 5.3 copy-start.32
  767.3 8.5 copy-start.19
  780.7 3.1 copy-start.7
  791.9 3.1 copy-start.10
  791.9 3.1 copy-start.54
  794.9 4.1 copy-start.11
  794.9 4.7 copy-start.20
  795.0 5.3 copy-start.28
  804.7 3.9 copy-start.29
  804.7 3.9 copy-start.46
  821.0 4.8 copy-start.2
  840.1 4.2 copy-start.25
  840.1 4.2 copy-start.33
  840.1 4.2 copy-start.50
  844.3 8.8 copy-start.24
  853.1 2.0 copy-start.34
  871.0 211.8 %copy-start.36 = (bf16[512,1024]{1,0:T(8,128)(2,1)S(1)}, bf16[512,1024]{1,0:T(8,128)(2,1)}, u32[]{:S(2)}) copy-start(bf16[512,1024]{1,0:T(8,128)(2,1)} %get-tuple-element.25) | copy-start | bytes 3145732
  1082.8 2.0 copy-start.48
  1082.8 2.7 copy-start.39
  1082.8 3.5 copy-start.43
  1084.0 3.1 copy-start.40
  1084.0 3.9 copy-start.47
  1084.8 3.7 copy-start.38
  1086.4 3.1 copy-start.42
  (6 other events, 10.0 us)

commit v3 on v2

--- a/solution.py
+++ b/solution.py
@@ -70,6 +70,8 @@
     return values.reshape(values.shape[0] * BLOCK, HEADS * HEAD)
 
 
+AXIS_NAMES = ("f", "zh", "zl", "y", "c")
+AXIS_OF = {"c": "c", "y": "y", "x": "f", "z1": "zl", "z2": "zh"}
 MESH = pl.DeviceIdType.MESH
 ANY = pl.BlockSpec(memory_space=pl.ANY)
 FULL = pl.BlockSpec(memory_space=pltpu.VMEM)
@@ -562,112 +564,85 @@
         ),
     )(*shards_of, tokens, validity)
 
-AXIS_NAMES = ("f", "zh", "zl", "y", "c")
-AXIS_OF = {"c": "c", "y": "y", "x": "f", "z1": "zl", "z2": "zh"}
+
 SCATTER_LAG = 3
 SCATTER_SLOTS = 3 * SCATTER_LAG + 1
-TERM_SLOTS = SCATTER_LAG + 1
-TALL = 64
-TALL_WIDTH = 256
-OTHER_WIDTH = 128
-
-
-def late_z(chunk):
-    return chunk % 5 == 3
+TERM_SLOTS = SCATTER_LAG
+TALL_SLOTS = 6
+TALL_TERM_SLOTS = 2
+OUTPUT_TURN = EXPAND_CHUNKS
+PROJECT_TURN = EXPAND_CHUNKS + OUTPUT_CHUNKS
+TALL_ROWS = 176
 
 
 class Scatter:
-    def __init__(self, chunks, rows_of, terms, outs, sems, buffers):
-        self.chunks = chunks
-        self.rows_of = rows_of
-        self.terms = terms
-        self.outs = outs
-        self.load_sem, self.store_sem, self.send_sem, self.recv_sem = sems
-        self.buffers = buffers
+    def __init__(self, outs, sems, wide, tall):
+        self.outs, self.tall_outs = outs
+        self.send_sem, self.recv_sem, self.tall_send, self.tall_recv = sems[:4]
+        self.store_sem, self.tall_store = sems[4:]
+        self.wide, self.tall = wide[:6], tall[:6]
+        self.result, self.tall_result = wide[6], tall[6]
         self.places, self.targets = neighbours()
 
-    def load(self, chunk):
-        weight, start, width = self.chunks[chunk]
-        return pltpu.make_async_copy(
-            self.terms[weight].at[..., pl.ds(start, width)],
-            self.buffers[self.rows_of[weight]][0].at[chunk % TERM_SLOTS],
-            self.load_sem.at[chunk % TERM_SLOTS],
+    def tall_turn(self, chunk):
+        layer = chunk // LAYER_CHUNKS
+        turn = chunk % LAYER_CHUNKS - OUTPUT_TURN
+        due = (turn >= 0) & (turn < 2 * SHRINK_PARTS) & (turn % 2 == 0)
+        return layer * SHRINK_PARTS + turn // 2, turn // 2, due
+
+    def wide_parts(self):
+        half = WIDTH // 2
+        return (
+            (pl.ds(0, half), ("c", "y", "x", "z1", "z2")),
+            (pl.ds(half, half), ("c", "x", "y", "z1", "z2")),
         )
 
-    def store(self, chunk):
-        weight, start, width = self.chunks[chunk]
-        return pltpu.make_async_copy(
-            self.result(chunk),
-            self.outs[weight].at[:, pl.ds(start, width)],
-            self.store_sem.at[chunk % 2],
-        )
-
-    def result(self, chunk):
-        return self.buffers[self.rows_of[self.chunks[chunk][0]]][6].at[chunk % 2]
-
-    def parts(self, chunk):
-        weight, start, width = self.chunks[chunk]
-        if self.rows_of[weight] == TALL:
-            halves = [(0, width // 2, 0), (width // 2, width // 2, 1)]
-        else:
-            halves = [(0, width, chunk % 2)]
-        out = []
-        for begin, extent, turn in halves:
-            plane = ("y", "x") if turn == 0 else ("x", "y")
-            order = ("z1", "z2") + plane if late_z(chunk) else plane + ("z1", "z2")
-            out.append((begin, extent, ("c",) + order))
-        return out
-
-    def arrived(self, chunk, phase):
-        rows = self.rows_of[self.chunks[chunk][0]]
-        return self.buffers[rows][1 + phase].at[chunk % SCATTER_SLOTS]
-
-    def dims_after(self, order, phase):
+    def tall_parts(self, odd):
+        plane = ("x", "y") if odd else ("y", "x")
+        return ((pl.ds(0, SHRINK_WIDTH), ("c", "z1", "z2") + plane),)
+
+    def left(self, order, phase):
         used = set(AXIS_OF[target] for target in order[: phase + 1])
         return [name for name in AXIS_NAMES if name not in used]
 
-    def source(self, chunk, phase, order):
-        rows = self.rows_of[self.chunks[chunk][0]]
+    def source(self, buffers, slots, phase, order):
         if phase == 0:
-            return self.buffers[rows][0].at[chunk % TERM_SLOTS], list(AXIS_NAMES)
-        return self.arrived(chunk, phase - 1), self.dims_after(order, phase - 1)
-
-    def messages(self, phase, chunk):
-        parts = self.parts(chunk)
-        if len(set(order[: phase + 1] for _, _, order in parts)) == 1:
-            parts = [(0, self.chunks[chunk][2], parts[0][2])]
+            return buffers[0].at[slots[0]], list(AXIS_NAMES)
+        return buffers[phase].at[slots[1]], self.left(order, phase - 1)
+
+    def messages(self, buffers, slots, sems, phase, parts):
+        if phase == 0 and len(parts) == 2:
+            parts = ((pl.ds(0, WIDTH), parts[0][1]),)
         out = []
-        for part, (begin, extent, order) in enumerate(parts):
-            source, dims = self.source(chunk, phase, order)
+        for part, (lanes, order) in enumerate(parts):
+            source, dims = self.source(buffers, slots, phase, order)
             target = order[phase]
-            cut = AXIS_OF[target]
-            lanes = pl.ds(begin, extent)
-            away = tuple(1 - self.places[d] if d == cut else slice(None) for d in dims)
-            whole = tuple(slice(None) for _ in self.dims_after(order, phase))
-            slot = chunk % SCATTER_SLOTS
+            away = tuple(
+                1 - self.places[d] if d == AXIS_OF[target] else slice(None) for d in dims
+            )
+            whole = tuple(slice(None) for _ in self.left(order, phase))
+            place = (2 * phase + part, slots[1])
             out.append(
                 pltpu.make_async_remote_copy(
                     src_ref=source.at[away + (slice(None), lanes)],
-                    dst_ref=self.arrived(chunk, phase).at[whole + (slice(None), lanes)],
-                    send_sem=self.send_sem.at[2 * phase + part, slot],
-                    recv_sem=self.recv_sem.at[2 * phase + part, slot],
+                    dst_ref=buffers[1 + phase].at[(slots[1],) + whole + (slice(None), lanes)],
+                    send_sem=sems[0].at[place],
+                    recv_sem=sems[1].at[place],
                     device_id=self.targets[target],
                     device_id_type=MESH,
                 )
             )
         return out
 
-    def add(self, phase, chunk):
-        for begin, extent, order in self.parts(chunk):
-            source, dims = self.source(chunk, phase, order)
+    def add(self, buffers, slots, phase, parts, result):
+        for lanes, order in parts:
+            source, dims = self.source(buffers, slots, phase, order)
             cut = AXIS_OF[order[phase]]
-            kept = self.dims_after(order, phase)
-            ref = self.arrived(chunk, phase)
-            lanes = pl.ds(begin, extent)
-            result = self.result(chunk)
+            kept = self.left(order, phase)
+            ref = buffers[1 + phase].at[slots[1]]
 
             def body(unit, carry):
-                index = tuple((unit >> (len(kept) - 1 - b)) & 1 for b in range(len(kept)))
+                index = tuple((unit // 2 ** (len(kept) - 1 - b)) % 2 for b in range(len(kept)))
                 where = dict(zip(kept, index))
                 where[cut] = self.places[cut]
                 mine = source[tuple(where[d] for d in dims) + (slice(None), lanes)]
@@ -675,7 +650,7 @@
                 if phase < 4:
                     ref[index + (slice(None), lanes)] = came + mine
                 else:
-                    result[:, lanes] = came.astype(jnp.float32) + mine.astype(jnp.float32)
+                    result[:, lanes] = came.astype(WIDE) + mine.astype(WIDE)
                 return carry
 
             if kept:
@@ -683,115 +658,585 @@
             else:
                 body(0, 0)
 
-
-def scatter_kernel(chunks, rows_of, *refs):
-    terms = refs[:WEIGHTS]
-    outs = refs[WEIGHTS : 2 * WEIGHTS]
-    scratch = refs[2 * WEIGHTS :]
-    buffers = {TALL: scratch[4:11], rows_of[3]: scratch[11:18]}
-    work = Scatter(chunks, rows_of, terms, outs, scratch[:4], buffers)
-    greet(work.targets)
-    loads = {0: work.load(0)}
-    loads[0].start()
-    phases = 5
-    live = {}
-    stores = {}
-    for step in range(len(chunks) + phases * SCATTER_LAG):
-        for phase in range(phases, -1, -1):
+    def wide_slots(self, chunk):
+        return (chunk % TERM_SLOTS, chunk % SCATTER_SLOTS)
+
+    def tall_slots(self, place):
+        return (place % TALL_TERM_SLOTS, place % TALL_SLOTS)
+
+    def wide_messages(self, phase, chunk):
+        return self.messages(
+            self.wide,
+            self.wide_slots(chunk),
+            (self.send_sem, self.recv_sem),
+            phase,
+            self.wide_parts(),
+        )
+
+    def tall_messages(self, phase, place, odd):
+        return self.messages(
+            self.tall,
+            self.tall_slots(place),
+            (self.tall_send, self.tall_recv),
+            phase,
+            self.tall_parts(odd),
+        )
+
+    def store(self, chunk):
+        return pltpu.make_async_copy(
+            self.result.at[chunk % 2], self.outs.at[chunk], self.store_sem.at[chunk % 2]
+        )
+
+    def store_tall(self, place):
+        return pltpu.make_async_copy(
+            self.tall_result.at[place % 2], self.tall_outs.at[place], self.tall_store.at[place % 2]
+        )
+
+    def start(self, phase, chunk):
+        for copy in self.wide_messages(phase, chunk):
+            copy.start()
+        place, part, due = self.tall_turn(chunk)
+        for odd in range(2):
+
+            @pl.when(due & (part % 2 == odd))
+            def _(odd=odd):
+                for copy in self.tall_messages(phase, place, odd):
+                    copy.start()
+
+    def take(self, phase, chunk):
+        for copy in self.wide_messages(phase, chunk):
+            copy.wait()
+        if phase == PHASES - 1:
+            pl.when(chunk >= 2)(lambda: self.store(chunk).wait())
+        self.add(
+            self.wide, self.wide_slots(chunk), phase, self.wide_parts(), self.result.at[chunk % 2]
+        )
+        place, part, due = self.tall_turn(chunk)
+        for odd in range(2):
+
+            @pl.when(due & (part % 2 == odd))
+            def _(odd=odd):
+                for copy in self.tall_messages(phase, place, odd):
+                    copy.wait()
+                if phase == PHASES - 1:
+                    pl.when(place >= 2)(lambda: self.store_tall(place).wait())
+                self.add(
+                    self.tall,
+                    self.tall_slots(place),
+                    phase,
+                    self.tall_parts(odd),
+                    self.tall_result.at[place % 2],
+                )
+                if phase == PHASES - 1:
+                    self.store_tall(place).start()
+
+        if phase == PHASES - 1:
+            self.store(chunk).start()
+
+    def older(self, step):
+        for phase in range(PHASES, 0, -1):
             chunk = step - phase * SCATTER_LAG
-            if not 0 <= chunk < len(chunks):
-                continue
-            if phase == 0:
-                loads.pop(chunk).wait()
-            else:
-                for copy in live.pop((phase - 1, chunk)):
-                    copy.wait()
-                if phase == phases and chunk - 2 in stores:
-                    stores.pop(chunk - 2).wait()
-                work.add(phase - 1, chunk)
-            if phase < phases:
-                live[(phase, chunk)] = work.messages(phase, chunk)
-                for copy in live[(phase, chunk)]:
-                    copy.start()
-            else:
-                stores[chunk] = work.store(chunk)
-                stores[chunk].start()
-        if step + 1 < len(chunks):
-            loads[step + 1] = work.load(step + 1)
-            loads[step + 1].start()
-    for copy in stores.values():
-        copy.wait()
-
-
-def scatter_buffers(rows, width):
-    low = jnp.bfloat16
-    out = [pltpu.VMEM((TERM_SLOTS, 2, 2, 2, 2, 2, rows, width), low)]
-    for phase in range(5):
-        out.append(pltpu.VMEM((SCATTER_SLOTS,) + (2,) * (4 - phase) + (rows, width), low))
-    out.append(pltpu.VMEM((2, rows, width), jnp.float32))
-    return out
-
-
-def scatter_all(terms):
-    shapes = [item.shape[5:] for item in terms]
-    rows_of = [shape[0] for shape in shapes]
-    chunks = []
-    for i in range(WEIGHTS - 1, -1, -1):
-        width = TALL_WIDTH if rows_of[i] == TALL else OTHER_WIDTH
-        chunks += [(i, start, width) for start in range(0, shapes[i][1], width)]
+
+            @pl.when((chunk >= 0) & (chunk < CHUNKS))
+            def _(phase=phase, chunk=chunk):
+                self.take(phase - 1, chunk)
+                if phase < PHASES:
+                    self.start(phase, chunk)
+
+    def finish(self):
+        for chunk in (CHUNKS - 2, CHUNKS - 1):
+            self.store(chunk).wait()
+        for place in (2 * SHRINK_PARTS - 2, 2 * SHRINK_PARTS - 1):
+            self.store_tall(place).wait()
+
+
+def norm_slope(values, inverse, upstream, mean):
+    return inverse * (upstream - values * (inverse * inverse) * mean)
+
+
+def gate_back(update, mixture, coming, first):
+    inverse = lax.rsqrt(pair_mean(mixture * mixture, first) + epsilon)
+    curve = logistic(update)
+    back_update = coming * (mixture * inverse) * (curve * (1.0 + update * (1.0 - curve)))
+    gate = coming * (update * curve)
+    back_mixture = norm_slope(mixture, inverse, gate, pair_mean(gate * mixture, first))
+    return back_update, back_mixture
+
+
+def local_mixer_back(group, stage, validity, coming, back):
+    def body(turn, carry):
+        rows = pl.ds(pl.multiple_of((turn // 2) * 128, 128), 128)
+        lanes = pl.ds(pl.multiple_of((turn % 2) * 128, 128), 128)
+        columns = pl.ds(pl.multiple_of(group * WIDTH + (turn % 2) * 128, 128), 128)
+        first = first_lanes(128)
+        q, k, v = stage[0, rows, lanes], stage[1, rows, lanes], stage[2, rows, lanes]
+        update = stage[3, rows, lanes].astype(WIDE)
+        mixture = stage[4, rows, lanes].astype(WIDE)
+        back_update, back_mixture = gate_back(update, mixture, coming[rows, columns], first)
+        back[1, 1, rows, lanes] = back_update.astype(LOW)
+        grad = (back_mixture.astype(LOW).astype(WIDE) * validity[rows, :]).astype(LOW)
+        keep = block_mask(128)
+        zero = jnp.zeros_like(q)
+        out = []
+        for head in range(2):
+            here = first == (head == 0)
+            scores = contract_cols(jnp.where(here, q, zero), k) * HEAD ** (-0.5)
+            scores = jnp.where(keep, scores, -1e30)
+            weights = jnp.exp(scores - jnp.max(scores, axis=-1, keepdims=True))
+            attend = weights / jnp.sum(weights, axis=-1, keepdims=True)
+            back_attend = contract_cols(jnp.where(here, grad, zero), v)
+            total = jnp.sum(back_attend * attend, axis=-1, keepdims=True)
+            back_scores = (attend * (back_attend - total)).astype(LOW)
+            out.append(
+                (
+                    dot(back_scores, k) * HEAD ** (-0.5),
+                    contract_rows(back_scores, q) * HEAD ** (-0.5),
+                    contract_rows(attend.astype(LOW), grad),
+                )
+            )
+        for kind, (i, j) in enumerate(((0, 0), (1, 0), (0, 1))):
+            back[i, j, rows, lanes] = jnp.where(first, out[0][kind], out[1][kind]).astype(LOW)
+        return carry
+
+    lax.fori_loop(0, 2 * ROWS // 128, body, 0)
+
+
+def linear_mixer_back(group, stage, coming, back):
+    half = ROWS // 2
+
+    def body(pair, carry):
+        lanes = pl.ds(pl.multiple_of(pair * 128, 128), 128)
+        columns = pl.ds(pl.multiple_of(group * WIDTH + pair * 128, 128), 128)
+        first = first_lanes(ROWS)
+        queries = stage[0, :, lanes].astype(WIDE)
+        keys_all = stage[1, :, lanes].astype(WIDE)
+        v = stage[2, :, lanes]
+        fq = softplus(queries).astype(LOW)
+        fk = softplus(keys_all).astype(LOW)
+        update = stage[3, :, lanes].astype(WIDE)
+        mixture = stage[4, :, lanes].astype(WIDE)
+        back_update, back_mixture = gate_back(update, mixture, coming[:, columns], first)
+        back[1, 1, :, lanes] = back_update.astype(LOW)
+        grad = back_mixture.astype(LOW)
+        zero = jnp.zeros((half, 128), LOW)
+        tiles = []
+        for t in range(2):
+            reach = (t + 1) * half
+            i = lax.broadcasted_iota(jnp.int32, (half, reach), 0) + t * half
+            j = lax.broadcasted_iota(jnp.int32, (half, reach), 1)
+            mine_q = fq[t * half : reach]
+            mine_g = grad[t * half : reach]
+            out = []
+            for head in range(2):
+                here = first[:half] == (head == 0)
+                scores = contract_cols(jnp.where(here, mine_q, zero), fk[:reach])
+                scores = jnp.where(j <= i, scores, 0.0).astype(LOW)
+                inner = contract_cols(jnp.where(here, mine_g, zero), v[:reach])
+                inner = jnp.where(j <= i, inner, 0.0).astype(LOW)
+                out.append(
+                    (dot(inner, fk[:reach]), contract_rows(inner, mine_q), contract_rows(scores, mine_g))
+                )
+            tiles.append(
+                [jnp.where(first[: out[0][n].shape[0]], out[0][n], out[1][n]) for n in range(3)]
+            )
+        for t in range(2):
+            rows = pl.ds(t * half, half)
+            span = slice(t * half, (t + 1) * half)
+            back_q = tiles[t][0]
+            back_k = tiles[1][1][span]
+            back_v = tiles[1][2][span]
+            if t == 0:
+                back_k = back_k + tiles[0][1]
+                back_v = back_v + tiles[0][2]
+            back[0, 0, rows, lanes] = (back_q * logistic(queries[span])).astype(LOW)
+            back[1, 0, rows, lanes] = (back_k * logistic(keys_all[span])).astype(LOW)
+            back[0, 1, rows, lanes] = back_v.astype(LOW)
+        return carry
+
+    lax.fori_loop(0, 2, body, 0)
+
+
+def over_rows(act):
+    def body(t, carry):
+        act(pl.ds(pl.multiple_of(t * 128, 128), 128))
+        return carry
+
+    lax.fori_loop(0, ROWS // 128, body, 0)
+
+
+def backward_kernel(*refs):
+    cotangent, tokens, validity = refs[:3]
+    held, tall, between, middles, gates, stages, halves_in = refs[3:10]
+    tokens_out, outs, tall_outs = refs[10:13]
+    scratch = refs[13:]
+    scatter_sems, loads = scratch[:6], scratch[6:10]
+    load_sem, half_sem, stage_sem, misc_sem = loads
+    wide_buffers, tall_buffers = scratch[10:17], scratch[17:24]
+    (
+        loaded,
+        half_in,
+        stage,
+        shrink,
+        hidden_turned,
+        branch,
+        gated_branch,
+        up,
+        sums,
+        middle,
+        layer_in,
+        gated,
+        turned,
+        back,
+    ) = scratch[24:]
+    scatter = Scatter((outs, tall_outs), scatter_sems, wide_buffers, tall_buffers)
+
+    def load(chunk, number):
+        return pltpu.make_async_copy(
+            held.at[chunk], loaded.at[number % 2], load_sem.at[number % 2]
+        )
+
+    def load_half(layer, part, number):
+        return pltpu.make_async_copy(
+            halves_in.at[layer, part], half_in.at[number % 2], half_sem.at[number % 2]
+        )
+
+    def load_stage(layer, group):
+        return pltpu.make_async_copy(stages.at[layer, group], stage, stage_sem)
+
+    def fetch(kind, layer):
+        source, target = (
+            (tall, shrink),
+            (middles, middle),
+            (gates, gated),
+        )[kind]
+        return pltpu.make_async_copy(source.at[layer], target, misc_sem.at[kind])
+
+    def fetch_between():
+        return pltpu.make_async_copy(between, layer_in, misc_sem.at[3])
+
+    def prefetch(number):
+        layer = 1 - number // LAYER_CHUNKS
+        turn = number % LAYER_CHUNKS
+        base = LAYER_CHUNKS * layer
+
+        @pl.when(turn < OUTPUT_TURN)
+        def _():
+            load(base + PROJECT_CHUNKS + OUTPUT_CHUNKS + turn, number).start()
+            load_half(layer, turn, number).start()
+
+        @pl.when((turn >= OUTPUT_TURN) & (turn < PROJECT_TURN))
+        def _():
+            load(base + PROJECT_CHUNKS + turn - OUTPUT_TURN, number).start()
+
+        @pl.when(turn >= PROJECT_TURN)
+        def _():
+            load(base + turn - PROJECT_TURN, number).start()
+
+            @pl.when((turn - PROJECT_TURN) % 2 == 0)
+            def _():
+                load_stage(layer, (turn - PROJECT_TURN) // 2).start()
+
+    prefetch(jnp.int32(0))
+    for kind in range(3):
+        fetch(kind, 1).start()
+    fetch_between().start()
+
+    def begin_rows(rows):
+        up[rows, :] = cotangent[rows, :].astype(WIDE) * validity[rows, :]
+
+    over_rows(begin_rows)
+    greet(scatter.targets)
+
+    def turn_norm(source):
+        def act(rows):
+            turned[:, rows] = simple_norm(source[rows, :]).astype(LOW).T
+
+        over_rows(act)
+
+    def expand_start(layer):
+        fetch(0, 1).wait()
+        fetch(1, 1).wait()
+
+        def act(rows):
+            branch[rows, :] = up[rows, :].astype(LOW)
+            sums[0, rows, :] = jnp.zeros((128, 1024), WIDE)
+
+        over_rows(act)
+        turn_norm(middle)
+
+    def expand_turn(part, number):
+        load_half(0, 0, number).wait()
+        rows = pl.ds(pl.multiple_of(part * WIDTH, WIDTH), WIDTH)
+        back_hidden = contract_cols(branch[:, :512], shrink[0, rows, :])
+        back_hidden = back_hidden + contract_cols(branch[:, 512:], shrink[1, rows, :])
+        first = half_in[number % 2, 0].astype(WIDE)
+        second = half_in[number % 2, 1].astype(WIDE)
+        back[0, 0] = (back_hidden * second).astype(LOW)
+        back[0, 1] = (back_hidden * first).astype(LOW)
+        hidden_turned[rows, :] = (first * second).astype(LOW).T
+
+    def output_start(layer):
+        fetch(2, 1).wait()
+
+        def act(rows):
+            values = middle[rows, :]
+            back_second = sums[0, rows, :]
+            new = up[rows, :] + norm_back(values, back_second)
+            up[rows, :] = new
+            gated_branch[rows, :] = new.astype(LOW)
+            sums[1, rows, :] = jnp.zeros((128, 1024), WIDE)
+            turned[:, rows] = gated[rows, :].T
+
+        over_rows(act)
+
+        @pl.when(layer == 1)
+        def _():
+            fetch(0, 0).start()
+
+    def output_turn(part):
+        for f in range(2):
+            lanes = pl.ds(pl.multiple_of(f * 512 + part * WIDTH, WIDTH), WIDTH)
+            back[0, f] = gated_branch[:, lanes]
+
+    def project_start(layer):
+        @pl.when(layer == 1)
+        def _():
+            fetch_between().wait()
+            fetch(1, 0).start()
+            fetch(2, 0).start()
+
+        @pl.when(layer == 0)
+        def _():
+            def act(rows):
+                layer_in[rows, :] = tokens[rows, :].astype(WIDE) * validity[rows, :]
+
+            over_rows(act)
+
+        def clear(rows):
+            sums[0, rows, :] = jnp.zeros((128, 1024), WIDE)
+
+        over_rows(clear)
+        turn_norm(layer_in)
+
+    def project_turn(layer, group):
+        load_stage(0, 0).wait()
+        coming = sums.at[1]
+        pl.when(layer == 1)(lambda: linear_mixer_back(group, stage, coming, back))
+        pl.when(layer == 0)(lambda: local_mixer_back(group, stage, validity, coming, back))
+
+    def finish_layer(layer):
+        def act(rows):
+            up[rows, :] = up[rows, :] + norm_back(layer_in[rows, :], sums[0, rows, :])
+
+        over_rows(act)
+
+    def terms(number, which):
+        slot = number % TERM_SLOTS
+        out = wide_buffers[0]
+
+        def body(tile, carry):
+            f = tile // 4
+            rows = pl.ds(pl.multiple_of((tile % 4) * 256, 256), 256)
+            value = dot(turned[rows, :], back[which, f]).astype(LOW)
+            out[slot, f, (tile % 4) // 2, tile % 2] = value.reshape(2, 2, 64, WIDTH)
+            return carry
+
+        lax.fori_loop(0, 8, body, 0)
+
+    def tall_terms(place, part):
+        slot = place % TALL_TERM_SLOTS
+        out = tall_buffers[0]
+
+        def body(tile, carry):
+            f = tile // 4
+            rows = pl.ds(pl.multiple_of((tile % 4) * 4 * TALL_ROWS, 4 * TALL_ROWS), 4 * TALL_ROWS)
+            lanes = pl.ds(pl.multiple_of(f * 512 + part * SHRINK_WIDTH, 128), SHRINK_WIDTH)
+            value = dot(hidden_turned[rows, :], branch[:, lanes]).astype(LOW)
+            out[slot, f, (tile % 4) // 2, tile % 2] = value.reshape(2, 2, TALL_ROWS, SHRINK_WIDTH)
+            return carry
+
+        lax.fori_loop(0, 8, body, 0)
+
+    def spread(number, which, kind):
+        def body(t, carry):
+            rows = pl.ds(pl.multiple_of(t * 256, 256), 256)
+            value = contract_cols(back[which, 0, rows, :], loaded[number % 2, 0])
+            value = value + contract_cols(back[which, 1, rows, :], loaded[number % 2, 1])
+            sums[kind, rows, :] = sums[kind, rows, :] + value
+            return carry
+
+        lax.fori_loop(0, 2, body, 0)
+
+    def body(step, carry):
+        pl.when(step + 1 < CHUNKS)(lambda: prefetch(step + 1))
+        scatter.older(step)
+
+        @pl.when(step < CHUNKS)
+        def _():
+            layer = 1 - step // LAYER_CHUNKS
+            turn = step % LAYER_CHUNKS
+            pl.when(turn == 0)(lambda: expand_start(layer))
+            pl.when(turn == OUTPUT_TURN)(lambda: output_start(layer))
+            pl.when(turn == PROJECT_TURN)(lambda: project_start(layer))
+            pl.when(turn < OUTPUT_TURN)(lambda: expand_turn(turn, step))
+            pl.when((turn >= OUTPUT_TURN) & (turn < PROJECT_TURN))(
+                lambda: output_turn(turn - OUTPUT_TURN)
+            )
+            pl.when((turn >= PROJECT_TURN) & ((turn - PROJECT_TURN) % 2 == 0))(
+                lambda: project_turn(layer, (turn - PROJECT_TURN) // 2)
+            )
+            in_project = jnp.minimum(jnp.maximum(turn - PROJECT_TURN + 1, 0), 1)
+            in_output = jnp.minimum(jnp.maximum(turn - OUTPUT_TURN + 1, 0), 1) - in_project
+            which = in_project * ((turn + PROJECT_TURN) % 2)
+            terms(step, which)
+            place, part, due = scatter.tall_turn(step)
+            pl.when(due)(lambda: tall_terms(place, part))
+            scatter.start(0, step)
+            load(0, step).wait()
+            spread(step, which, in_output)
+            pl.when(turn == LAYER_CHUNKS - 1)(lambda: finish_layer(layer))
+
+            @pl.when(step == CHUNKS - 1)
+            def _():
+                def act(rows):
+                    up[rows, :] = up[rows, :] * validity[rows, :]
+
+                over_rows(act)
+                pltpu.make_async_copy(up, tokens_out, misc_sem.at[3]).start()
+
+        return carry
+
+    lax.fori_loop(0, CHUNKS + PHASES * SCATTER_LAG, body, 0)
+    pltpu.make_async_copy(up, tokens_out, misc_sem.at[3]).wait()
+    scatter.finish()
+
+
+def scatter_buffers(terms, slots, rows, width):
+    bits = [(2,) * (4 - phase) for phase in range(5)]
+    return (
+        [pltpu.VMEM((terms, 2, 2, 2, 2, 2, rows, width), LOW)]
+        + [pltpu.VMEM((slots,) + lead + (rows, width), LOW) for lead in bits]
+        + [pltpu.VMEM((2, rows, width), WIDE)]
+    )
+
+
+def run_backward(cotangent, tokens, validity, forward):
+    struct = jax.ShapeDtypeStruct
+    held, tall, mixed_out, between, middles, gates, stages, kept = forward
     return pl.pallas_call(
-        functools.partial(scatter_kernel, chunks, rows_of),
-        out_shape=tuple(jax.ShapeDtypeStruct(shape, jnp.float32) for shape in shapes),
-        in_specs=[ANY] * WEIGHTS,
-        out_specs=(ANY,) * WEIGHTS,
+        backward_kernel,
+        out_shape=(
+            struct((ROWS, 1024), WIDE),
+            struct((CHUNKS, 64, WIDTH), WIDE),
+            struct((2 * SHRINK_PARTS, TALL_ROWS, SHRINK_WIDTH), WIDE),
+        ),
+        in_specs=[FULL] * 3 + [ANY] * 7,
+        out_specs=(ANY,) * 3,
         scratch_shapes=[
-            pltpu.SemaphoreType.DMA((TERM_SLOTS,)),
-            pltpu.SemaphoreType.DMA((2,)),
             pltpu.SemaphoreType.DMA((10, SCATTER_SLOTS)),
             pltpu.SemaphoreType.DMA((10, SCATTER_SLOTS)),
+            pltpu.SemaphoreType.DMA((10, TALL_SLOTS)),
+            pltpu.SemaphoreType.DMA((10, TALL_SLOTS)),
+            pltpu.SemaphoreType.DMA((2,)),
+            pltpu.SemaphoreType.DMA((2,)),
+            pltpu.SemaphoreType.DMA((2,)),
+            pltpu.SemaphoreType.DMA((2,)),
+            pltpu.SemaphoreType.DMA,
+            pltpu.SemaphoreType.DMA((4,)),
         ]
-        + scatter_buffers(TALL, TALL_WIDTH)
-        + scatter_buffers(rows_of[3], OTHER_WIDTH),
+        + scatter_buffers(TERM_SLOTS, SCATTER_SLOTS, 64, WIDTH)
+        + scatter_buffers(TALL_TERM_SLOTS, TALL_SLOTS, TALL_ROWS, SHRINK_WIDTH)
+        + [
+            pltpu.VMEM((2, 2, 1024, WIDTH), LOW),
+            pltpu.VMEM((2, 2, ROWS, WIDTH), LOW),
+            pltpu.VMEM((5, ROWS, WIDTH), LOW),
+            pltpu.VMEM((2, 2816, 512), LOW),
+            pltpu.VMEM((2816, ROWS), LOW),
+            pltpu.VMEM((ROWS, 1024), LOW),
+            pltpu.VMEM((ROWS, 1024), LOW),
+            pltpu.VMEM((ROWS, 1024), WIDE),
+            pltpu.VMEM((2, ROWS, 1024), WIDE),
+            pltpu.VMEM((ROWS, 1024), WIDE),
+            pltpu.VMEM((ROWS, 1024), WIDE),
+            pltpu.VMEM((ROWS, 1024), LOW),
+            pltpu.VMEM((1024, ROWS), LOW),
+            pltpu.VMEM((2, 2, ROWS, WIDTH), LOW),
+        ],
         compiler_params=pltpu.CompilerParams(
-            collective_id=1, has_side_effects=True, vmem_limit_bytes=60 << 20
+            collective_id=1, has_side_effects=True, vmem_limit_bytes=62 << 20
         ),
-    )(*terms)
+    )(
+        cotangent,
+        tokens,
+        validity,
+        held.reshape(CHUNKS, 2, 1024, WIDTH),
+        tall.reshape(2, 2, 2816, 512),
+        between,
+        middles,
+        gates,
+        stages,
+        kept,
+    )
+
+
+def unpack_kernel(mixed_in, tokens_in, chunks, parts, *refs):
+    outs, sem = refs[:-1], refs[-1]
+    copies = [(mixed_in, outs[0]), (tokens_in, outs[1])]
+    for order in range(2):
+        layer = 1 - order
+        for turn in range(LAYER_CHUNKS):
+            number = order * LAYER_CHUNKS + turn
+            if turn < OUTPUT_TURN:
+                weight, start = 2, chunk_columns(2, turn)
+            elif turn < PROJECT_TURN:
+                weight, start = 1, chunk_columns(1, turn - OUTPUT_TURN)
+            else:
+                weight, start = 0, chunk_columns(0, turn - PROJECT_TURN)
+            target = outs[2 + 4 * layer + weight].at[:, pl.ds(start, WIDTH)]
+            copies.append((chunks.at[number], target))
+        for part in range(SHRINK_PARTS):
+            target = outs[5 + 4 * layer].at[:, pl.ds(part * SHRINK_WIDTH, SHRINK_WIDTH)]
+            copies.append((parts.at[order * SHRINK_PARTS + part], target))
+    copies = [
+        pltpu.make_async_copy(source, target, sem.at[i])
+        for i, (source, target) in enumerate(copies)
+    ]
+    for copy in copies:
+        copy.start()
+    for copy in copies:
+        copy.wait()
+
+
+def unpack(mixed_out, tokens_gradient, chunks, parts, shards_of):
+    struct = jax.ShapeDtypeStruct
+    count = 2 + CHUNKS + 2 * SHRINK_PARTS
+    return pl.pallas_call(
+        unpack_kernel,
+        out_shape=(struct(mixed_out.shape, LOW), struct(tokens_gradient.shape, WIDE))
+        + tuple(struct(item.shape, WIDE) for item in shards_of),
+        in_specs=[FULL] * 4,
+        out_specs=(ANY,) * (2 + WEIGHTS),
+        scratch_shapes=[pltpu.SemaphoreType.DMA((count,))],
+        compiler_params=pltpu.CompilerParams(vmem_limit_bytes=32 << 20),
+    )(mixed_out, tokens_gradient, chunks, parts)
 
 
 def gather_weights(shards_of):
-    wide = [
+    return [
         lax.all_gather(lax.all_gather(item, "fsdp", axis=1, tiled=True), "dp", axis=0, tiled=True)
         for item in shards_of
     ]
-    return [
-        item.reshape(item.shape[0], 2, item.shape[1] // 2).transpose(1, 0, 2) for item in wide
+
+
+def settle_gradients(terms):
+    tall = [
+        lax.psum_scatter(item.astype(jnp.bfloat16), "dp", scatter_dimension=0, tiled=True)
+        for item in terms
     ]
-
-
-def settle_gradients(terms, direct):
-    if direct:
-        return scatter_all(
-            [
-                item.reshape(2, 2, 2, 2, 2, item.shape[1] // 16, item.shape[2])
-                for item in terms
-            ]
-        )
-    wide = [
-        item.transpose(1, 0, 2).reshape(item.shape[1], 2 * item.shape[2]) for item in terms
-    ]
-    tall = [lax.psum_scatter(item, "dp", scatter_dimension=0, tiled=True) for item in wide]
     return [
         lax.psum_scatter(item, "fsdp", scatter_dimension=1, tiled=True).astype(jnp.float32)
         for item in tall
     ]
-
-
-def halves(matrix):
-    return matrix.reshape(matrix.shape[0], 2, matrix.shape[1] // 2).transpose(1, 0, 2)
-
-
-def joined(stack):
-    return stack.transpose(1, 0, 2).reshape(stack.shape[1], 2 * stack.shape[2])
 
 
 def local_scores(queries, keys_all):
@@ -988,7 +1433,6 @@
 ):
     positions = lax.broadcasted_iota(jnp.int32, (tokens.shape[1], 1), 0)
     validity = (positions < lengths[0]).astype(jnp.float32)
-    layer_in = tokens[0].astype(jnp.float32) * validity
     shards_of = [
         local_project,
         local_output,
@@ -1000,53 +1444,17 @@
         linear_shrink,
     ]
     if direct:
-        held, tall, result, between, middles, gates, stages, kept = run_forward(
-            shards_of, tokens[0], validity
-        )
-        whole = []
-        saved = []
-        for layer in range(2):
-            mats = held.reshape(2, LAYER_CHUNKS, 2, 1024, WIDTH)[layer]
-            project = mats[:8].reshape(4, 2, 2, 1024, WIDTH).transpose(3, 2, 1, 0, 4)
-            output = mats[8:10].transpose(2, 1, 0, 3)
-            expand = mats[10:].transpose(2, 1, 0, 3)
-            whole += [
-                project.reshape(1024, 4096),
-                output.reshape(1024, 1024),
-                expand.reshape(1024, 5632),
-                joined(tall[layer].reshape(2, 2816, 512)),
-            ]
-            source = (layer_in, between)[layer]
-            five = stages[layer].transpose(1, 2, 0, 3).reshape(5, ROWS, 1024).astype(jnp.float32)
-            projected = jnp.concatenate([five[0], five[1], five[2], five[3]], axis=1)
-            projected = jnp.concatenate([five[0], five[1], five[2], five[3]], axis=1)
-            queries, keys_all = five[0], five[1]
-            logsum = None
-            if layer == 0:
-                scores = local_scores(queries, keys_all)[2]
-                logsum = jax.nn.logsumexp(scores, axis=-1, keepdims=True)
-            saved.append(
-                (
-                    source,
-                    simple_norm(source).astype(jnp.bfloat16),
-                    projected,
-                    five[2].astype(jnp.bfloat16),
-                    five[4],
-                    logsum,
-                    gates[layer],
-                    middles[layer],
-                    simple_norm(middles[layer]).astype(jnp.bfloat16),
-                )
-            )
-        local_weights, linear_weights = whole[:4], whole[4:]
-        local_saved, linear_saved = saved
-    else:
-        whole = [joined(item) for item in gather_weights(shards_of)]
-        local_weights = whole[:4]
-        linear_weights = whole[4:]
-        between, local_saved = forward_layer(layer_in, validity, local_weights, True)
-        result, linear_saved = forward_layer(between, validity, linear_weights, False)
-        result = (result * validity).astype(jnp.bfloat16)
+        forward = run_forward(shards_of, tokens[0], validity)
+        back_tokens, chunks, parts = run_backward(cotangent[0], tokens[0], validity, forward)
+        outs = unpack(forward[2], back_tokens, chunks, parts, shards_of)
+        return (outs[0][None], outs[1][None]) + tuple(outs[2:])
+    layer_in = tokens[0].astype(jnp.float32) * validity
+    whole = gather_weights(shards_of)
+    local_weights = whole[:4]
+    linear_weights = whole[4:]
+    between, local_saved = forward_layer(layer_in, validity, local_weights, True)
+    result, linear_saved = forward_layer(between, validity, linear_weights, False)
+    result = (result * validity).astype(jnp.bfloat16)
     upstream = cotangent[0].astype(jnp.float32) * validity
     back_between, linear_terms = backward_layer(
         upstream, linear_saved, linear_weights, validity, False
@@ -1054,9 +1462,7 @@
     back_input, local_terms = backward_layer(
         back_between, local_saved, local_weights, validity, True
     )
-    sums = settle_gradients(
-        [halves(item.astype(jnp.bfloat16)) for item in local_terms + linear_terms], direct
-    )
+    sums = settle_gradients(local_terms + linear_terms)
     return (
         result[None],
         (back_input * validity)[None],

time: 1100 us -> 599 us (0.54)
  local copies, waits for them, and re-layouts: 357 us -> 4.47 us
  matrix products: 201 us -> 0 us
  Pallas kernels: 452 us -> 592 us
  other arithmetic: 77.3 us -> 0.73 us
    dot_general x32 -> x0, matrix products: 201 us -> none  [the longest x8 63.1 us: contract_rows(): lax.dot_general(first_matrix, second_matrix, (((0,), (0,)), ((), ())), pr...]
    pallas_call x1 -> x2, Pallas kernels: 212 us -> 351 us  [the longest x1 348 us: run_backward(): pl.pallas_call(backward_kernel, out_shape=(struct((ROWS, 1024), WIDE), st...]
    reshape x20 -> x0, local copies, waits for them, and re-layouts: 117 us -> none  [the longest x8 56.4 us: halves(): matrix.reshape(matrix.shape[0], 2, matrix.shape[1] // 2).transpose(1, 0, 2)]
    slice x23 -> x0, local copies, waits for them, and re-layouts: 112 us -> none  [the longest x3 47.6 us: shards(): expand = mats[10:].transpose(2, 1, 0, 3)]
    convert_element_type x6 -> x0, other arithmetic: 33.2 us -> none  [the longest x1 12.4 us: shards(): stages[layer].transpose(1, 2, 0, 3).reshape(5, ROWS, 1024)]
    mul x16 -> x0, local copies, waits for them, and re-layouts: 26.7 us -> none  [the longest x8 8.4 us: norm_back(): values * (inverse_rms * inverse_rms)]
    another operation x4 -> x0, local copies, waits for them, and re-layouts: 20.6 us -> none  [the longest x2 16.7 us: shards(): tall[layer].reshape(2, 2816, 512)]
    convert_element_type x7 -> x0, local copies, waits for them, and re-layouts: 18.7 us -> none  [the longest x3 6.21 us: shards(): five[2].astype(jnp.bfloat16)]
where the time goes in v3:
time: 599 us; the launch traced here: 598 us
  Pallas kernels  592 us (99%)
    pallas_call x1, Pallas kernels, run_backward(): pl.pallas_call(backward_kernel, out_shape=(struct((ROWS, 1024), WIDE), st...  348 us
    pallas_call x1, Pallas kernels, run_forward(): pl.pallas_call(forward_kernel, out_shape=(struct((CHUNKS,) + bits + (64,...  241 us

profile of v3, /device:TPU:0, one launch (start us, length us, event | category | flops | bytes accessed | tf_op | source)
XLA Modules:
  0.0 598.2 jit_solution(874125010642766603)
XLA Ops:
  1.3 0.7 fusion.refs_9_.refs_2_
  2.0 240.6 %shard_map.186 = (bf16[42,2,2,2,2,2,64,256]{7,6,5,4,3,2,1,0:T(8,128)(2,1)}, bf16[2,2,2,2,2,2,176,512]{7,6,5,4,3,2,1,0:T(8,128)(2,1)}, bf16[512,1024]{1,0:T(8,128...) custom-call(bf16[64,2048]{1,0:T(8,128)(2,1)} %refs_0_.1, ...), custom_call_target="tpu_custom_call" | custom-call | tf_op jit(solution)/shard_map/pallas_call | solution.py:525
  242.7 0.0 copy-start.2
  242.7 347.9 %shard_map.187 = (f32[512,1024]{1,0:T(8,128)}, f32[42,64,256]{2,1,0:T(8,128)}, f32[8,176,128]{2,1,0:T(8,128)}) custom-call(bf16[512,1024]{1,0:T(8,128)(2,1)} %bitcast.12, bf16[512,1024]{1,0:T(8,128)(2,1)} %bitcast.11, f32[512,1]{1,0:T(8,128)} %fusion.refs_9_.refs_2_, bf16[42,2,1024,256]{3,2,1,0:T(8,128)(2,1)} %bitcast.8, bf16[2,2,2816,512]{3,2,1,0:T(8,128)(2,1)} %bitcast.9, ...), custom_call_target="tpu_custom_call" | custom-call | tf_op jit(solution)/shard_map/pallas_call | solution.py:1126
  590.5 0.0 copy-done.2
  590.5 0.0 copy-start
  590.5 1.8 copy-done
  592.3 0.0 copy-start.1
  592.3 1.6 copy-done.1
  593.9 0.0 copy-start.3
  593.9 1.1 copy-done.3
  595.0 3.2 shard_map.188
Async XLA Ops:
  242.7 347.9 %copy-start.2 = (bf16[512,1024]{1,0:T(8,128)(2,1)S(1)}, bf16[512,1024]{1,0:T(8,128)(2,1)}, u32[]{:S(2)}) copy-start(bf16[512,1024]{1,0:T(8,128)(2,1)} %get-tuple-element.31.mixed_in) | copy-start | bytes 3145732
  590.5 1.8 copy-start
  592.3 1.6 copy-start.1
  593.9 1.1 copy-start.3

commit v4 on v3

--- a/solution.py
+++ b/solution.py
@@ -155,7 +155,7 @@
     lax.fori_loop(0, ROWS // 128, body, 0)
 
 
-def local_mixer(group, parts, validity, gated, stage):
+def local_mixer(group, parts, validity, gated, stage, attends):
     def body(turn, carry):
         t = turn // 2
         rows = pl.ds(pl.multiple_of(t * 128, 128), 128)
@@ -174,8 +174,9 @@
             scores = jnp.where(keep, scores, -1e30)
             highest_score = jnp.max(scores, axis=-1, keepdims=True)
             weights = jnp.exp(scores - highest_score)
-            attend = weights / jnp.sum(weights, axis=-1, keepdims=True)
-            mixed.append(dot(attend.astype(LOW), v))
+            attend = (weights / jnp.sum(weights, axis=-1, keepdims=True)).astype(LOW)
+            attends[turn, head] = attend
+            mixed.append(dot(attend, v))
         mixture = jnp.where(first, mixed[0], mixed[1]) * validity[rows, :]
         scale = lax.rsqrt(pair_mean(mixture * mixture, first) + epsilon)
         columns = pl.ds(pl.multiple_of(group * WIDTH + pair * 128, 128), 128)
@@ -351,10 +352,12 @@
 def forward_kernel(*refs):
     own = refs[:WEIGHTS]
     tokens, validity = refs[WEIGHTS : WEIGHTS + 2]
-    held, tall, mixed_out, between, middles, gates, stages, halves_out = refs[10:18]
-    scratch = refs[18:]
-    sems, (load_sem, tall_sem, stage_sem, half_sem, misc_sem) = scratch[:5], scratch[5:10]
-    loaded, shrink, x, middle, normed, gated, hidden, parts, stage, half_stage, final = scratch[10:]
+    held, tall, mixed_out, between, middles, turns, stages, halves_out = refs[10:18]
+    hidden_out, attends_out = refs[18:20]
+    scratch = refs[20:]
+    sems, (load_sem, tall_sem, stage_sem, half_sem, hidden_sem, misc_sem) = scratch[:5], scratch[5:11]
+    loaded, shrink, x, middle, normed, gated, hidden, parts, stage, half_stage, final = scratch[11:22]
+    turned, hidden_stage, attends = scratch[22:]
     gather = Gather(own, held, tall, sems)
     gather.begin()
 
@@ -366,8 +369,21 @@
         x[rows, :] = tokens[rows, :].astype(WIDE) * validity[rows, :]
         return carry
 
+    def keep_turned(layer, kind):
+        return pltpu.make_async_copy(turned, turns.at[layer, kind], misc_sem.at[0])
+
+    def turn(source, layer, kind):
+        def act(t, carry):
+            rows = rows_of(t)
+            turned[:, rows] = source[rows, :].T
+            return carry
+
+        lax.fori_loop(0, ROWS // 128, act, 0)
+        keep_turned(layer, kind).start()
+
     lax.fori_loop(0, ROWS // 128, start_rows, 0)
     norm_into(x, normed)
+    turn(normed, 0, 0)
 
     def load(chunk):
         return pltpu.make_async_copy(
@@ -385,9 +401,17 @@
             half_stage.at[part % 2], halves_out.at[layer, part], half_sem.at[part % 2]
         )
 
-    def keep(kind, layer):
-        source, target = ((gated, gates), (middle, middles))[kind]
-        return pltpu.make_async_copy(source, target.at[layer], misc_sem.at[kind])
+    def keep_hidden(layer, part):
+        rows = pl.ds(pl.multiple_of(part * WIDTH, WIDTH), WIDTH)
+        return pltpu.make_async_copy(
+            hidden_stage.at[part % 2], hidden_out.at[layer, rows, :], hidden_sem.at[part % 2]
+        )
+
+    def keep_attends(group):
+        return pltpu.make_async_copy(attends, attends_out.at[group], misc_sem.at[4])
+
+    def keep_middle(layer):
+        return pltpu.make_async_copy(middle, middles.at[layer], misc_sem.at[1])
 
     def keep_between():
         return pltpu.make_async_copy(x, between, misc_sem.at[2])
@@ -406,24 +430,30 @@
             def _():
                 keep_stage(layer, group).wait()
 
-            @pl.when((layer > 0) & (group == 0))
+            @pl.when((layer == 0) & (group > 0))
             def _():
-                keep(0, 0).wait()
+                keep_attends(0).wait()
 
             for kind in range(4):
                 stage[kind] = parts[kind % 2, kind // 2].astype(LOW)
-            pl.when(layer == 0)(lambda: local_mixer(group, parts, validity, gated, stage))
+
+            @pl.when(layer == 0)
+            def _():
+                local_mixer(group, parts, validity, gated, stage, attends)
+                keep_attends(group).start()
+
             pl.when(layer > 0)(lambda: linear_mixer(group, parts, gated, stage))
             keep_stage(layer, group).start()
 
     def output_step(layer, part, slot):
         @pl.when(part == 0)
         def _():
-            keep(0, layer).start()
+            keep_turned(0, 0).wait()
+            turn(gated, layer, 1)
 
             @pl.when(layer > 0)
             def _():
-                keep(1, 0).wait()
+                keep_middle(0).wait()
 
         for f in range(2):
             lanes = pl.ds(pl.multiple_of(f * 512 + part * WIDTH, WIDTH), WIDTH)
@@ -431,20 +461,26 @@
 
         @pl.when(part == OUTPUT_CHUNKS - 1)
         def _():
-            keep(1, layer).start()
+            keep_middle(layer).start()
             norm_into(middle, normed)
+            keep_turned(0, 0).wait()
+            turn(normed, layer, 2)
 
     def expand_step(layer, part, slot):
         @pl.when((layer > 0) | (part > 1))
         def _():
             keep_half(layer, part).wait()
+            keep_hidden(layer, part).wait()
 
         first = dot(normed[...], weight(slot, 0))
         second = dot(normed[...], weight(slot, 1))
         half_stage[part % 2, 0] = first.astype(LOW)
         half_stage[part % 2, 1] = second.astype(LOW)
-        hidden[:, pl.ds(pl.multiple_of(part * WIDTH, WIDTH), WIDTH)] = (first * second).astype(LOW)
+        both = (first * second).astype(LOW)
+        hidden[:, pl.ds(pl.multiple_of(part * WIDTH, WIDTH), WIDTH)] = both
+        hidden_stage[part % 2] = both.T
         keep_half(layer, part).start()
+        keep_hidden(layer, part).start()
 
     def shrink_step(layer):
         load_tall(layer).wait()
@@ -467,6 +503,8 @@
         def _():
             keep_between().start()
             norm_into(x, normed)
+            keep_turned(0, 0).wait()
+            turn(normed, 1, 0)
 
         @pl.when(layer > 0)
         def _():
@@ -512,10 +550,13 @@
     last = pltpu.make_async_copy(final, mixed_out, misc_sem.at[3])
     last.start()
     keep_stage(1, HEAD_GROUPS - 1).wait()
-    keep(0, 1).wait()
-    keep(1, 1).wait()
+    keep_attends(0).wait()
+    keep_turned(0, 0).wait()
+    keep_middle(1).wait()
     keep_half(1, EXPAND_CHUNKS - 2).wait()
     keep_half(1, EXPAND_CHUNKS - 1).wait()
+    keep_hidden(1, EXPAND_CHUNKS - 2).wait()
+    keep_hidden(1, EXPAND_CHUNKS - 1).wait()
     last.wait()
 
 
@@ -530,12 +571,14 @@
             struct((ROWS, 1024), LOW),
             struct((ROWS, 1024), WIDE),
             struct((2, ROWS, 1024), WIDE),
-            struct((2, ROWS, 1024), LOW),
+            struct((2, 3, 1024, ROWS), LOW),
             struct((2, HEAD_GROUPS, 5, ROWS, WIDTH), LOW),
             struct((2, EXPAND_CHUNKS, 2, ROWS, WIDTH), LOW),
+            struct((2, 2816, ROWS), LOW),
+            struct((HEAD_GROUPS, 8, 2, 128, 128), LOW),
         ),
-        in_specs=[ANY] * WEIGHTS + [FULL, FULL],
-        out_specs=(ANY,) * 8,
+        in_specs=[FULL] * (WEIGHTS + 2),
+        out_specs=(ANY,) * 10,
         scratch_shapes=[
             pltpu.SemaphoreType.DMA((CHUNKS + 2,)),
             pltpu.SemaphoreType.DMA((10, GATHER_SLOTS)),
@@ -546,7 +589,8 @@
             pltpu.SemaphoreType.DMA,
             pltpu.SemaphoreType.DMA,
             pltpu.SemaphoreType.DMA((2,)),
-            pltpu.SemaphoreType.DMA((4,)),
+            pltpu.SemaphoreType.DMA((2,)),
+            pltpu.SemaphoreType.DMA((5,)),
             pltpu.VMEM((LOAD_SLOTS,) + bits + (64, WIDTH), LOW),
             pltpu.VMEM(bits + (176, 512), LOW),
             pltpu.VMEM((ROWS, 1024), WIDE),
@@ -558,6 +602,9 @@
             pltpu.VMEM((5, ROWS, WIDTH), LOW),
             pltpu.VMEM((2, 2, ROWS, WIDTH), LOW),
             pltpu.VMEM((ROWS, 1024), LOW),
+            pltpu.VMEM((1024, ROWS), LOW),
+            pltpu.VMEM((2, WIDTH, ROWS), LOW),
+            pltpu.VMEM((8, 2, 128, 128), LOW),
         ],
         compiler_params=pltpu.CompilerParams(
             collective_id=0, has_side_effects=True, vmem_limit_bytes=60 << 20
@@ -568,8 +615,7 @@
 SCATTER_LAG = 3
 SCATTER_SLOTS = 3 * SCATTER_LAG + 1
 TERM_SLOTS = SCATTER_LAG
-TALL_SLOTS = 6
-TALL_TERM_SLOTS = 2
+TALL_SLOTS = 3
 OUTPUT_TURN = EXPAND_CHUNKS
 PROJECT_TURN = EXPAND_CHUNKS + OUTPUT_CHUNKS
 TALL_ROWS = 176
@@ -586,9 +632,8 @@
 
     def tall_turn(self, chunk):
         layer = chunk // LAYER_CHUNKS
-        turn = chunk % LAYER_CHUNKS - OUTPUT_TURN
-        due = (turn >= 0) & (turn < 2 * SHRINK_PARTS) & (turn % 2 == 0)
-        return layer * SHRINK_PARTS + turn // 2, turn // 2, due
+        turn = chunk % LAYER_CHUNKS
+        return layer * SHRINK_PARTS + turn // 5, turn // 5, turn % 5 == 4
 
     def wide_parts(self):
         half = WIDTH // 2
@@ -635,34 +680,26 @@
         return out
 
     def add(self, buffers, slots, phase, parts, result):
+        if phase == 0 and len(parts) == 2:
+            parts = ((pl.ds(0, WIDTH), parts[0][1]),)
         for lanes, order in parts:
             source, dims = self.source(buffers, slots, phase, order)
             cut = AXIS_OF[order[phase]]
-            kept = self.left(order, phase)
+            near = tuple(self.places[d] if d == cut else slice(None) for d in dims)
+            whole = tuple(slice(None) for _ in self.left(order, phase))
             ref = buffers[1 + phase].at[slots[1]]
-
-            def body(unit, carry):
-                index = tuple((unit // 2 ** (len(kept) - 1 - b)) % 2 for b in range(len(kept)))
-                where = dict(zip(kept, index))
-                where[cut] = self.places[cut]
-                mine = source[tuple(where[d] for d in dims) + (slice(None), lanes)]
-                came = ref[index + (slice(None), lanes)]
-                if phase < 4:
-                    ref[index + (slice(None), lanes)] = came + mine
-                else:
-                    result[:, lanes] = came.astype(WIDE) + mine.astype(WIDE)
-                return carry
-
-            if kept:
-                lax.fori_loop(0, 2 ** len(kept), body, 0)
+            mine = source[near + (slice(None), lanes)]
+            came = ref[whole + (slice(None), lanes)]
+            if phase < 4:
+                ref[whole + (slice(None), lanes)] = came + mine
             else:
-                body(0, 0)
+                result[:, lanes] = came.astype(WIDE) + mine.astype(WIDE)
 
     def wide_slots(self, chunk):
         return (chunk % TERM_SLOTS, chunk % SCATTER_SLOTS)
 
     def tall_slots(self, place):
-        return (place % TALL_TERM_SLOTS, place % TALL_SLOTS)
+        return (0, place % TALL_SLOTS)
 
     def wide_messages(self, phase, chunk):
         return self.messages(
@@ -763,27 +800,28 @@
     return back_update, back_mixture
 
 
-def local_mixer_back(group, stage, validity, coming, back):
+def local_mixer_back(group, stage, attends, validity, coming, back):
     def body(turn, carry):
         rows = pl.ds(pl.multiple_of((turn // 2) * 128, 128), 128)
         lanes = pl.ds(pl.multiple_of((turn % 2) * 128, 128), 128)
         columns = pl.ds(pl.multiple_of(group * WIDTH + (turn % 2) * 128, 128), 128)
         first = first_lanes(128)
+
+        def put(i, j, value):
+            start = j * WIDTH + (turn % 2) * 128
+            back[i, rows, pl.ds(pl.multiple_of(start, 128), 128)] = value.astype(LOW)
+
         q, k, v = stage[0, rows, lanes], stage[1, rows, lanes], stage[2, rows, lanes]
         update = stage[3, rows, lanes].astype(WIDE)
         mixture = stage[4, rows, lanes].astype(WIDE)
         back_update, back_mixture = gate_back(update, mixture, coming[rows, columns], first)
-        back[1, 1, rows, lanes] = back_update.astype(LOW)
+        put(1, 1, back_update)
         grad = (back_mixture.astype(LOW).astype(WIDE) * validity[rows, :]).astype(LOW)
-        keep = block_mask(128)
         zero = jnp.zeros_like(q)
         out = []
         for head in range(2):
             here = first == (head == 0)
-            scores = contract_cols(jnp.where(here, q, zero), k) * HEAD ** (-0.5)
-            scores = jnp.where(keep, scores, -1e30)
-            weights = jnp.exp(scores - jnp.max(scores, axis=-1, keepdims=True))
-            attend = weights / jnp.sum(weights, axis=-1, keepdims=True)
+            attend = attends[turn, head].astype(WIDE)
             back_attend = contract_cols(jnp.where(here, grad, zero), v)
             total = jnp.sum(back_attend * attend, axis=-1, keepdims=True)
             back_scores = (attend * (back_attend - total)).astype(LOW)
@@ -791,14 +829,14 @@
                 (
                     dot(back_scores, k) * HEAD ** (-0.5),
                     contract_rows(back_scores, q) * HEAD ** (-0.5),
-                    contract_rows(attend.astype(LOW), grad),
+                    contract_rows(attends[turn, head], grad),
                 )
             )
         for kind, (i, j) in enumerate(((0, 0), (1, 0), (0, 1))):
-            back[i, j, rows, lanes] = jnp.where(first, out[0][kind], out[1][kind]).astype(LOW)
+            put(i, j, jnp.where(first, out[0][kind], out[1][kind]))
         return carry
 
-    lax.fori_loop(0, 2 * ROWS // 128, body, 0)
+    lax.fori_loop(0, 2 * ROWS // 128, body, 0, unroll=4)
 
 
 def linear_mixer_back(group, stage, coming, back):
@@ -816,7 +854,12 @@
         update = stage[3, :, lanes].astype(WIDE)
         mixture = stage[4, :, lanes].astype(WIDE)
         back_update, back_mixture = gate_back(update, mixture, coming[:, columns], first)
-        back[1, 1, :, lanes] = back_update.astype(LOW)
+
+        def put(i, j, rows, value):
+            start = j * WIDTH + pair * 128
+            back[i, rows, pl.ds(pl.multiple_of(start, 128), 128)] = value.astype(LOW)
+
+        put(1, 1, slice(None), back_update)
         grad = back_mixture.astype(LOW)
         zero = jnp.zeros((half, 128), LOW)
         tiles = []
@@ -848,9 +891,9 @@
             if t == 0:
                 back_k = back_k + tiles[0][1]
                 back_v = back_v + tiles[0][2]
-            back[0, 0, rows, lanes] = (back_q * logistic(queries[span])).astype(LOW)
-            back[1, 0, rows, lanes] = (back_k * logistic(keys_all[span])).astype(LOW)
-            back[0, 1, rows, lanes] = back_v.astype(LOW)
+            put(0, 0, rows, back_q * logistic(queries[span]))
+            put(1, 0, rows, back_k * logistic(keys_all[span]))
+            put(0, 1, rows, back_v)
         return carry
 
     lax.fori_loop(0, 2, body, 0)
@@ -866,16 +909,17 @@
 
 def backward_kernel(*refs):
     cotangent, tokens, validity = refs[:3]
-    held, tall, between, middles, gates, stages, halves_in = refs[3:10]
-    tokens_out, outs, tall_outs = refs[10:13]
-    scratch = refs[13:]
-    scatter_sems, loads = scratch[:6], scratch[6:10]
-    load_sem, half_sem, stage_sem, misc_sem = loads
-    wide_buffers, tall_buffers = scratch[10:17], scratch[17:24]
+    held, tall, between, middles, turns, stages, halves_in, hidden_in, attends_in = refs[3:12]
+    tokens_out, outs, tall_outs = refs[12:15]
+    scratch = refs[15:]
+    scatter_sems, loads = scratch[:6], scratch[6:12]
+    load_sem, half_sem, shrink_sem, stage_sem, turn_sem, misc_sem = loads
+    wide_buffers, tall_buffers = scratch[12:19], scratch[19:26]
     (
         loaded,
         half_in,
         stage,
+        attends,
         shrink,
         hidden_turned,
         branch,
@@ -884,30 +928,57 @@
         sums,
         middle,
         layer_in,
-        gated,
         turned,
         back,
-    ) = scratch[24:]
+    ) = scratch[26:]
     scatter = Scatter((outs, tall_outs), scatter_sems, wide_buffers, tall_buffers)
 
-    def load(chunk, number):
+    class Load:
+        def __init__(self, chunk, number):
+            self.copies = [
+                pltpu.make_async_copy(
+                    held.at[chunk, f],
+                    loaded.at[number % 2, :, pl.ds(f * WIDTH, WIDTH)],
+                    load_sem.at[number % 2, f],
+                )
+                for f in range(2)
+            ]
+
+        def start(self):
+            for copy in self.copies:
+                copy.start()
+
+        def wait(self):
+            for copy in self.copies:
+                copy.wait()
+
+    def load_turned(layer, kind, order):
         return pltpu.make_async_copy(
-            held.at[chunk], loaded.at[number % 2], load_sem.at[number % 2]
+            turns.at[layer, kind], turned.at[order % 2], turn_sem.at[order % 2]
         )
+
+    def load_attends(group):
+        return pltpu.make_async_copy(attends_in.at[group], attends, misc_sem.at[4])
 
     def load_half(layer, part, number):
         return pltpu.make_async_copy(
             halves_in.at[layer, part], half_in.at[number % 2], half_sem.at[number % 2]
         )
 
+    def load_shrink(layer, part, number):
+        rows = pl.ds(pl.multiple_of(part * WIDTH, WIDTH), WIDTH)
+        return pltpu.make_async_copy(
+            tall.at[layer, :, rows, :], shrink.at[number % 2], shrink_sem.at[number % 2]
+        )
+
     def load_stage(layer, group):
         return pltpu.make_async_copy(stages.at[layer, group], stage, stage_sem)
 
     def fetch(kind, layer):
         source, target = (
-            (tall, shrink),
+            (None, None),
             (middles, middle),
-            (gates, gated),
+            (hidden_in, hidden_turned),
         )[kind]
         return pltpu.make_async_copy(source.at[layer], target, misc_sem.at[kind])
 
@@ -921,24 +992,28 @@
 
         @pl.when(turn < OUTPUT_TURN)
         def _():
-            load(base + PROJECT_CHUNKS + OUTPUT_CHUNKS + turn, number).start()
+            Load(base + PROJECT_CHUNKS + OUTPUT_CHUNKS + turn, number).start()
             load_half(layer, turn, number).start()
+            load_shrink(layer, turn, number).start()
 
         @pl.when((turn >= OUTPUT_TURN) & (turn < PROJECT_TURN))
         def _():
-            load(base + PROJECT_CHUNKS + turn - OUTPUT_TURN, number).start()
+            Load(base + PROJECT_CHUNKS + turn - OUTPUT_TURN, number).start()
 
         @pl.when(turn >= PROJECT_TURN)
         def _():
-            load(base + turn - PROJECT_TURN, number).start()
+            Load(base + turn - PROJECT_TURN, number).start()
 
             @pl.when((turn - PROJECT_TURN) % 2 == 0)
             def _():
                 load_stage(layer, (turn - PROJECT_TURN) // 2).start()
+                pl.when(layer == 0)(lambda: load_attends((turn - PROJECT_TURN) // 2).start())
 
     prefetch(jnp.int32(0))
-    for kind in range(3):
-        fetch(kind, 1).start()
+    load_turned(1, 2, 0).start()
+    load_turned(1, 1, 1).start()
+    fetch(2, 1).start()
+    fetch(1, 1).start()
     fetch_between().start()
 
     def begin_rows(rows):
@@ -947,36 +1022,30 @@
     over_rows(begin_rows)
     greet(scatter.targets)
 
-    def turn_norm(source):
-        def act(rows):
-            turned[:, rows] = simple_norm(source[rows, :]).astype(LOW).T
-
-        over_rows(act)
-
     def expand_start(layer):
-        fetch(0, 1).wait()
-        fetch(1, 1).wait()
-
         def act(rows):
             branch[rows, :] = up[rows, :].astype(LOW)
             sums[0, rows, :] = jnp.zeros((128, 1024), WIDE)
 
         over_rows(act)
-        turn_norm(middle)
+        load_turned(0, 0, 1 - layer).wait()
+        pl.when(layer == 0)(lambda: load_turned(0, 1, 4).start())
 
     def expand_turn(part, number):
         load_half(0, 0, number).wait()
-        rows = pl.ds(pl.multiple_of(part * WIDTH, WIDTH), WIDTH)
-        back_hidden = contract_cols(branch[:, :512], shrink[0, rows, :])
-        back_hidden = back_hidden + contract_cols(branch[:, 512:], shrink[1, rows, :])
+        load_shrink(0, 0, number).wait()
+        low, high = pl.ds(0, WIDTH), pl.ds(WIDTH, WIDTH)
+        back_hidden = contract_cols(branch[:, :512], shrink[number % 2, 0])
+        back_hidden = back_hidden + contract_cols(branch[:, 512:], shrink[number % 2, 1])
         first = half_in[number % 2, 0].astype(WIDE)
         second = half_in[number % 2, 1].astype(WIDE)
-        back[0, 0] = (back_hidden * second).astype(LOW)
-        back[0, 1] = (back_hidden * first).astype(LOW)
-        hidden_turned[rows, :] = (first * second).astype(LOW).T
+        back[0, :, low] = (back_hidden * second).astype(LOW)
+        back[0, :, high] = (back_hidden * first).astype(LOW)
 
     def output_start(layer):
-        fetch(2, 1).wait()
+        load_turned(0, 0, 2 - layer).wait()
+        load_turned(layer, 0, 3 - layer).start()
+        fetch(1, 1).wait()
 
         def act(rows):
             values = middle[rows, :]
@@ -985,25 +1054,20 @@
             up[rows, :] = new
             gated_branch[rows, :] = new.astype(LOW)
             sums[1, rows, :] = jnp.zeros((128, 1024), WIDE)
-            turned[:, rows] = gated[rows, :].T
 
         over_rows(act)
-
-        @pl.when(layer == 1)
-        def _():
-            fetch(0, 0).start()
 
     def output_turn(part):
         for f in range(2):
             lanes = pl.ds(pl.multiple_of(f * 512 + part * WIDTH, WIDTH), WIDTH)
-            back[0, f] = gated_branch[:, lanes]
+            back[0, :, pl.ds(f * WIDTH, WIDTH)] = gated_branch[:, lanes]
 
     def project_start(layer):
         @pl.when(layer == 1)
         def _():
             fetch_between().wait()
             fetch(1, 0).start()
-            fetch(2, 0).start()
+            load_turned(0, 2, 3).start()
 
         @pl.when(layer == 0)
         def _():
@@ -1016,13 +1080,17 @@
             sums[0, rows, :] = jnp.zeros((128, 1024), WIDE)
 
         over_rows(clear)
-        turn_norm(layer_in)
+        load_turned(0, 0, 1 - layer).wait()
 
     def project_turn(layer, group):
         load_stage(0, 0).wait()
         coming = sums.at[1]
         pl.when(layer == 1)(lambda: linear_mixer_back(group, stage, coming, back))
-        pl.when(layer == 0)(lambda: local_mixer_back(group, stage, validity, coming, back))
+
+        @pl.when(layer == 0)
+        def _():
+            load_attends(0).wait()
+            local_mixer_back(group, stage, attends, validity, coming, back)
 
     def finish_layer(layer):
         def act(rows):
@@ -1030,39 +1098,46 @@
 
         over_rows(act)
 
-    def terms(number, which):
+    def terms(number, which, order):
         slot = number % TERM_SLOTS
         out = wide_buffers[0]
 
         def body(tile, carry):
-            f = tile // 4
-            rows = pl.ds(pl.multiple_of((tile % 4) * 256, 256), 256)
-            value = dot(turned[rows, :], back[which, f]).astype(LOW)
-            out[slot, f, (tile % 4) // 2, tile % 2] = value.reshape(2, 2, 64, WIDTH)
+            rows = pl.ds(pl.multiple_of(tile * 512, 512), 512)
+            value = dot(turned[order % 2, rows, :], back[which]).astype(LOW)
+            for f in range(2):
+                part = value[:, f * WIDTH : (f + 1) * WIDTH]
+                out[slot, f, tile] = part.reshape(2, 2, 2, 64, WIDTH)
             return carry
 
-        lax.fori_loop(0, 8, body, 0)
-
-    def tall_terms(place, part):
-        slot = place % TALL_TERM_SLOTS
+        lax.fori_loop(0, 2, body, 0)
+
+    def tall_terms(part, number):
         out = tall_buffers[0]
+        pl.when(part == 0)(lambda: fetch(2, 0).wait())
+        lanes = [pl.ds(pl.multiple_of(f * 512 + part * 128, 128), 128) for f in range(2)]
+        both = jnp.concatenate([branch[:, lanes[0]], branch[:, lanes[1]]], axis=1)
 
         def body(tile, carry):
-            f = tile // 4
-            rows = pl.ds(pl.multiple_of((tile % 4) * 4 * TALL_ROWS, 4 * TALL_ROWS), 4 * TALL_ROWS)
-            lanes = pl.ds(pl.multiple_of(f * 512 + part * SHRINK_WIDTH, 128), SHRINK_WIDTH)
-            value = dot(hidden_turned[rows, :], branch[:, lanes]).astype(LOW)
-            out[slot, f, (tile % 4) // 2, tile % 2] = value.reshape(2, 2, TALL_ROWS, SHRINK_WIDTH)
+            rows = pl.ds(pl.multiple_of(tile * 8 * TALL_ROWS, 8 * TALL_ROWS), 8 * TALL_ROWS)
+            value = dot(hidden_turned[rows, :], both).astype(LOW)
+            for f in range(2):
+                out[0, f, tile] = value[:, f * 128 : f * 128 + 128].reshape(
+                    2, 2, 2, TALL_ROWS, SHRINK_WIDTH
+                )
             return carry
 
-        lax.fori_loop(0, 8, body, 0)
+        lax.fori_loop(0, 2, body, 0)
+
+        @pl.when((part == SHRINK_PARTS - 1) & (number < LAYER_CHUNKS))
+        def _():
+            fetch(2, 0).start()
 
     def spread(number, which, kind):
         def body(t, carry):
-            rows = pl.ds(pl.multiple_of(t * 256, 256), 256)
-            value = contract_cols(back[which, 0, rows, :], loaded[number % 2, 0])
-            value = value + contract_cols(back[which, 1, rows, :], loaded[number % 2, 1])
-            sums[kind, rows, :] = sums[kind, rows, :] + value
+            rows = pl.ds(pl.multiple_of(t * 512, 512), 512)
+            value = contract_cols(back[which], loaded[number % 2, rows, :])
+            sums[kind, :, rows] = sums[kind, :, rows] + value
             return carry
 
         lax.fori_loop(0, 2, body, 0)
@@ -1088,11 +1163,11 @@
             in_project = jnp.minimum(jnp.maximum(turn - PROJECT_TURN + 1, 0), 1)
             in_output = jnp.minimum(jnp.maximum(turn - OUTPUT_TURN + 1, 0), 1) - in_project
             which = in_project * ((turn + PROJECT_TURN) % 2)
-            terms(step, which)
+            terms(step, which, 1 - layer + in_output)
             place, part, due = scatter.tall_turn(step)
-            pl.when(due)(lambda: tall_terms(place, part))
+            pl.when(due)(lambda: tall_terms(part, step))
             scatter.start(0, step)
-            load(0, step).wait()
+            Load(0, step).wait()
             spread(step, which, in_output)
             pl.when(turn == LAYER_CHUNKS - 1)(lambda: finish_layer(layer))
 
@@ -1122,7 +1197,7 @@
 
 def run_backward(cotangent, tokens, validity, forward):
     struct = jax.ShapeDtypeStruct
-    held, tall, mixed_out, between, middles, gates, stages, kept = forward
+    held, tall, mixed_out, between, middles, turns, stages, kept, hidden, attends = forward
     return pl.pallas_call(
         backward_kernel,
         out_shape=(
@@ -1130,7 +1205,7 @@
             struct((CHUNKS, 64, WIDTH), WIDE),
             struct((2 * SHRINK_PARTS, TALL_ROWS, SHRINK_WIDTH), WIDE),
         ),
-        in_specs=[FULL] * 3 + [ANY] * 7,
+        in_specs=[FULL] * 3 + [ANY] * 9,
         out_specs=(ANY,) * 3,
         scratch_shapes=[
             pltpu.SemaphoreType.DMA((10, SCATTER_SLOTS)),
@@ -1139,18 +1214,21 @@
             pltpu.SemaphoreType.DMA((10, TALL_SLOTS)),
             pltpu.SemaphoreType.DMA((2,)),
             pltpu.SemaphoreType.DMA((2,)),
+            pltpu.SemaphoreType.DMA((2, 2)),
             pltpu.SemaphoreType.DMA((2,)),
             pltpu.SemaphoreType.DMA((2,)),
             pltpu.SemaphoreType.DMA,
-            pltpu.SemaphoreType.DMA((4,)),
+            pltpu.SemaphoreType.DMA((2,)),
+            pltpu.SemaphoreType.DMA((5,)),
         ]
         + scatter_buffers(TERM_SLOTS, SCATTER_SLOTS, 64, WIDTH)
-        + scatter_buffers(TALL_TERM_SLOTS, TALL_SLOTS, TALL_ROWS, SHRINK_WIDTH)
+        + scatter_buffers(1, TALL_SLOTS, TALL_ROWS, SHRINK_WIDTH)
         + [
-            pltpu.VMEM((2, 2, 1024, WIDTH), LOW),
+            pltpu.VMEM((2, 1024, 2 * WIDTH), LOW),
             pltpu.VMEM((2, 2, ROWS, WIDTH), LOW),
             pltpu.VMEM((5, ROWS, WIDTH), LOW),
-            pltpu.VMEM((2, 2816, 512), LOW),
+            pltpu.VMEM((8, 2, 128, 128), LOW),
+            pltpu.VMEM((2, 2, WIDTH, 512), LOW),
             pltpu.VMEM((2816, ROWS), LOW),
             pltpu.VMEM((ROWS, 1024), LOW),
             pltpu.VMEM((ROWS, 1024), LOW),
@@ -1158,9 +1236,8 @@
             pltpu.VMEM((2, ROWS, 1024), WIDE),
             pltpu.VMEM((ROWS, 1024), WIDE),
             pltpu.VMEM((ROWS, 1024), WIDE),
-            pltpu.VMEM((ROWS, 1024), LOW),
-            pltpu.VMEM((1024, ROWS), LOW),
-            pltpu.VMEM((2, 2, ROWS, WIDTH), LOW),
+            pltpu.VMEM((2, 1024, ROWS), LOW),
+            pltpu.VMEM((2, ROWS, 2 * WIDTH), LOW),
         ],
         compiler_params=pltpu.CompilerParams(
             collective_id=1, has_side_effects=True, vmem_limit_bytes=62 << 20
@@ -1173,9 +1250,11 @@
         tall.reshape(2, 2, 2816, 512),
         between,
         middles,
-        gates,
+        turns,
         stages,
         kept,
+        hidden,
+        attends,
     )
 
 

time: 599 us -> 466 us (0.78)
  Pallas kernels: 592 us -> 459 us
    pallas_call x1, Pallas kernels: 348 us -> 229 us  [run_backward(): pl.pallas_call(backward_kernel, out_shape=(struct((ROWS, 1024), WIDE), st...]
    pallas_call x1, Pallas kernels: 241 us -> 227 us  [run_forward(): pl.pallas_call(forward_kernel, out_shape=(struct((CHUNKS,) + bits + (64,...]
where the time goes in v4:
time: 466 us
  Pallas kernels  459 us (98%)
    pallas_call x1, Pallas kernels, run_backward(): pl.pallas_call(backward_kernel, out_shape=(struct((ROWS, 1024), WIDE), st...  229 us
    pallas_call x1, Pallas kernels, run_forward(): pl.pallas_call(forward_kernel, out_shape=(struct((CHUNKS,) + bits + (64,...  227 us

profile of v4, /device:TPU:0, one launch (start us, length us, event | category | flops | bytes accessed | tf_op | source)
XLA Modules:
  0.0 466.0 jit_solution(4610798832486127905)
XLA Ops:
  1.3 0.7 fusion.refs_9_.refs_2_
  2.0 227.0 %shard_map.186 = (bf16[42,2,2,2,2,2,64,256]{7,6,5,4,3,2,1,0:T(8,128)(2,1)}, bf16[2,2,2,2,2,2,176,512]{7,6,5,4,3,2,1,0:T(8,128)(2,1)}, bf16[512,1024]{1,0:T(8,128...) custom-call(bf16[64,2048]{1,0:T(8,128)(2,1)} %refs_0_.1, ...), custom_call_target="tpu_custom_call" | custom-call | tf_op jit(solution)/shard_map/pallas_call | solution.py:566
  229.0 0.0 copy-start.2
  229.0 229.2 %shard_map.187 = (f32[512,1024]{1,0:T(8,128)}, f32[42,64,256]{2,1,0:T(8,128)}, f32[8,176,128]{2,1,0:T(8,128)}) custom-call(bf16[512,1024]{1,0:T(8,128)(2,1)} %bitcast.12, bf16[512,1024]{1,0:T(8,128)(2,1)} %bitcast.11, f32[512,1]{1,0:T(8,128)} %fusion.refs_9_.refs_2_, bf16[42,2,1024,256]{3,2,1,0:T(8,128)(2,1)} %bitcast.8, bf16[2,2,2816,512]{3,2,1,0:T(8,128)(2,1)} %bitcast.9, ...), custom_call_target="tpu_custom_call" | custom-call | tf_op jit(solution)/shard_map/pallas_call | solution.py:1201
  458.2 0.0 copy-done.2
  458.2 0.0 copy-start
  458.2 1.8 copy-done
  460.0 0.0 copy-start.1
  460.0 1.6 copy-done.1
  461.6 0.0 copy-start.3
  461.6 1.1 copy-done.3
  462.7 3.2 shard_map.188
Async XLA Ops:
  229.0 229.2 %copy-start.2 = (bf16[512,1024]{1,0:T(8,128)(2,1)S(1)}, bf16[512,1024]{1,0:T(8,128)(2,1)}, u32[]{:S(2)}) copy-start(bf16[512,1024]{1,0:T(8,128)(2,1)} %get-tuple-element.33.mixed_in) | copy-start | bytes 3145732
  458.2 1.8 copy-start
  460.0 1.6 copy-start.1
  461.6 1.1 copy-start.3

commit v5 on v4

--- a/solution.py
+++ b/solution.py
@@ -77,8 +77,8 @@
 FULL = pl.BlockSpec(memory_space=pltpu.VMEM)
 WEIGHTS = 8
 WIDTH = 256
-LAG = 3
 PHASES = 5
+GATHER_STEPS = (0, 3, 6, 9, 12, 15)
 HEAD_GROUPS = 4
 PROJECT_CHUNKS = 8
 OUTPUT_CHUNKS = 2
@@ -319,7 +319,7 @@
 
     def step(self, step):
         for phase in range(PHASES, -1, -1):
-            chunk = step - phase * LAG
+            chunk = step - GATHER_STEPS[phase]
 
             @pl.when((chunk >= 0) & (chunk < CHUNKS))
             def _(phase=phase, chunk=chunk):
@@ -517,7 +517,7 @@
 
     def body(step, carry):
         gather.step(step)
-        arrived = step - PHASES * LAG
+        arrived = step - GATHER_STEPS[PHASES]
 
         @pl.when((arrived >= 0) & (arrived < CHUNKS))
         def _():
@@ -546,7 +546,7 @@
 
         return carry
 
-    lax.fori_loop(0, CHUNKS + PHASES * LAG + 1, body, 0)
+    lax.fori_loop(0, CHUNKS + GATHER_STEPS[PHASES] + 1, body, 0)
     last = pltpu.make_async_copy(final, mixed_out, misc_sem.at[3])
     last.start()
     keep_stage(1, HEAD_GROUPS - 1).wait()
@@ -612,9 +612,9 @@
     )(*shards_of, tokens, validity)
 
 
-SCATTER_LAG = 3
-SCATTER_SLOTS = 3 * SCATTER_LAG + 1
-TERM_SLOTS = SCATTER_LAG
+SCATTER_STEPS = (0, 2, 5, 8, 11, 14)
+SCATTER_SLOTS = 10
+TERM_SLOTS = SCATTER_STEPS[1]
 TALL_SLOTS = 3
 OUTPUT_TURN = EXPAND_CHUNKS
 PROJECT_TURN = EXPAND_CHUNKS + OUTPUT_CHUNKS
@@ -772,7 +772,7 @@
 
     def older(self, step):
         for phase in range(PHASES, 0, -1):
-            chunk = step - phase * SCATTER_LAG
+            chunk = step - SCATTER_STEPS[phase]
 
             @pl.when((chunk >= 0) & (chunk < CHUNKS))
             def _(phase=phase, chunk=chunk):
@@ -800,6 +800,16 @@
     return back_update, back_mixture
 
 
+def both_heads(values, first):
+    zero = jnp.zeros_like(values)
+    return jnp.concatenate([jnp.where(first, values, zero), jnp.where(first, zero, values)], axis=0)
+
+
+def side_by_side(values):
+    half = values.shape[0] // 2
+    return jnp.concatenate([values[:half], values[half:]], axis=1)
+
+
 def local_mixer_back(group, stage, attends, validity, coming, back):
     def body(turn, carry):
         rows = pl.ds(pl.multiple_of((turn // 2) * 128, 128), 128)
@@ -817,23 +827,15 @@
         back_update, back_mixture = gate_back(update, mixture, coming[rows, columns], first)
         put(1, 1, back_update)
         grad = (back_mixture.astype(LOW).astype(WIDE) * validity[rows, :]).astype(LOW)
-        zero = jnp.zeros_like(q)
-        out = []
-        for head in range(2):
-            here = first == (head == 0)
-            attend = attends[turn, head].astype(WIDE)
-            back_attend = contract_cols(jnp.where(here, grad, zero), v)
-            total = jnp.sum(back_attend * attend, axis=-1, keepdims=True)
-            back_scores = (attend * (back_attend - total)).astype(LOW)
-            out.append(
-                (
-                    dot(back_scores, k) * HEAD ** (-0.5),
-                    contract_rows(back_scores, q) * HEAD ** (-0.5),
-                    contract_rows(attends[turn, head], grad),
-                )
-            )
-        for kind, (i, j) in enumerate(((0, 0), (1, 0), (0, 1))):
-            put(i, j, jnp.where(first, out[0][kind], out[1][kind]))
+        grads = both_heads(grad, first)
+        attend_low = attends[turn].reshape(256, 128)
+        attend = attend_low.astype(WIDE)
+        back_attend = contract_cols(grads, v)
+        total = jnp.sum(back_attend * attend, axis=-1, keepdims=True)
+        back_scores = (attend * (back_attend - total)).astype(LOW)
+        put(0, 0, dot(side_by_side(back_scores), both_heads(k, first)) * HEAD ** (-0.5))
+        put(1, 0, contract_rows(back_scores, both_heads(q, first)) * HEAD ** (-0.5))
+        put(0, 1, contract_rows(attend_low, grads))
         return carry
 
     lax.fori_loop(0, 2 * ROWS // 128, body, 0, unroll=4)
@@ -861,26 +863,21 @@
 
         put(1, 1, slice(None), back_update)
         grad = back_mixture.astype(LOW)
-        zero = jnp.zeros((half, 128), LOW)
         tiles = []
         for t in range(2):
             reach = (t + 1) * half
-            i = lax.broadcasted_iota(jnp.int32, (half, reach), 0) + t * half
-            j = lax.broadcasted_iota(jnp.int32, (half, reach), 1)
-            mine_q = fq[t * half : reach]
-            mine_g = grad[t * half : reach]
-            out = []
-            for head in range(2):
-                here = first[:half] == (head == 0)
-                scores = contract_cols(jnp.where(here, mine_q, zero), fk[:reach])
-                scores = jnp.where(j <= i, scores, 0.0).astype(LOW)
-                inner = contract_cols(jnp.where(here, mine_g, zero), v[:reach])
-                inner = jnp.where(j <= i, inner, 0.0).astype(LOW)
-                out.append(
-                    (dot(inner, fk[:reach]), contract_rows(inner, mine_q), contract_rows(scores, mine_g))
+            i = lax.broadcasted_iota(jnp.int32, (2 * half, reach), 0) % half + t * half
+            j = lax.broadcasted_iota(jnp.int32, (2 * half, reach), 1)
+            pair_q = both_heads(fq[t * half : reach], first[:half])
+            pair_g = both_heads(grad[t * half : reach], first[:half])
+            scores = jnp.where(j <= i, contract_cols(pair_q, fk[:reach]), 0.0).astype(LOW)
+            inner = jnp.where(j <= i, contract_cols(pair_g, v[:reach]), 0.0).astype(LOW)
+            tiles.append(
+                (
+                    dot(side_by_side(inner), both_heads(fk[:reach], first[:reach])),
+                    contract_rows(inner, pair_q),
+                    contract_rows(scores, pair_g),
                 )
-            tiles.append(
-                [jnp.where(first[: out[0][n].shape[0]], out[0][n], out[1][n]) for n in range(3)]
             )
         for t in range(2):
             rows = pl.ds(t * half, half)
@@ -1181,7 +1178,7 @@
 
         return carry
 
-    lax.fori_loop(0, CHUNKS + PHASES * SCATTER_LAG, body, 0)
+    lax.fori_loop(0, CHUNKS + SCATTER_STEPS[PHASES], body, 0)
     pltpu.make_async_copy(up, tokens_out, misc_sem.at[3]).wait()
     scatter.finish()
 

time: 466 us -> 456 us (0.979)
  Pallas kernels: 459 us -> 450 us
    pallas_call x1, Pallas kernels: 229 us -> 219 us  [run_backward(): pl.pallas_call(backward_kernel, out_shape=(struct((ROWS, 1024), WIDE), st...]
where the time goes in v5:
time: 456 us
  Pallas kernels  450 us (99%)
    pallas_call x1, Pallas kernels, run_forward(): pl.pallas_call(forward_kernel, out_shape=(struct((CHUNKS,) + bits + (64,...  227 us
    pallas_call x1, Pallas kernels, run_backward(): pl.pallas_call(backward_kernel, out_shape=(struct((ROWS, 1024), WIDE), st...  219 us

profile of v5, /device:TPU:0, one launch (start us, length us, event | category | flops | bytes accessed | tf_op | source)
XLA Modules:
  0.0 456.1 jit_solution(2376829907431686818)
XLA Ops:
  1.3 0.7 fusion.refs_9_.refs_2_
  2.0 227.0 %shard_map.186 = (bf16[42,2,2,2,2,2,64,256]{7,6,5,4,3,2,1,0:T(8,128)(2,1)}, bf16[2,2,2,2,2,2,176,512]{7,6,5,4,3,2,1,0:T(8,128)(2,1)}, bf16[512,1024]{1,0:T(8,128...) custom-call(bf16[64,2048]{1,0:T(8,128)(2,1)} %refs_0_.1, ...), custom_call_target="tpu_custom_call" | custom-call | tf_op jit(solution)/shard_map/pallas_call | solution.py:566
  229.0 0.0 copy-start.2
  229.0 219.4 %shard_map.187 = (f32[512,1024]{1,0:T(8,128)}, f32[42,64,256]{2,1,0:T(8,128)}, f32[8,176,128]{2,1,0:T(8,128)}) custom-call(bf16[512,1024]{1,0:T(8,128)(2,1)} %bitcast.12, bf16[512,1024]{1,0:T(8,128)(2,1)} %bitcast.11, f32[512,1]{1,0:T(8,128)} %fusion.refs_9_.refs_2_, bf16[42,2,1024,256]{3,2,1,0:T(8,128)(2,1)} %bitcast.8, bf16[2,2,2816,512]{3,2,1,0:T(8,128)(2,1)} %bitcast.9, ...), custom_call_target="tpu_custom_call" | custom-call | tf_op jit(solution)/shard_map/pallas_call | solution.py:1198
  448.4 0.0 copy-done.2
  448.4 0.0 copy-start
  448.4 1.8 copy-done
  450.2 0.0 copy-start.1
  450.2 1.6 copy-done.1
  451.8 0.0 copy-start.3
  451.8 1.1 copy-done.3
  452.9 3.2 shard_map.188
Async XLA Ops:
  229.0 219.4 %copy-start.2 = (bf16[512,1024]{1,0:T(8,128)(2,1)S(1)}, bf16[512,1024]{1,0:T(8,128)(2,1)}, u32[]{:S(2)}) copy-start(bf16[512,1024]{1,0:T(8,128)(2,1)} %get-tuple-element.33.mixed_in) | copy-start | bytes 3145732
  448.4 1.8 copy-start
  450.2 1.6 copy-start.1
  451.8 1.1 copy-start.3

commit v6 on v5

--- a/solution.py
+++ b/solution.py
@@ -983,6 +983,10 @@
         return pltpu.make_async_copy(between, layer_in, misc_sem.at[3])
 
     def prefetch(number):
+        pl.when(number >= CHUNKS)(lambda: Load(number - CHUNKS, number).start())
+        pl.when(number < CHUNKS)(lambda: prefetch_turn(number))
+
+    def prefetch_turn(number):
         layer = 1 - number // LAYER_CHUNKS
         turn = number % LAYER_CHUNKS
         base = LAYER_CHUNKS * layer
@@ -999,14 +1003,14 @@
 
         @pl.when(turn >= PROJECT_TURN)
         def _():
-            Load(base + turn - PROJECT_TURN, number).start()
+            pl.when(layer == 1)(lambda: Load(base + turn - PROJECT_TURN, number).start())
 
             @pl.when((turn - PROJECT_TURN) % 2 == 0)
             def _():
                 load_stage(layer, (turn - PROJECT_TURN) // 2).start()
                 pl.when(layer == 0)(lambda: load_attends((turn - PROJECT_TURN) // 2).start())
 
-    prefetch(jnp.int32(0))
+    prefetch_turn(jnp.int32(0))
     load_turned(1, 2, 0).start()
     load_turned(1, 1, 1).start()
     fetch(2, 1).start()
@@ -1036,8 +1040,8 @@
         back_hidden = back_hidden + contract_cols(branch[:, 512:], shrink[number % 2, 1])
         first = half_in[number % 2, 0].astype(WIDE)
         second = half_in[number % 2, 1].astype(WIDE)
-        back[0, :, low] = (back_hidden * second).astype(LOW)
-        back[0, :, high] = (back_hidden * first).astype(LOW)
+        back[0, 0, :, low] = (back_hidden * second).astype(LOW)
+        back[0, 0, :, high] = (back_hidden * first).astype(LOW)
 
     def output_start(layer):
         load_turned(0, 0, 2 - layer).wait()
@@ -1057,7 +1061,7 @@
     def output_turn(part):
         for f in range(2):
             lanes = pl.ds(pl.multiple_of(f * 512 + part * WIDTH, WIDTH), WIDTH)
-            back[0, :, pl.ds(f * WIDTH, WIDTH)] = gated_branch[:, lanes]
+            back[0, 0, :, pl.ds(f * WIDTH, WIDTH)] = gated_branch[:, lanes]
 
     def project_start(layer):
         @pl.when(layer == 1)
@@ -1082,12 +1086,13 @@
     def project_turn(layer, group):
         load_stage(0, 0).wait()
         coming = sums.at[1]
-        pl.when(layer == 1)(lambda: linear_mixer_back(group, stage, coming, back))
+        mine = back.at[group]
+        pl.when(layer == 1)(lambda: linear_mixer_back(group, stage, coming, mine))
 
         @pl.when(layer == 0)
         def _():
             load_attends(0).wait()
-            local_mixer_back(group, stage, attends, validity, coming, back)
+            local_mixer_back(group, stage, attends, validity, coming, mine)
 
     def finish_layer(layer):
         def act(rows):
@@ -1095,13 +1100,13 @@
 
         over_rows(act)
 
-    def terms(number, which, order):
+    def terms(number, group, which, order):
         slot = number % TERM_SLOTS
         out = wide_buffers[0]
 
         def body(tile, carry):
             rows = pl.ds(pl.multiple_of(tile * 512, 512), 512)
-            value = dot(turned[order % 2, rows, :], back[which]).astype(LOW)
+            value = dot(turned[order % 2, rows, :], back[group, which]).astype(LOW)
             for f in range(2):
                 part = value[:, f * WIDTH : (f + 1) * WIDTH]
                 out[slot, f, tile] = part.reshape(2, 2, 2, 64, WIDTH)
@@ -1130,17 +1135,17 @@
         def _():
             fetch(2, 0).start()
 
-    def spread(number, which, kind):
+    def spread(number, group, which, kind):
         def body(t, carry):
             rows = pl.ds(pl.multiple_of(t * 512, 512), 512)
-            value = contract_cols(back[which], loaded[number % 2, rows, :])
+            value = contract_cols(back[group, which], loaded[number % 2, rows, :])
             sums[kind, :, rows] = sums[kind, :, rows] + value
             return carry
 
         lax.fori_loop(0, 2, body, 0)
 
     def body(step, carry):
-        pl.when(step + 1 < CHUNKS)(lambda: prefetch(step + 1))
+        pl.when(step + 1 < CHUNKS + PROJECT_CHUNKS)(lambda: prefetch(step + 1))
         scatter.older(step)
 
         @pl.when(step < CHUNKS)
@@ -1160,16 +1165,29 @@
             in_project = jnp.minimum(jnp.maximum(turn - PROJECT_TURN + 1, 0), 1)
             in_output = jnp.minimum(jnp.maximum(turn - OUTPUT_TURN + 1, 0), 1) - in_project
             which = in_project * ((turn + PROJECT_TURN) % 2)
-            terms(step, which, 1 - layer + in_output)
+            group = in_project * ((turn - PROJECT_TURN) // 2)
+            terms(step, group, which, 1 - layer + in_output)
             place, part, due = scatter.tall_turn(step)
             pl.when(due)(lambda: tall_terms(part, step))
             scatter.start(0, step)
+
+            @pl.when((layer == 1) | (turn < PROJECT_TURN))
+            def _():
+                Load(0, step).wait()
+                spread(step, group, which, in_output)
+
+            pl.when(step == LAYER_CHUNKS - 1)(lambda: finish_layer(layer))
+
+        @pl.when((step >= CHUNKS) & (step < CHUNKS + PROJECT_CHUNKS))
+        def _():
+            place = step - CHUNKS
             Load(0, step).wait()
-            spread(step, which, in_output)
-            pl.when(turn == LAYER_CHUNKS - 1)(lambda: finish_layer(layer))
-
-            @pl.when(step == CHUNKS - 1)
+            spread(step, place // 2, place % 2, 0)
+
+            @pl.when(place == PROJECT_CHUNKS - 1)
             def _():
+                finish_layer(0)
+
                 def act(rows):
                     up[rows, :] = up[rows, :] * validity[rows, :]
 
@@ -1234,7 +1252,7 @@
             pltpu.VMEM((ROWS, 1024), WIDE),
             pltpu.VMEM((ROWS, 1024), WIDE),
             pltpu.VMEM((2, 1024, ROWS), LOW),
-            pltpu.VMEM((2, ROWS, 2 * WIDTH), LOW),
+            pltpu.VMEM((HEAD_GROUPS, 2, ROWS, 2 * WIDTH), LOW),
         ],
         compiler_params=pltpu.CompilerParams(
             collective_id=1, has_side_effects=True, vmem_limit_bytes=62 << 20
@@ -1255,8 +1273,15 @@
     )
 
 
-def unpack_kernel(mixed_in, tokens_in, chunks, parts, *refs):
-    outs, sem = refs[:-1], refs[-1]
+def unpack_kernel(*refs):
+    outs, held, sem, load_sem = refs[4 : 6 + WEIGHTS], refs[6 + WEIGHTS : -2], refs[-2], refs[-1]
+    loads = [
+        pltpu.make_async_copy(source, target, load_sem.at[i])
+        for i, (source, target) in enumerate(zip(refs[:4], held))
+    ]
+    for copy in loads:
+        copy.start()
+    mixed_in, tokens_in, chunks, parts = held
     copies = [(mixed_in, outs[0]), (tokens_in, outs[1])]
     for order in range(2):
         layer = 1 - order
@@ -1277,8 +1302,12 @@
         pltpu.make_async_copy(source, target, sem.at[i])
         for i, (source, target) in enumerate(copies)
     ]
-    for copy in copies:
-        copy.start()
+    groups = ([0], [1], range(2, len(copies)))
+    for group, waited in zip(groups, (loads[:1], loads[1:2], loads[2:])):
+        for copy in waited:
+            copy.wait()
+        for i in group:
+            copies[i].start()
     for copy in copies:
         copy.wait()
 
@@ -1290,10 +1319,14 @@
         unpack_kernel,
         out_shape=(struct(mixed_out.shape, LOW), struct(tokens_gradient.shape, WIDE))
         + tuple(struct(item.shape, WIDE) for item in shards_of),
-        in_specs=[FULL] * 4,
+        in_specs=[ANY] * 4,
         out_specs=(ANY,) * (2 + WEIGHTS),
-        scratch_shapes=[pltpu.SemaphoreType.DMA((count,))],
-        compiler_params=pltpu.CompilerParams(vmem_limit_bytes=32 << 20),
+        scratch_shapes=[
+            pltpu.VMEM(item.shape, item.dtype)
+            for item in (mixed_out, tokens_gradient, chunks, parts)
+        ]
+        + [pltpu.SemaphoreType.DMA((count,)), pltpu.SemaphoreType.DMA((4,))],
+        compiler_params=pltpu.CompilerParams(vmem_limit_bytes=60 << 20),
     )(mixed_out, tokens_gradient, chunks, parts)
 
 

time: 456 us -> 452 us (level)
  no operation moved by 1% of the time
where the time goes in v6:
time: 452 us
  Pallas kernels  449 us (99%)
    pallas_call x1, Pallas kernels, run_forward(): pl.pallas_call(forward_kernel, out_shape=(struct((CHUNKS,) + bits + (64,...  227 us
    pallas_call x1, Pallas kernels, run_backward(): pl.pallas_call(backward_kernel, out_shape=(struct((ROWS, 1024), WIDE), st...  216 us

profile of v6, /device:TPU:0, one launch (start us, length us, event | category | flops | bytes accessed | tf_op | source)
XLA Modules:
  0.0 451.7 jit_solution(1904580018515752785)
XLA Ops:
  1.3 0.7 fusion.refs_9_.refs_2_
  2.0 227.0 %shard_map.186 = (bf16[42,2,2,2,2,2,64,256]{7,6,5,4,3,2,1,0:T(8,128)(2,1)}, bf16[2,2,2,2,2,2,176,512]{7,6,5,4,3,2,1,0:T(8,128)(2,1)}, bf16[512,1024]{1,0:T(8,128...) custom-call(bf16[64,2048]{1,0:T(8,128)(2,1)} %refs_0_.1, ...), custom_call_target="tpu_custom_call" | custom-call | tf_op jit(solution)/shard_map/pallas_call | solution.py:566
  229.0 216.3 %shard_map.187 = (f32[512,1024]{1,0:T(8,128)}, f32[42,64,256]{2,1,0:T(8,128)}, f32[8,176,128]{2,1,0:T(8,128)}) custom-call(bf16[512,1024]{1,0:T(8,128)(2,1)} %bitcast.12, bf16[512,1024]{1,0:T(8,128)(2,1)} %bitcast.11, f32[512,1]{1,0:T(8,128)} %fusion.refs_9_.refs_2_, bf16[42,2,1024,256]{3,2,1,0:T(8,128)(2,1)} %bitcast.8, bf16[2,2,2816,512]{3,2,1,0:T(8,128)(2,1)} %bitcast.9, ...), custom_call_target="tpu_custom_call" | custom-call | tf_op jit(solution)/shard_map/pallas_call | solution.py:1216
  445.3 6.2 %shard_map.188 = (bf16[512,1024]{1,0:T(8,128)(2,1)}, f32[512,1024]{1,0:T(8,128)}, f32[64,2048]{1,0:T(8,128)}, f32[64,512]{1,0:T(8,128)}, f32[64,2816]{1,0:T(8,12...) custom-call(bf16[512,1024]{1,0:T(8,128)(2,1)} %get-tuple-element.33., ...), custom_call_target="tpu_custom_call" | custom-call | tf_op jit(solution)/shard_map/pallas_call | solution.py:1318

commit v7 on v6

--- a/solution.py
+++ b/solution.py
@@ -381,9 +381,10 @@
         lax.fori_loop(0, ROWS // 128, act, 0)
         keep_turned(layer, kind).start()
 
-    lax.fori_loop(0, ROWS // 128, start_rows, 0)
-    norm_into(x, normed)
-    turn(normed, 0, 0)
+    def start_layers():
+        lax.fori_loop(0, ROWS // 128, start_rows, 0)
+        norm_into(x, normed)
+        turn(normed, 0, 0)
 
     def load(chunk):
         return pltpu.make_async_copy(
@@ -517,6 +518,7 @@
 
     def body(step, carry):
         gather.step(step)
+        pl.when(step == 2)(start_layers)
         arrived = step - GATHER_STEPS[PHASES]
 
         @pl.when((arrived >= 0) & (arrived < CHUNKS))

time: 452 us -> 450 us (level)
  no operation moved by 1% of the time
where the time goes in v7:
time: 450 us
  Pallas kernels  448 us (100%)
    pallas_call x1, Pallas kernels, run_forward(): pl.pallas_call(forward_kernel, out_shape=(struct((CHUNKS,) + bits + (64,...  225 us
    pallas_call x1, Pallas kernels, run_backward(): pl.pallas_call(backward_kernel, out_shape=(struct((ROWS, 1024), WIDE), st...  216 us

profile of v7, /device:TPU:0, one launch (start us, length us, event | category | flops | bytes accessed | tf_op | source)
XLA Modules:
  0.0 450.1 jit_solution(4309549277863751601)
XLA Ops:
  1.3 0.7 fusion.refs_9_.refs_2_
  2.0 225.5 %shard_map.186 = (bf16[42,2,2,2,2,2,64,256]{7,6,5,4,3,2,1,0:T(8,128)(2,1)}, bf16[2,2,2,2,2,2,176,512]{7,6,5,4,3,2,1,0:T(8,128)(2,1)}, bf16[512,1024]{1,0:T(8,128...) custom-call(bf16[64,2048]{1,0:T(8,128)(2,1)} %refs_0_.1, ...), custom_call_target="tpu_custom_call" | custom-call | tf_op jit(solution)/shard_map/pallas_call | solution.py:568
  227.5 216.2 %shard_map.187 = (f32[512,1024]{1,0:T(8,128)}, f32[42,64,256]{2,1,0:T(8,128)}, f32[8,176,128]{2,1,0:T(8,128)}) custom-call(bf16[512,1024]{1,0:T(8,128)(2,1)} %bitcast.12, bf16[512,1024]{1,0:T(8,128)(2,1)} %bitcast.11, f32[512,1]{1,0:T(8,128)} %fusion.refs_9_.refs_2_, bf16[42,2,1024,256]{3,2,1,0:T(8,128)(2,1)} %bitcast.8, bf16[2,2,2816,512]{3,2,1,0:T(8,128)(2,1)} %bitcast.9, ...), custom_call_target="tpu_custom_call" | custom-call | tf_op jit(solution)/shard_map/pallas_call | solution.py:1218
  443.7 6.2 %shard_map.188 = (bf16[512,1024]{1,0:T(8,128)(2,1)}, f32[512,1024]{1,0:T(8,128)}, f32[64,2048]{1,0:T(8,128)}, f32[64,512]{1,0:T(8,128)}, f32[64,2816]{1,0:T(8,12...) custom-call(bf16[512,1024]{1,0:T(8,128)(2,1)} %get-tuple-element.33., ...), custom_call_target="tpu_custom_call" | custom-call | tf_op jit(solution)/shard_map/pallas_call | solution.py:1320

commit v8 on v7

--- a/solution.py
+++ b/solution.py
@@ -115,7 +115,7 @@
     barrier = pltpu.get_barrier_semaphore()
     for target in targets.values():
         pl.semaphore_signal(barrier, inc=1, device_id=target, device_id_type=MESH)
-    pl.semaphore_wait(barrier, len(targets))
+    return lambda: pl.semaphore_wait(barrier, len(targets))
 
 
 def dot(left, right):
@@ -231,6 +231,7 @@
         self.at = tuple(self.places[name] for name in ("f", "zh", "zl", "y", "c"))
 
     def begin(self):
+        met = greet(self.targets)
         counts = (PROJECT_CHUNKS, OUTPUT_CHUNKS, EXPAND_CHUNKS)
         for layer in range(2):
             chunk = LAYER_CHUNKS * layer
@@ -248,7 +249,7 @@
                 self.tall.at[(layer,) + self.at],
                 self.local_sem.at[CHUNKS + layer],
             ).start()
-        greet(self.targets)
+        met()
 
     def message(self, block, target, sems, place):
         return pltpu.make_async_remote_copy(
@@ -1012,6 +1013,7 @@
                 load_stage(layer, (turn - PROJECT_TURN) // 2).start()
                 pl.when(layer == 0)(lambda: load_attends((turn - PROJECT_TURN) // 2).start())
 
+    met = greet(scatter.targets)
     prefetch_turn(jnp.int32(0))
     load_turned(1, 2, 0).start()
     load_turned(1, 1, 1).start()
@@ -1023,7 +1025,7 @@
         up[rows, :] = cotangent[rows, :].astype(WIDE) * validity[rows, :]
 
     over_rows(begin_rows)
-    greet(scatter.targets)
+    met()
 
     def expand_start(layer):
         def act(rows):

time: 450 us -> 451 us (level)
  no operation moved by 1% of the time
where the time goes in v8:
time: 451 us; the launch traced here: 450 us
  Pallas kernels  448 us (99%)
    pallas_call x1, Pallas kernels, run_forward(): pl.pallas_call(forward_kernel, out_shape=(struct((CHUNKS,) + bits + (64,...  225 us
    pallas_call x1, Pallas kernels, run_backward(): pl.pallas_call(backward_kernel, out_shape=(struct((ROWS, 1024), WIDE), st...  217 us

profile of v8, /device:TPU:0, one launch (start us, length us, event | category | flops | bytes accessed | tf_op | source)
XLA Modules:
  0.0 450.4 jit_solution(10698510632006405705)
XLA Ops:
  1.3 0.7 fusion.refs_9_.refs_2_
  2.0 225.4 %shard_map.186 = (bf16[42,2,2,2,2,2,64,256]{7,6,5,4,3,2,1,0:T(8,128)(2,1)}, bf16[2,2,2,2,2,2,176,512]{7,6,5,4,3,2,1,0:T(8,128)(2,1)}, bf16[512,1024]{1,0:T(8,128...) custom-call(bf16[64,2048]{1,0:T(8,128)(2,1)} %refs_0_.1, ...), custom_call_target="tpu_custom_call" | custom-call | tf_op jit(solution)/shard_map/pallas_call | solution.py:569
  227.4 216.5 %shard_map.187 = (f32[512,1024]{1,0:T(8,128)}, f32[42,64,256]{2,1,0:T(8,128)}, f32[8,176,128]{2,1,0:T(8,128)}) custom-call(bf16[512,1024]{1,0:T(8,128)(2,1)} %bitcast.12, bf16[512,1024]{1,0:T(8,128)(2,1)} %bitcast.11, f32[512,1]{1,0:T(8,128)} %fusion.refs_9_.refs_2_, bf16[42,2,1024,256]{3,2,1,0:T(8,128)(2,1)} %bitcast.8, bf16[2,2,2816,512]{3,2,1,0:T(8,128)(2,1)} %bitcast.9, ...), custom_call_target="tpu_custom_call" | custom-call | tf_op jit(solution)/shard_map/pallas_call | solution.py:1220
  444.0 6.2 %shard_map.188 = (bf16[512,1024]{1,0:T(8,128)(2,1)}, f32[512,1024]{1,0:T(8,128)}, f32[64,2048]{1,0:T(8,128)}, f32[64,512]{1,0:T(8,128)}, f32[64,2816]{1,0:T(8,12...) custom-call(bf16[512,1024]{1,0:T(8,128)(2,1)} %get-tuple-element.33., ...), custom_call_target="tpu_custom_call" | custom-call | tf_op jit(solution)/shard_map/pallas_call | solution.py:1322
